TPU v7x, 32 devices: a whole 2x2x4 slice. The times are simulated.
32 devices in a mesh: dp: 4 (over x, core), sol: 4 (over z), tensor: 2 (over y).
Axes of the slice: x: 2, y: 2, z: 4, core: 2. Of those that a mesh axis runs over, the one named last changes fastest.
Arguments:
- inputs: bfloat16 [8192, 2048], P(('dp', 'sol')), may hold values from -6 to 6
- cotangent: bfloat16 [8192, 2048], P(('dp', 'sol')), may hold values from -6 to 6
- attn_gain: float32 [2048], replicated, may hold values from 0.25 to 1.75
- attn_shift: float32 [2048], replicated, may hold values from -3 to 3
- query_weight: bfloat16 [2048, 2048], P(('dp', 'sol'), 'tensor'), may hold values from -0.25 to 0.25
- key_weight: bfloat16 [2048, 2048], P(('dp', 'sol'), 'tensor'), may hold values from -0.125 to 0.125
- value_weight: bfloat16 [2048, 2048], P(('dp', 'sol'), 'tensor'), may hold values from -0.125 to 0.125
- out_weight: bfloat16 [2048, 2048], P(('dp', 'sol'), 'tensor'), may hold values from -0.5 to 0.5
- mlp_gain: float32 [2048], replicated, may hold values from 0.25 to 1.75
- mlp_shift: float32 [2048], replicated, may hold values from -3 to 3
- up_weight: bfloat16 [2048, 8192], P(('dp', 'sol'), 'tensor'), may hold values from -0.125 to 0.125
- up_bias: float32 [8192], P('tensor'), may hold values from -3 to 3
- down_weight: bfloat16 [2048, 8192], P(('dp', 'sol'), 'tensor'), may hold values from -0.0625 to 0.0625
- down_bias: float32 [2048], replicated, may hold values from -3 to 3
- live_rows: int32 [16], replicated, may hold values from 128 to 512, as said below
Outputs:
- outputs: bfloat16 [8192, 2048], P(('dp', 'sol'))
- input_grad: bfloat16 [8192, 2048], P(('dp', 'sol'))
- attn_gain_grad: float32 [2048], replicated
- attn_shift_grad: float32 [2048], replicated
- query_grad: float32 [2048, 2048], P(('dp', 'sol'), 'tensor')
- key_grad: float32 [2048, 2048], P(('dp', 'sol'), 'tensor')
- value_grad: float32 [2048, 2048], P(('dp', 'sol'), 'tensor')
- out_grad: float32 [2048, 2048], P(('dp', 'sol'), 'tensor')
- mlp_gain_grad: float32 [2048], replicated
- mlp_shift_grad: float32 [2048], replicated
- up_grad: float32 [2048, 8192], P(('dp', 'sol'), 'tensor')
- up_bias_grad: float32 [8192], P('tensor')
- down_grad: float32 [2048, 8192], P(('dp', 'sol'), 'tensor')
- down_bias_grad: float32 [2048], replicated
Inputs may be any that keep to these rules, and one draw needn't show every extreme that they name: Entry g * 4 of live_rows is the length of problem g's prefix; entry g * 4 + s for s > 0 the length of the solution in that block. Some entry equals 512 and some other entry equals 128.
All inputs are finite; a program needn't handle non-finite values.
Results may differ from a plain program's by a relative error of at most 0.014.
Values may be sent and summed in bfloat16 or wider, within the bound.
A program may use at most 448 MiB of HBM per device.

v0:
```python
import math

import jax
import jax.numpy as jnp
from jax import lax
from jax.sharding import PartitionSpec as P

HEAD_DIM = 128


EPSILON = 1e-05
NEG_FILL = -1e30


def from_root(value, axis, source):
    kept = jnp.where(lax.axis_index(axis) == source, value, 0).astype(value.dtype)
    return lax.psum(kept, axis)


def layer_norm(features, norm_gain, norm_shift):
    row_mean = jnp.mean(features, axis=-1, keepdims=True)
    centered = features - row_mean
    variance = jnp.mean(centered * centered, axis=-1, keepdims=True)
    return centered * lax.rsqrt(variance + EPSILON) * norm_gain + norm_shift


def gelu_tanh(upward):
    return jax.nn.gelu(upward, approximate=True)


def dot_plain(left_side, right_side):
    return jnp.dot(left_side, right_side, preferred_element_type=jnp.float32)


def dot_right_t(left_side, right_side):
    return lax.dot_general(
        left_side, right_side, (((1,), (1,)), ((), ())), preferred_element_type=jnp.float32
    )


def dot_left_t(left_side, right_side):
    return lax.dot_general(
        left_side, right_side, (((0,), (0,)), ((), ())), preferred_element_type=jnp.float32
    )


def per_device(
    inputs,
    cotangent,
    attn_gain,
    attn_shift,
    query_weight,
    key_weight,
    value_weight,
    out_weight,
    mlp_gain,
    mlp_shift,
    up_weight,
    up_bias,
    down_weight,
    down_bias,
    live_rows,
):
    block_rows = inputs.shape[0]
    half_width = query_weight.shape[1]
    ff_half = up_weight.shape[1]
    local_heads = half_width // HEAD_DIM
    score_scale = 1.0 / math.sqrt(HEAD_DIM)
    group_size = lax.axis_size("sol")
    sol_place = lax.axis_index("sol")
    group_start = lax.axis_index("dp") * group_size
    is_first = sol_place == 0
    own_live = live_rows[group_start + sol_place]
    prefix_live = live_rows[group_start]
    row_ids = jnp.arange(block_rows)[:, None]
    col_ids = jnp.arange(block_rows)[None, :]
    prefix_ok = jnp.logical_and(col_ids < prefix_live, jnp.logical_not(is_first))
    own_ok = jnp.logical_and(col_ids <= row_ids, col_ids < own_live)
    allowed = jnp.concatenate(
        [jnp.broadcast_to(prefix_ok, (block_rows, block_rows)), own_ok], axis=1
    )[None]
    query_full, key_full, value_full, out_full = (
        lax.all_gather(query_weight, ("dp", "sol"), axis=0, tiled=True),
        lax.all_gather(key_weight, ("dp", "sol"), axis=0, tiled=True),
        lax.all_gather(value_weight, ("dp", "sol"), axis=0, tiled=True),
        lax.all_gather(out_weight, ("dp", "sol"), axis=0, tiled=True),
    )
    features = inputs.astype(jnp.float32)
    normed = layer_norm(features, attn_gain, attn_shift).astype(jnp.bfloat16)
    query_rows = dot_plain(normed, query_full).astype(jnp.bfloat16)
    key_rows = dot_plain(normed, key_full).astype(jnp.bfloat16)
    value_rows = dot_plain(normed, value_full).astype(jnp.bfloat16)
    prefix_key, prefix_value = (from_root(key_rows, "sol", 0), from_root(value_rows, "sol", 0))
    all_keys = jnp.concatenate([prefix_key, key_rows], 0).reshape(
        2 * block_rows, local_heads, HEAD_DIM
    )
    all_values = jnp.concatenate([prefix_value, value_rows], 0).reshape(
        2 * block_rows, local_heads, HEAD_DIM
    )
    head_queries = query_rows.reshape(block_rows, local_heads, HEAD_DIM)

    def masked_scores():
        raw_scores = (
            jnp.einsum("qhd,khd->hqk", head_queries, all_keys, preferred_element_type=jnp.float32)
            * score_scale
        )
        return jnp.where(allowed, raw_scores, NEG_FILL)

    scores = masked_scores()
    row_peak = jnp.max(scores, axis=-1, keepdims=True)
    exp_scores = jnp.exp(scores - row_peak)
    totals = jnp.sum(exp_scores, axis=-1, keepdims=True)
    attn_probs = exp_scores / totals
    log_total = row_peak + jnp.log(totals)
    mixed = jnp.einsum(
        "hqk,khd->qhd",
        attn_probs.astype(jnp.bfloat16),
        all_values,
        preferred_element_type=jnp.float32,
    )
    mixed_low = mixed.reshape(block_rows, half_width).astype(jnp.bfloat16)
    attn_total = lax.psum(dot_right_t(mixed_low, out_full), "tensor")
    hidden = features + attn_total
    up_full, down_full = (
        lax.all_gather(up_weight, ("dp", "sol"), axis=0, tiled=True),
        lax.all_gather(down_weight, ("dp", "sol"), axis=0, tiled=True),
    )
    normed_two = layer_norm(hidden, mlp_gain, mlp_shift).astype(jnp.bfloat16)
    upward = dot_plain(normed_two, up_full) + up_bias
    active = gelu_tanh(upward).astype(jnp.bfloat16)
    mlp_total = lax.psum(dot_right_t(active, down_full).astype(jnp.bfloat16), "tensor").astype(
        jnp.float32
    )
    outputs = (hidden + mlp_total + down_bias).astype(jnp.bfloat16)
    up_back, down_back = (
        lax.all_gather(up_weight, ("dp", "sol"), axis=0, tiled=True),
        lax.all_gather(down_weight, ("dp", "sol"), axis=0, tiled=True),
    )
    grad_out = cotangent.astype(jnp.float32)
    down_bias_grad = jnp.sum(grad_out, axis=0)
    grad_active = dot_plain(cotangent, down_back)
    unused_gelu, gelu_pull = jax.vjp(gelu_tanh, upward)
    grad_up = gelu_pull(grad_active)[0]
    grad_up_low = grad_up.astype(jnp.bfloat16)
    up_bias_grad = jnp.sum(grad_up_low.astype(jnp.float32), axis=0)
    grad_normed_two = lax.psum(dot_right_t(grad_up_low, up_back), "tensor")
    unused_norm, norm_two_pull = jax.vjp(layer_norm, hidden, mlp_gain, mlp_shift)
    grad_hidden_norm, mlp_gain_grad, mlp_shift_grad = norm_two_pull(grad_normed_two)
    grad_hidden = grad_out + grad_hidden_norm
    grad_branch = grad_hidden.astype(jnp.bfloat16)
    query_back, key_back, value_back, out_back = (
        lax.all_gather(query_weight, ("dp", "sol"), axis=0, tiled=True),
        lax.all_gather(key_weight, ("dp", "sol"), axis=0, tiled=True),
        lax.all_gather(value_weight, ("dp", "sol"), axis=0, tiled=True),
        lax.all_gather(out_weight, ("dp", "sol"), axis=0, tiled=True),
    )
    grad_mixed_low = dot_plain(grad_branch, out_back).astype(jnp.bfloat16)
    grad_head_mixed = grad_mixed_low.reshape(block_rows, local_heads, HEAD_DIM)
    scores = masked_scores()
    attn_probs = jnp.exp(scores - log_total)
    grad_probs = jnp.einsum(
        "qhd,khd->hqk", grad_head_mixed, all_values, preferred_element_type=jnp.float32
    )
    row_delta = jnp.sum(attn_probs * grad_probs, axis=-1, keepdims=True)
    grad_scores = (attn_probs * (grad_probs - row_delta)).astype(jnp.bfloat16)
    grad_queries = (
        jnp.einsum("hqk,khd->qhd", grad_scores, all_keys, preferred_element_type=jnp.float32)
        * score_scale
    ).reshape(block_rows, half_width)
    grad_keys = (
        jnp.einsum("hqk,qhd->khd", grad_scores, head_queries, preferred_element_type=jnp.float32)
        * score_scale
    ).reshape(2 * block_rows, half_width)
    grad_values = jnp.einsum(
        "hqk,qhd->khd",
        attn_probs.astype(jnp.bfloat16),
        grad_head_mixed,
        preferred_element_type=jnp.float32,
    ).reshape(2 * block_rows, half_width)
    prefix_key_sum, prefix_value_sum = lax.psum(
        (grad_keys[:block_rows], grad_values[:block_rows]), "sol"
    )
    key_grad_rows = jnp.where(
        is_first, grad_keys[block_rows:] + prefix_key_sum, grad_keys[block_rows:]
    )
    value_grad_rows = jnp.where(
        is_first, grad_values[block_rows:] + prefix_value_sum, grad_values[block_rows:]
    )
    query_grad_low = grad_queries.astype(jnp.bfloat16)
    key_grad_low = key_grad_rows.astype(jnp.bfloat16)
    value_grad_low = value_grad_rows.astype(jnp.bfloat16)
    grad_normed_part = (
        dot_right_t(query_grad_low, query_back)
        + dot_right_t(key_grad_low, key_back)
        + dot_right_t(value_grad_low, value_back)
    )
    grad_normed = lax.psum(grad_normed_part, "tensor")
    unused_first, norm_one_pull = jax.vjp(layer_norm, features, attn_gain, attn_shift)
    grad_features, attn_gain_grad, attn_shift_grad = norm_one_pull(grad_normed)
    input_grad = (grad_hidden + grad_features).astype(jnp.bfloat16)
    weight_grads = lax.psum_scatter(
        jnp.concatenate(
            [
                dot_left_t(normed, query_grad_low),
                dot_left_t(normed, key_grad_low),
                dot_left_t(normed, value_grad_low),
                dot_left_t(grad_branch, mixed_low),
                dot_left_t(normed_two, grad_up_low),
                dot_left_t(cotangent, active),
            ],
            axis=1,
        ),
        ("dp", "sol"),
        scatter_dimension=0,
        tiled=True,
    )
    small_sums = lax.psum(
        (
            attn_gain_grad,
            attn_shift_grad,
            mlp_gain_grad,
            mlp_shift_grad,
            up_bias_grad,
            down_bias_grad,
        ),
        ("dp", "sol"),
    )
    mlp_start = 4 * half_width
    return (
        outputs,
        input_grad,
        small_sums[0],
        small_sums[1],
        weight_grads[:, :half_width],
        weight_grads[:, half_width : 2 * half_width],
        weight_grads[:, 2 * half_width : 3 * half_width],
        weight_grads[:, 3 * half_width : mlp_start],
        small_sums[2],
        small_sums[3],
        weight_grads[:, mlp_start : mlp_start + ff_half],
        small_sums[4],
        weight_grads[:, mlp_start + ff_half :],
        small_sums[5],
    )


def solution(mesh):
    return jax.shard_map(
        per_device,
        mesh=mesh,
        in_specs=(
            P(("dp", "sol"), None),
            P(("dp", "sol"), None),
            P(),
            P(),
            P(("dp", "sol"), "tensor"),
            P(("dp", "sol"), "tensor"),
            P(("dp", "sol"), "tensor"),
            P(("dp", "sol"), "tensor"),
            P(),
            P(),
            P(("dp", "sol"), "tensor"),
            P("tensor"),
            P(("dp", "sol"), "tensor"),
            P(),
            P(),
        ),
        out_specs=(
            P(("dp", "sol"), None),
            P(("dp", "sol"), None),
            P(),
            P(),
            P(("dp", "sol"), "tensor"),
            P(("dp", "sol"), "tensor"),
            P(("dp", "sol"), "tensor"),
            P(("dp", "sol"), "tensor"),
            P(),
            P(),
            P(("dp", "sol"), "tensor"),
            P("tensor"),
            P(("dp", "sol"), "tensor"),
            P(),
        ),
        check_vma=False,
    )
```

profile of v0, /device:TPU:0, one launch (start us, length us, event | category | flops | bytes accessed | tf_op | source)
XLA Modules:
  0.0 2882.9 jit_solution(16317560800203567539)
XLA Ops:
  12.7 51.0 %all-gather.11.cloned.1.call-done = bf16[2048,1024]{1,0:T(8,128)(2,1)} async-done(((bf16[128,1024]{1,0:T(8,128)(2,1)}), bf16[2048,1024]{1,0:T(8,128)(2,1)}) %all-gather.11.cloned.1.call-update) | async-done | bytes 4194320 | tf_op jit(solution)/shard_map/all_gather | solution.py:84
  63.7 5.9 broadcast_select_fusion
  69.6 45.6 %all-gather.7.cloned.1.call-done = bf16[2048,1024]{1,0:T(8,128)(2,1)} async-done(((bf16[128,1024]{1,0:T(8,128)(2,1)}), bf16[2048,1024]{1,0:T(8,128)(2,1)}) %all-gather.7.cloned.1.call-update) | async-done | bytes 4194320 | tf_op jit(solution)/shard_map/all_gather | solution.py:85
  115.2 5.9 broadcast_select_fusion.1
  124.9 41.6 %all-gather.9.cloned.1.call-done = bf16[2048,1024]{1,0:T(8,128)(2,1)} async-done(((bf16[128,1024]{1,0:T(8,128)(2,1)}), bf16[2048,1024]{1,0:T(8,128)(2,1)}) %all-gather.9.cloned.1.call-update) | async-done | bytes 4194320 | tf_op jit(solution)/shard_map/all_gather | solution.py:83
  166.5 5.5 convolution_convert_fusion.3
  173.6 81.9 %all-reduce.24.cloned.1.call-done = (bf16[512,1024]{1,0:T(8,128)(2,1)}, bf16[512,1024]{1,0:T(8,128)(2,1)}) async-done(((bf16[512,1024]{1,0:T(8,128)(2,1)}, bf16[512,1024]{1,0:T(8,128)(2,1)}), (bf16[512,1024]{1,0:T(8,128)(2,1)}, bf16[512,1024]{1,0:T(8,128)(2,1)})) %all-reduce.24.cloned.1.call-update) | async-done | bytes 2097168 | tf_op jit(solution)/shard_map/psum | solution.py:17
  255.5 3.0 pad_maximum_fusion
  258.5 3.9 copy.73
  262.5 5.1 fusion.59
  267.6 3.8 fusion
  273.9 8.6 fusion.35
  282.5 25.0 all-gather.13.cloned.1.call-done
  307.5 7.0 fusion.60
  316.3 104.7 %all-reduce.12.cloned.1.call-done = f32[512,2048]{1,0:T(8,128)} async-done(((f32[512,2048]{1,0:T(8,128)}), f32[512,2048]{1,0:T(8,128)}) %all-reduce.12.cloned.1.call-update) | async-done | bytes 4194320 | tf_op jit(solution)/shard_map/psum | solution.py:122
  426.2 123.9 %all-gather.15.cloned.1.call-done = bf16[2048,4096]{1,0:T(8,128)(2,1)} async-done(((bf16[128,4096]{1,0:T(8,128)(2,1)}), bf16[2048,4096]{1,0:T(8,128)(2,1)}) %all-gather.15.cloned.1.call-update) | async-done | bytes 16777232 | tf_op jit(solution)/shard_map/all_gather | solution.py:125
  550.1 15.7 fusion.43
  565.9 111.6 %all-gather.17.cloned.1.call-done = bf16[2048,4096]{1,0:T(8,128)(2,1)} async-done(((bf16[128,4096]{1,0:T(8,128)(2,1)}), bf16[2048,4096]{1,0:T(8,128)(2,1)}) %all-gather.17.cloned.1.call-update) | async-done | bytes 16777232 | tf_op jit(solution)/shard_map/all_gather | solution.py:126
  677.4 19.1 convert_reduce_fusion
  698.6 14.2 fusion.61
  712.9 18.3 convolution_convert_fusion
  731.3 87.7 %all-reduce.16.cloned.1.call-done = f32[512,2048]{1,0:T(8,128)} async-done(((f32[512,2048]{1,0:T(8,128)}), f32[512,2048]{1,0:T(8,128)}) %all-reduce.16.cloned.1.call-update) | async-done | bytes 4194320 | tf_op jit(solution)/shard_map/psum | solution.py:146
  819.0 5.0 multiply_reduce_fusion.1
  824.0 60.8 %all-reduce.14.cloned.1.call-done = bf16[512,2048]{1,0:T(8,128)(2,1)} async-done(((bf16[512,2048]{1,0:T(8,128)(2,1)}), bf16[512,2048]{1,0:T(8,128)(2,1)}) %all-reduce.14.cloned.1.call-update) | async-done | bytes 2097168 | tf_op jit(solution)/shard_map/psum | solution.py:131
  884.8 5.8 fusion.52
  898.0 11.4 multiply_reduce_fusion
  909.4 9.8 fusion.25
  921.5 7.8 multiply_convert_fusion
  937.2 4.8 fusion.56
  946.8 3.1 copy.70
  950.0 7.5 multiply_convert_fusion.2
  957.6 5.9 convolution_dynamic-update-slice_fusion.4
  963.5 4.4 fusion.62
  967.9 132.6 %all-reduce.22.cloned.1.call-done = (f32[512,1024]{1,0:T(8,128)}, f32[512,1024]{1,0:T(8,128)}) async-done(((f32[512,1024]{1,0:T(8,128)}, f32[512,1024]{1,0:T(8,128)}), (f32[512,1024]{1,0:T(8,128)}, f32[512,1024]{1,0:T(8,128)})) %all-reduce.22.cloned.1.call-update) | async-done | bytes 4194320 | tf_op jit(solution)/shard_map/psum | solution.py:180
  1100.5 4.7 fusion.28
  1109.1 4.8 add_add_fusion.2
  1113.9 7.1 convolution_dynamic-update-slice_fusion.3
  1121.1 5.8 convolution_dynamic-update-slice_fusion.2
  1126.9 5.8 convolution_dynamic-update-slice_fusion.1
  1132.6 18.4 convolution_dynamic-update-slice_fusion
  1151.1 19.1 bitcast_dynamic-update-slice_fusion
  1172.0 49.0 %all-reduce.18.cloned.1.call-done = f32[512,2048]{1,0:T(8,128)} async-done(((f32[512,2048]{1,0:T(8,128)}), f32[512,2048]{1,0:T(8,128)}) %all-reduce.18.cloned.1.call-update) | async-done | bytes 4194320 | tf_op jit(solution)/shard_map/psum | solution.py:197
  1221.0 3.3 fusion.50
  1227.1 3.4 convert_reduce_fusion.2
  1230.5 66.6 %all-reduce.1 = (f32[2048]{0:T(1024)}, f32[2048]{0:T(1024)}, f32[2048]{0:T(1024)}, f32[2048]{0:T(1024)}, f32[4096]{0:T(1024)}, /*index=5*/f32[2048]{0:T(1024)}) all-reduce(f32[2048]{0:T(1024)S(1)} %get-tuple-element.16, f32[2048]{0:T(1024)S(1)} %get-tuple-element.19, ...), channel_id=1, replica_groups=mesh['dp'=4,'sol'=4,'tensor'=2] {'dp','sol'}, use_global_device_ids=true, to_apply=%region_20.21 | all-reduce | flops 14336 | bytes 114688 | tf_op jit(solution)/shard_map/psum | solution.py:217
  1297.1 1570.2 %all-reduce.20.cloned.1.call-done = f32[2048,12288]{1,0:T(8,128)} async-done(((f32[2048,12288]{1,0:T(8,128)}), f32[2048,12288]{1,0:T(8,128)}) %all-reduce.20.cloned.1.call-update) | async-done | bytes 100663312
  2867.4 5.4 fusion.54
  2872.8 3.3 fusion.55
  (155 shorter events, 52.7 us)
Async XLA Ops:
  7.2 4.3 copy-start.2
  7.2 56.5 %copy-start.41 = (f32[2048]{0:T(1024)S(1)}, f32[2048]{0:T(1024)}, u32[]{:S(2)}) copy-start(f32[2048]{0:T(1024)} %param.18) | copy-start | bytes 24580
  7.2 56.5 %copy-start.20 = (f32[2048]{0:T(1024)S(1)}, f32[2048]{0:T(1024)}, u32[]{:S(2)}) copy-start(f32[2048]{0:T(1024)} %param.17) | copy-start | bytes 24580
  7.2 56.5 %all-gather.11.cloned.1.call-start = ((), (), s32[]{:S(2)}) async-start(), calls=%async_computation.2 | async-start | bytes 4456448 | tf_op jit(solution)/shard_map/all_gather | solution.py:84
  7.9 107.2 %all-gather.7.cloned.1.call-start = ((), (), s32[]{:S(2)}) async-start(), calls=%async_computation | async-start | bytes 4456448 | tf_op jit(solution)/shard_map/all_gather | solution.py:85
  8.7 157.8 %all-gather.9.cloned.1.call-start = ((), (), s32[]{:S(2)}) async-start(), calls=%async_computation.1 | async-start | bytes 4456448 | tf_op jit(solution)/shard_map/all_gather | solution.py:83
  9.4 246.1 %all-reduce.24.cloned.1.call-start = ((), (), s32[]{:S(2)}) async-start(), calls=%async_computation.12 | async-start | bytes 4194304 | tf_op jit(solution)/shard_map/psum | solution.py:17
  11.4 155.1 %copy-start.22 = (f32[512]{0:T(512)}, f32[512]{0:T(512)S(1)}, u32[]{:S(2)}) copy-start(f32[512]{0:T(512)S(1)} %broadcast_multiply_fusion.1) | copy-start | bytes 6148
  12.7 153.8 %copy-start.27 = (f32[512]{0:T(512)}, f32[512]{0:T(512)S(1)}, u32[]{:S(2)}) copy-start(f32[512]{0:T(512)S(1)} %fusion.40) | copy-start | bytes 6148
  69.6 52.3 %copy-start.35 = (s32[16]{0:T(128)S(1)}, s32[16]{0:T(128)}, u32[]{:S(2)}) copy-start(s32[16]{0:T(128)} %param.29) | copy-start | bytes 196
  121.1 186.4 %all-gather.13.cloned.1.call-start = ((), (), s32[]{:S(2)}) async-start(), calls=%async_computation.3 | async-start | bytes 4456448 | tf_op jit(solution)/shard_map/all_gather | solution.py:86
  121.7 299.3 %all-reduce.12.cloned.1.call-start = ((), (), s32[]{:S(2)}) async-start(), calls=%async_computation.4 | async-start | bytes 8388608 | tf_op jit(solution)/shard_map/psum | solution.py:122
  173.5 88.9 %copy-start.10 = (bf16[512,1024]{0,1:T(8,128)(2,1)}, bf16[512,1024]{0,1:T(8,128)(2,1)S(1)}, u32[]{:S(2)}) copy-start(bf16[512,1024]{0,1:T(8,128)(2,1)S(1)} %copy.72) | copy-start | bytes 3145732
  267.5 6.4 copy-start
  267.6 6.3 copy-start.18
  267.6 6.3 copy-start.19
  314.5 235.6 %all-gather.15.cloned.1.call-start = ((), (), s32[]{:S(2)}) async-start(), calls=%async_computation.5 | async-start | bytes 17825792 | tf_op jit(solution)/shard_map/all_gather | solution.py:125
  315.2 362.2 %all-gather.17.cloned.1.call-start = ((), (), s32[]{:S(2)}) async-start(), calls=%async_computation.6 | async-start | bytes 17825792 | tf_op jit(solution)/shard_map/all_gather | solution.py:126
  316.0 503.0 %all-reduce.16.cloned.1.call-start = ((), (), s32[]{:S(2)}) async-start(), calls=%async_computation.8 | async-start | bytes 8388608 | tf_op jit(solution)/shard_map/psum | solution.py:146
  423.7 126.4 %copy-start.24 = (f32[2048]{0:T(1024)S(1)}, f32[2048]{0:T(1024)}, u32[]{:S(2)}) copy-start(f32[2048]{0:T(1024)} %param.23) | copy-start | bytes 24580
  423.7 126.4 %copy-start.43 = (f32[2048]{0:T(1024)S(1)}, f32[2048]{0:T(1024)}, u32[]{:S(2)}) copy-start(f32[2048]{0:T(1024)} %param.24) | copy-start | bytes 24580
  426.2 251.2 %copy-start.12 = (bf16[512,2048]{1,0:T(8,128)(2,1)S(1)}, bf16[512,2048]{1,0:T(8,128)(2,1)}, u32[]{:S(2)}) copy-start(bf16[512,2048]{1,0:T(8,128)(2,1)} %param.16) | copy-start | bytes 6291460
  426.2 251.2 %copy-start.40 = (f32[4096]{0:T(1024)S(1)}, f32[4096]{0:T(1024)}, u32[]{:S(2)}) copy-start(f32[4096]{0:T(1024)} %param.26) | copy-start | bytes 49156
  712.8 172.0 %all-reduce.14.cloned.1.call-start = ((), (), s32[]{:S(2)}) async-start(), calls=%async_computation.7 | async-start | bytes 4194304 | tf_op jit(solution)/shard_map/psum | solution.py:131
  731.2 369.2 %all-reduce.22.cloned.1.call-start = ((), (), s32[]{:S(2)}) async-start(), calls=%async_computation.11 | async-start | bytes 8388608 | tf_op jit(solution)/shard_map/psum | solution.py:180
  731.3 153.5 %copy-start.34 = (f32[2048]{0:T(1024)S(1)}, f32[2048]{0:T(1024)}, u32[]{:S(2)}) copy-start(f32[2048]{0:T(1024)} %param.28) | copy-start | bytes 24580
  890.6 4.5 copy-start.39
  909.4 12.1 copy-start.6
  921.5 7.8 copy-start.11
  945.0 276.0 %all-reduce.18.cloned.1.call-start = ((), (), s32[]{:S(2)}) async-start(), calls=%async_computation.9 | async-start | bytes 8388608 | tf_op jit(solution)/shard_map/psum | solution.py:197
  950.0 7.6 copy-start.3
  950.0 7.6 copy-start.21
  950.0 7.6 copy-start.23
  950.0 7.6 copy-start.28
  950.0 7.6 copy-start.42
  957.6 5.9 copy-start.38
  1100.5 4.7 copy-start.36
  1105.2 3.8 copy-start.47
  1113.9 1753.5 %all-reduce.20.cloned.1.call-start = ((), (), s32[]{:S(2)}) async-start(), calls=%async_computation.10 | async-start | bytes 201326592
  1121.1 5.8 copy-start.16
  1121.1 5.8 copy-start.45
  1126.9 5.8 copy-start.5
  1126.9 5.8 copy-start.44
  1132.6 18.4 copy-start.13
  1170.2 54.1 %copy-start.32 = (f32[512]{0:T(512)S(1)}, f32[512]{0:T(512)}, u32[]{:S(2)}) copy-start(f32[512]{0:T(512)} %copy-done.31) | copy-start | bytes 6148
  1221.0 3.4 copy-start.9
  1227.1 3.4 copy-start.26
  1227.1 3.4 copy-start.33
  (14 other events, 30.4 us)
Sparse Core Ops, SparseCore 0:
  10.3 53.3 all-gather.10
  65.9 49.1 all-gather.6
  117.4 49.0 all-gather.8
  169.9 85.5 all-reduce.23
  257.8 49.6 all-gather.12
  314.6 106.3 all-reduce.11
  423.2 126.8 all-gather.14
  552.3 125.0 all-gather.16
  712.9 106.0 all-reduce.15
  821.8 62.9 all-reduce.13
  945.1 155.3 all-reduce.21
  1114.0 106.9 all-reduce.17
  1225.3 1642.0 all-reduce.19
where the time goes:
time: 2890 us; the launch traced here: 2880 us
  waiting for transfers between devices  2490 us (86%)
  matrix products  211 us (7%)
  blocking collectives  66.6 us (2%)
  local copies, waits for them, and re-layouts  51.3 us (2%)
  other arithmetic  47.6 us (2%)
    unnamed x14, waiting for transfers between devices  1570 us
    psum x1, waiting for transfers between devices, per_device(): lax.psum((grad_keys[:block_rows], grad_values[:block_rows]), 'sol')  133 us
    all_gather x1, waiting for transfers between devices, per_device(): lax.all_gather(up_weight, ('dp', 'sol'), axis=0, tiled=True)  124 us
    all_gather x1, waiting for transfers between devices, per_device(): lax.all_gather(down_weight, ('dp', 'sol'), axis=0, tiled=True)  112 us
    psum x1, waiting for transfers between devices, per_device(): attn_total = lax.psum(dot_right_t(mixed_low, out_full), 'tensor')  105 us
    psum x1, waiting for transfers between devices, per_device(): grad_normed_two = lax.psum(dot_right_t(grad_up_low, up_back), 'tensor')  87.7 us
    psum x1, waiting for transfers between devices, from_root(): return lax.psum(kept, axis)  81.9 us
    psum x1, blocking collectives, per_device(): lax.psum((attn_gain_grad, attn_shift_grad, mlp_gain_grad, mlp_shift_grad,...  66.6 us
  transfers between devices with their start and end apart: 13, of which 13 were waited for; matrix products, arithmetic and copies ran while one was open for 6% of the time, Pallas kernels for 0%

commit v1 on v0

v1 whole, which is shorter than its diff:
```python
import math

import jax
import jax.numpy as jnp
from jax import lax
from jax.experimental import pallas as pl
from jax.experimental.pallas import tpu as pltpu
from jax.sharding import PartitionSpec as P

HEAD_DIM = 128
EPSILON = 1e-05
NEG_FILL = -1e30
ROWS_AXES = ("dp", "sol")
LOW = jnp.bfloat16
WIDE = jnp.float32


def ring_place(position, sol_size):
    x, along = position // sol_size, position % sol_size
    return x, (along if x % 2 == 0 else sol_size - 1 - along)


def ring_pairs(dp_size, sol_size):
    count = dp_size // 2 * sol_size

    def flat(position, core):
        x, z = ring_place(position % count, sol_size)
        return (x * 2 + core) * sol_size + z

    places = [(q, c) for q in range(count) for c in range(2)]
    ahead = [(flat(q, c), flat(q + 1, c)) for q, c in places]
    back = [(b, a) for a, b in ahead]
    cores = [(flat(q, c), flat(q, 1 - c)) for q, c in places]
    return count, ahead, back, cores


def dot_plain(left_side, right_side):
    return jnp.dot(left_side, right_side, preferred_element_type=WIDE)


def dot_right_t(left_side, right_side):
    return lax.dot_general(
        left_side, right_side, (((1,), (1,)), ((), ())), preferred_element_type=WIDE
    )


def dot_left_t(left_side, right_side):
    return lax.dot_general(
        left_side, right_side, (((0,), (0,)), ((), ())), preferred_element_type=WIDE
    )


def norm_stats(features):
    row_mean = jnp.mean(features, axis=-1, keepdims=True)
    centered = features - row_mean
    variance = jnp.mean(centered * centered, axis=-1, keepdims=True)
    return row_mean, lax.rsqrt(variance + EPSILON)


def layer_norm(features, norm_gain, norm_shift):
    row_mean, inverse = norm_stats(features)
    return (features - row_mean) * inverse * norm_gain + norm_shift


def layer_norm_back(features, norm_gain, grad):
    row_mean, inverse = norm_stats(features)
    unit = (features - row_mean) * inverse
    scaled = grad * norm_gain
    along = jnp.mean(scaled * unit, axis=-1, keepdims=True)
    level = jnp.mean(scaled, axis=-1, keepdims=True)
    grad_features = (scaled - level - unit * along) * inverse
    return grad_features, jnp.sum(grad * unit, axis=0), jnp.sum(grad, axis=0)


def gelu_tanh(upward):
    return jax.nn.gelu(upward, approximate=True)


def copy_block(order_ref, in_ref, out_ref):
    out_ref[...] = in_ref[...]


def reorder(rows, order):
    blocks = order.shape[0]
    height, width = rows.shape
    part = width // blocks
    if part % 128:
        return jnp.take(rows.reshape(height, blocks, part), order, axis=1).reshape(height, width)
    return pl.pallas_call(
        copy_block,
        grid_spec=pltpu.PrefetchScalarGridSpec(
            num_scalar_prefetch=1,
            grid=(blocks,),
            in_specs=[pl.BlockSpec((height, part), lambda j, order_ref: (0, order_ref[j]))],
            out_specs=pl.BlockSpec((height, part), lambda j, order_ref: (0, j)),
        ),
        out_shape=jax.ShapeDtypeStruct(rows.shape, rows.dtype),
        cost_estimate=pl.CostEstimate(
            flops=0, bytes_accessed=4 * height * width, transcendentals=0
        ),
    )(order, rows)


def per_device(
    inputs,
    cotangent,
    attn_gain,
    attn_shift,
    query_weight,
    key_weight,
    value_weight,
    out_weight,
    mlp_gain,
    mlp_shift,
    up_weight,
    up_bias,
    down_weight,
    down_bias,
    live_rows,
):
    block_rows, width = inputs.shape
    shard_rows = query_weight.shape[0]
    head_cols = query_weight.shape[1] // 2
    ff_cols = up_weight.shape[1] // 2
    ff_part = ff_cols // 2
    local_heads = head_cols // HEAD_DIM
    score_scale = 1.0 / math.sqrt(HEAD_DIM)
    dp_size, sol_size = lax.axis_size("dp"), lax.axis_size("sol")
    count, ahead, back, cores = ring_pairs(dp_size, sol_size)
    dp_place, sol_place = lax.axis_index("dp"), lax.axis_index("sol")
    x_place, core = dp_place // 2, dp_place % 2
    first_core = core == 0
    along = jnp.where(x_place % 2 == 0, sol_place, sol_size - 1 - sol_place)
    ring_here = x_place * sol_size + along

    order_list = []
    for j in range(count):
        q = (ring_here + j) % count
        qx, qa = q // sol_size, q % sol_size
        qz = jnp.where(qx % 2 == 0, qa, sol_size - 1 - qa)
        order_list += [(qx * 2) * sol_size + qz, (qx * 2 + 1) * sol_size + qz]
    order = jnp.stack(order_list).astype(jnp.int32)
    back_order = jnp.argsort(order).astype(jnp.int32)

    def to_core(value):
        return lax.ppermute(value, ROWS_AXES, cores)

    def to_tensor(value):
        return lax.ppermute(value, "tensor", [(0, 1), (1, 0)])

    def reorder_vector(vector, by):
        return jnp.take(vector.reshape(by.shape[0], -1), by, axis=0).reshape(vector.shape)

    def gather_ring(piece, flip):
        hops_ahead = count // 2 - (1 if flip else 0)
        hops_back = count - 1 - hops_ahead
        got = {0: piece}
        moving_a, moving_b = piece, piece
        for k in range(1, count // 2 + 1):
            if k <= hops_ahead:
                moving_a = lax.ppermute(moving_a, ROWS_AXES, ahead)
                got[count - k] = moving_a
            if k <= hops_back:
                moving_b = lax.ppermute(moving_b, ROWS_AXES, back)
                got[k] = moving_b
        return jnp.concatenate([got[j] for j in range(count)], axis=0)

    def scatter_ring(chunk, flip):
        hops_ahead = count // 2 - (1 if flip else 0)
        hops_back = count - 1 - hops_ahead
        carried_a = carried_b = None
        for k in range(count // 2, 0, -1):
            if k <= hops_ahead:
                value = chunk(k)
                if carried_a is not None:
                    value = value + carried_a.astype(WIDE)
                carried_a = lax.ppermute(value.astype(LOW), ROWS_AXES, ahead)
            if k <= hops_back:
                value = chunk(count - k)
                if carried_b is not None:
                    value = value + carried_b.astype(WIDE)
                carried_b = lax.ppermute(value.astype(LOW), ROWS_AXES, back)
        return chunk(0) + carried_a.astype(WIDE) + carried_b.astype(WIDE)

    def own_part(shards):
        firsts, seconds = [], []
        for shard, start, size in shards:
            half = shard.shape[1] // 2
            firsts.append(shard[:, start : start + size])
            seconds.append(shard[:, half + start : half + start + size])
        low_half = jnp.concatenate(firsts, axis=1) if len(firsts) > 1 else firsts[0]
        high_half = jnp.concatenate(seconds, axis=1) if len(seconds) > 1 else seconds[0]
        mine = jnp.where(first_core, low_half, high_half)
        other = to_core(jnp.where(first_core, high_half, low_half))
        return jnp.concatenate(
            [jnp.where(first_core, mine, other), jnp.where(first_core, other, mine)], axis=0
        )

    def split_rows(full):
        upper, lower = full[:shard_rows], full[shard_rows:]
        mine = jnp.where(first_core, upper, lower)
        other = to_core(jnp.where(first_core, lower, upper))
        return jnp.where(first_core, mine, other), jnp.where(first_core, other, mine)

    def sum_partials(partial):
        mine = partial[:block_rows] + to_core(partial[block_rows:].astype(LOW)).astype(WIDE)
        low = mine.astype(LOW)
        return low.astype(WIDE) + to_tensor(low).astype(WIDE)

    def pair_rows(own):
        return jnp.concatenate([own, to_core(own)], axis=0)

    qk_piece = own_part([(query_weight, 0, head_cols), (key_weight, 0, head_cols)])
    vo_piece = own_part([(value_weight, 0, head_cols), (out_weight, 0, head_cols)])
    up_pieces = [own_part([(up_weight, s, ff_part)]) for s in (0, ff_part)]
    down_pieces = [own_part([(down_weight, s, ff_part)]) for s in (0, ff_part)]
    qk_full = gather_ring(qk_piece, False)
    vo_full = gather_ring(vo_piece, True)
    up_full = [gather_ring(up_pieces[0], False), gather_ring(up_pieces[1], True)]
    down_full = [gather_ring(down_pieces[0], False), gather_ring(down_pieces[1], True)]
    query_full, key_full = qk_full[:, :head_cols], qk_full[:, head_cols:]
    value_full, out_full = vo_full[:, :head_cols], vo_full[:, head_cols:]

    tensor_place = lax.axis_index("tensor")
    half_rows = block_rows // 2
    half = jnp.where(tensor_place == 0, inputs[:half_rows], inputs[half_rows:])
    prefix_half = half
    hop = half
    for k in range(1, sol_size):
        hop = lax.ppermute(hop, "sol", [(k - 1, k)])
        prefix_half = jnp.where(sol_place == k, hop, prefix_half)
    other_half = to_tensor(prefix_half)
    prefix_inputs = jnp.concatenate(
        [
            jnp.where(tensor_place == 0, prefix_half, other_half),
            jnp.where(tensor_place == 0, other_half, prefix_half),
        ],
        axis=0,
    )

    own_low = reorder(inputs, order)
    prefix_low = reorder(prefix_inputs, order)
    cot_low = reorder(cotangent, order)
    attn_gain_o, attn_shift_o, mlp_gain_o, mlp_shift_o, down_bias_o = [
        reorder_vector(v, order) for v in (attn_gain, attn_shift, mlp_gain, mlp_shift, down_bias)
    ]
    up_bias_c = jnp.where(first_core, up_bias[:ff_cols], up_bias[ff_cols:])
    up_bias_parts = [up_bias_c[:ff_part], up_bias_c[ff_part:]]

    features = own_low.astype(WIDE)
    normed = pair_rows(layer_norm(features, attn_gain_o, attn_shift_o).astype(LOW))
    normed_prefix = pair_rows(
        layer_norm(prefix_low.astype(WIDE), attn_gain_o, attn_shift_o).astype(LOW)
    )
    cot_pair = pair_rows(cot_low)

    query_rows = dot_plain(normed, query_full).astype(LOW)
    key_rows = dot_plain(normed, key_full).astype(LOW)
    value_rows = dot_plain(normed, value_full).astype(LOW)
    key_prefix = dot_plain(normed_prefix, key_full).astype(LOW)
    value_prefix = dot_plain(normed_prefix, value_full).astype(LOW)

    def heads_of(rows):
        return rows.reshape(2, -1, local_heads, HEAD_DIM)

    head_queries = heads_of(query_rows)
    all_keys = jnp.concatenate([heads_of(key_prefix), heads_of(key_rows)], axis=1)
    all_values = jnp.concatenate([heads_of(value_prefix), heads_of(value_rows)], axis=1)

    row_ids = jnp.arange(block_rows)[:, None]
    col_ids = jnp.arange(block_rows)[None, :]
    masks = []
    for place in (dp_place, dp_place + 1 - 2 * core):
        own_live = live_rows[place * sol_size + sol_place]
        prefix_live = live_rows[place * sol_size]
        prefix_ok = jnp.logical_and(col_ids < prefix_live, sol_place != 0)
        own_ok = jnp.logical_and(col_ids <= row_ids, col_ids < own_live)
        masks.append(
            jnp.concatenate(
                [jnp.broadcast_to(prefix_ok, (block_rows, block_rows)), own_ok], axis=1
            )
        )
    allowed = jnp.stack(masks)[:, None]

    def masked_scores():
        raw = jnp.einsum("bqhd,bkhd->bhqk", head_queries, all_keys, preferred_element_type=WIDE)
        return jnp.where(allowed, raw * score_scale, NEG_FILL)

    scores = masked_scores()
    row_peak = jnp.max(scores, axis=-1, keepdims=True)
    exp_scores = jnp.exp(scores - row_peak)
    totals = jnp.sum(exp_scores, axis=-1, keepdims=True)
    attn_probs = exp_scores / totals
    log_total = row_peak + jnp.log(totals)
    mixed = jnp.einsum(
        "bhqk,bkhd->bqhd", attn_probs.astype(LOW), all_values, preferred_element_type=WIDE
    )
    mixed_low = mixed.reshape(2 * block_rows, head_cols).astype(LOW)

    hidden = features + sum_partials(dot_right_t(mixed_low, out_full))
    normed_two = pair_rows(layer_norm(hidden, mlp_gain_o, mlp_shift_o).astype(LOW))
    upward = [dot_plain(normed_two, up_full[i]) + up_bias_parts[i] for i in range(2)]
    active = [gelu_tanh(u).astype(LOW) for u in upward]
    down_grads = [
        scatter_ring(
            lambda j, i=i: dot_left_t(
                cot_pair[:, j * 2 * shard_rows : (j + 1) * 2 * shard_rows], active[i]
            ),
            i == 1,
        )
        for i in range(2)
    ]
    grad_up = []
    for i in range(2):
        grad_active = dot_plain(cot_pair, down_full[i])
        unused_gelu, gelu_pull = jax.vjp(gelu_tanh, upward[i])
        grad_up.append(gelu_pull(grad_active)[0].astype(LOW))
    grad_normed_two = sum_partials(
        dot_right_t(grad_up[0], up_full[0]) + dot_right_t(grad_up[1], up_full[1])
    )
    up_grads = [
        scatter_ring(
            lambda j, i=i: dot_left_t(
                normed_two[:, j * 2 * shard_rows : (j + 1) * 2 * shard_rows], grad_up[i]
            ),
            i == 1,
        )
        for i in range(2)
    ]
    mlp_total = sum_partials(
        dot_right_t(active[0], down_full[0]) + dot_right_t(active[1], down_full[1])
    )
    outputs = reorder((hidden + mlp_total + down_bias_o).astype(LOW), back_order)

    grad_out = cot_low.astype(WIDE)
    down_bias_grad = jnp.sum(grad_out, axis=0)
    grad_hidden_norm, mlp_gain_grad, mlp_shift_grad = layer_norm_back(
        hidden, mlp_gain_o, grad_normed_two
    )
    grad_hidden = grad_out + grad_hidden_norm
    grad_branch = pair_rows(grad_hidden.astype(LOW))
    grad_mixed_low = dot_plain(grad_branch, out_full).astype(LOW)

    grad_head_mixed = heads_of(grad_mixed_low)
    attn_probs = jnp.exp(masked_scores() - log_total)
    grad_probs = jnp.einsum(
        "bqhd,bkhd->bhqk", grad_head_mixed, all_values, preferred_element_type=WIDE
    )
    row_delta = jnp.sum(attn_probs * grad_probs, axis=-1, keepdims=True)
    grad_scores = (attn_probs * (grad_probs - row_delta)).astype(LOW)
    grad_queries = (
        jnp.einsum("bhqk,bkhd->bqhd", grad_scores, all_keys, preferred_element_type=WIDE)
        * score_scale
    )
    grad_keys = (
        jnp.einsum("bhqk,bqhd->bkhd", grad_scores, head_queries, preferred_element_type=WIDE)
        * score_scale
    )
    grad_values = jnp.einsum(
        "bhqk,bqhd->bkhd", attn_probs.astype(LOW), grad_head_mixed, preferred_element_type=WIDE
    )

    def rows_of(heads):
        return heads.reshape(2 * block_rows, head_cols).astype(LOW)

    query_grad_low = rows_of(grad_queries)
    key_own = rows_of(grad_keys[:, block_rows:])
    value_own = rows_of(grad_values[:, block_rows:])
    key_pre = rows_of(grad_keys[:, :block_rows])
    value_pre = rows_of(grad_values[:, :block_rows])

    kv_pre = jnp.concatenate([key_pre, value_pre], axis=1)
    carried = kv_pre
    for k in range(sol_size - 1, 0, -1):
        came = lax.ppermute(carried, "sol", [(k, k - 1)])
        if k > 1:
            carried = (kv_pre.astype(WIDE) + came.astype(WIDE)).astype(LOW)
    key_all = (key_own.astype(WIDE) + came[:, :head_cols].astype(WIDE)).astype(LOW)
    value_all = (value_own.astype(WIDE) + came[:, head_cols:].astype(WIDE)).astype(LOW)

    normed_all = jnp.concatenate([normed, normed_prefix], axis=0)
    key_rows_grad = jnp.concatenate([key_own, key_pre], axis=0)
    value_rows_grad = jnp.concatenate([value_own, value_pre], axis=0)

    def qk_chunk(j):
        at = slice(j * 2 * shard_rows, (j + 1) * 2 * shard_rows)
        return jnp.concatenate(
            [
                dot_left_t(normed[:, at], query_grad_low),
                dot_left_t(normed_all[:, at], key_rows_grad),
            ],
            axis=1,
        )

    def vo_chunk(j):
        at = slice(j * 2 * shard_rows, (j + 1) * 2 * shard_rows)
        return jnp.concatenate(
            [
                dot_left_t(normed_all[:, at], value_rows_grad),
                dot_left_t(grad_branch[:, at], mixed_low),
            ],
            axis=1,
        )

    qk_grad = scatter_ring(qk_chunk, False)
    vo_grad = scatter_ring(vo_chunk, True)

    grad_normed = sum_partials(
        dot_right_t(query_grad_low, query_full)
        + dot_right_t(key_all, key_full)
        + dot_right_t(value_all, value_full)
    )
    grad_features, attn_gain_grad, attn_shift_grad = layer_norm_back(
        features, attn_gain_o, grad_normed
    )
    input_grad = reorder((grad_hidden + grad_features).astype(LOW), back_order)

    up_bias_grad = jnp.concatenate([jnp.sum(g.astype(WIDE), axis=0) for g in grad_up])
    up_bias_both = jnp.concatenate(
        [
            jnp.where(first_core, up_bias_grad, 0.0),
            jnp.where(first_core, 0.0, up_bias_grad),
        ]
    )

    def sum_rows_axes(vector):
        vector = vector + to_core(vector)
        step = 1
        while step < sol_size:
            vector = vector + lax.ppermute(vector, "sol", [(i, i ^ step) for i in range(sol_size)])
            step *= 2
        step = 2
        while step < dp_size:
            vector = vector + lax.ppermute(vector, "dp", [(i, i ^ step) for i in range(dp_size)])
            step *= 2
        return vector

    early = sum_rows_axes(
        jnp.concatenate(
            [reorder_vector(v, back_order) for v in (mlp_gain_grad, mlp_shift_grad, down_bias_grad)]
            + [up_bias_both]
        )
    )
    late = sum_rows_axes(
        jnp.concatenate([reorder_vector(v, back_order) for v in (attn_gain_grad, attn_shift_grad)])
    )

    qk_low, qk_high = split_rows(qk_grad)
    vo_low, vo_high = split_rows(vo_grad)
    up_low, up_high = zip(*[split_rows(g) for g in up_grads])
    down_low, down_high = zip(*[split_rows(g) for g in down_grads])

    def both(low_cols, high_cols):
        return jnp.concatenate([low_cols, high_cols], axis=1)

    return (
        outputs,
        input_grad,
        late[:width],
        late[width:],
        both(qk_low[:, :head_cols], qk_high[:, :head_cols]),
        both(qk_low[:, head_cols:], qk_high[:, head_cols:]),
        both(vo_low[:, :head_cols], vo_high[:, :head_cols]),
        both(vo_low[:, head_cols:], vo_high[:, head_cols:]),
        early[:width],
        early[width : 2 * width],
        jnp.concatenate(up_low + up_high, axis=1),
        early[3 * width :],
        jnp.concatenate(down_low + down_high, axis=1),
        early[2 * width : 3 * width],
    )


def solution(mesh):
    rows = P(("dp", "sol"), None)
    matrix = P(("dp", "sol"), "tensor")
    return jax.shard_map(
        per_device,
        mesh=mesh,
        in_specs=(
            rows,
            rows,
            P(),
            P(),
            matrix,
            matrix,
            matrix,
            matrix,
            P(),
            P(),
            matrix,
            P("tensor"),
            matrix,
            P(),
            P(),
        ),
        out_specs=(
            rows,
            rows,
            P(),
            P(),
            matrix,
            matrix,
            matrix,
            matrix,
            P(),
            P(),
            matrix,
            P("tensor"),
            matrix,
            P(),
        ),
        check_vma=False,
    )
```

time: 2890 us -> 1200 us (0.42)
  waiting for transfers between devices: 2490 us -> 438 us
  starting transfers between devices: 0.98 us -> 220 us
  other arithmetic: 47.6 us -> 119 us
  blocking collectives: 66.6 us -> 0 us
  local copies, waits for them, and re-layouts: 51.3 us -> 106 us
  Pallas kernels: 0 us -> 50.7 us
  matrix products: 211 us -> 249 us
    unnamed x14 -> x0, waiting for transfers between devices: 1570 us -> none
    psum x6 -> x0, waiting for transfers between devices: 517 us -> none  [the longest x1 133 us: per_device(): lax.psum((grad_keys[:block_rows], grad_values[:block_rows]), 'sol')]
    ppermute x0 -> x124, waiting for transfers between devices: none -> 438 us  [the longest x21 111 us: gather_ring(): moving_b = lax.ppermute(moving_b, ROWS_AXES, back)]
    all_gather x6 -> x0, waiting for transfers between devices: 399 us -> none  [the longest x1 124 us: per_device(): lax.all_gather(up_weight, ('dp', 'sol'), axis=0, tiled=True)]
    ppermute x0 -> x124, starting transfers between devices: none -> 220 us  [the longest x21 51.1 us: scatter_ring(): carried_a = lax.ppermute(value.astype(LOW), ROWS_AXES, ahead)]
    psum x1 -> x0, blocking collectives: 66.6 us -> none  [per_device(): lax.psum((attn_gain_grad, attn_shift_grad, mlp_gain_grad, mlp_shift_grad,...]
    pallas_call x0 -> x5, Pallas kernels: none -> 50.7 us  [reorder(): pl.pallas_call(copy_block, grid_spec=pltpu.PrefetchScalarGridSpec(num_sca...]
    convert_element_type x3 -> x21, other arithmetic: 13.1 us -> 43.9 us  [the longest x1 10.5 us: per_device(): grad_scores = (attn_probs * (grad_probs - row_delta)).astype(LOW)]
  transfers between devices with their start and end apart: 13 -> 124, of which waited for: 13 -> 58; matrix products, arithmetic and copies ran while one was open for 6% -> 28% of each run, Pallas kernels for 0% -> 4%
where the time goes in v1:
time: 1200 us; the launch traced here: 1190 us
  waiting for transfers between devices  438 us (36%)
  matrix products  249 us (21%)
  starting transfers between devices  220 us (18%)
  other arithmetic  119 us (10%)
  local copies, waits for them, and re-layouts  106 us (9%)
  Pallas kernels  50.7 us (4%)
    ppermute x21, waiting for transfers between devices, gather_ring(): moving_b = lax.ppermute(moving_b, ROWS_AXES, back)  111 us
    ppermute x5, waiting for transfers between devices, to_tensor(): return lax.ppermute(value, 'tensor', [(0, 1), (1, 0)])  110 us
    ppermute x21, waiting for transfers between devices, scatter_ring(): carried_b = lax.ppermute(value.astype(LOW), ROWS_AXES, back)  88.5 us
    dot_general x64, matrix products, dot_left_t(): lax.dot_general(left_side, right_side, (((0,), (0,)), ((), ())), preferre...  79.5 us
    dot_general x10, matrix products, dot_plain(): return jnp.dot(left_side, right_side, preferred_element_type=WIDE)  65.7 us
    dot_general x8, matrix products, dot_right_t(): lax.dot_general(left_side, right_side, (((1,), (1,)), ((), ())), preferre...  56.2 us
    ppermute x21, waiting for transfers between devices, scatter_ring(): carried_a = lax.ppermute(value.astype(LOW), ROWS_AXES, ahead)  54.3 us
    ppermute x21, starting transfers between devices, scatter_ring(): carried_a = lax.ppermute(value.astype(LOW), ROWS_AXES, ahead)  51.1 us
  transfers between devices with their start and end apart: 124, of which 58 were waited for; matrix products, arithmetic and copies ran while one was open for 28% of the time, Pallas kernels for 4%

profile of v1, /device:TPU:0, one launch (start us, length us, event | category | flops | bytes accessed | tf_op | source)
XLA Modules:
  0.0 1186.7 jit_solution(14617735443773265999)
XLA Ops:
  15.6 10.1 shard_map.254
  57.8 20.6 %collective-permute-start.10 = (bf16[256,1024]{1,0:T(8,128)(2,1)S(1)}, bf16[256,1024]{1,0:T(8,128)(2,1)}, u32[]{:S(2)}, u32[]{:S(2)}) collective-permute-start(bf16[256,1024]{1,0:T(8,128)(2,1)S(1)} %pad_maximum_fusion.32), channel_id=1, source_target_pairs={{0,2},{8,10},{2,4},{10,12},{4,6},{12,14},{6,22},{14,30},{22,20},{3... | collective-permute-start | bytes 1572872 | tf_op jit(solution)/shard_map/ppermute | solution.py:161
  85.1 21.7 %collective-permute-start.18 = (bf16[256,1024]{1,0:T(8,128)(2,1)S(1)}, bf16[256,1024]{1,0:T(8,128)(2,1)}, u32[]{:S(2)}, u32[]{:S(2)}) collective-permute-start(bf16[256,1024]{1,0:T(8,128)(2,1)S(1)} %pad_maximum_fusion.33), channel_id=1, source_target_pairs={{0,2},{8,10},{2,4},{10,12},{4,6},{12,14},{6,22},{14,30},{22,20},{3... | collective-permute-start | bytes 1572872 | tf_op jit(solution)/shard_map/ppermute | solution.py:161
  108.6 10.2 shard_map.255
  125.8 11.2 collective-permute-start.16
  141.7 7.8 collective-permute-done.16
  153.9 7.0 collective-permute-done.19
  164.8 7.1 collective-permute-done.17
  190.8 7.6 collective-permute-done.21
  288.1 9.7 collective-permute-done.50
  300.5 8.5 collective-permute-done.26
  311.0 9.2 collective-permute-done.34
  322.9 10.1 shard_map.257
  365.1 11.2 collective-permute-done.44
  376.4 11.2 collective-permute-done.52
  389.7 9.2 collective-permute-done.28
  402.8 7.3 collective-permute-done.36
  412.1 9.2 collective-permute-done.45
  449.8 7.8 collective-permute-done.40
  458.5 8.0 pad_maximum_fusion.4
  471.9 9.0 convert_reduce_fusion.3
  480.9 9.1 fusion.353
  490.0 8.3 multiply_convert_fusion.3
  498.4 10.3 convert_reduce_fusion.4
  508.7 9.1 convolution_add_fusion
  521.2 6.9 fusion.352
  528.1 10.2 convolution_add_fusion.1
  560.2 7.4 collective-permute-done.96
  594.5 6.8 collective-permute-done.104
  638.0 7.9 collective-permute-done.105
  648.4 11.2 collective-permute-done.94
  663.2 8.6 collective-permute-done.110
  687.2 13.2 %collective-permute-done.95 = bf16[256,1024]{1,0:T(8,128)(2,1)S(1)} collective-permute-done((bf16[256,1024]{1,0:T(8,128)(2,1)S(1)}, bf16[256,1024]{1,0:T(8,128)(2,1)S(1)}, u32[]{:S(2)}, u32[]{:S(2)}) %collective-permute-start.95) | collective-permute-done | bytes 524320 | tf_op jit(solution)/shard_map/ppermute | solution.py:177
  713.2 35.8 %collective-permute-done.61 = bf16[512,2048]{1,0:T(8,128)(2,1)S(1)} collective-permute-done((bf16[512,2048]{1,0:T(8,128)(2,1)S(1)}, bf16[512,2048]{1,0:T(8,128)(2,1)S(1)}, u32[]{:S(2)}, u32[]{:S(2)}) %collective-permute-start.61) | collective-permute-done | bytes 2097184 | tf_op jit(solution)/shard_map/ppermute | solution.py:149
  751.8 33.6 %collective-permute-done.58 = bf16[512,2048]{1,0:T(8,128)(2,1)S(1)} collective-permute-done((bf16[512,2048]{1,0:T(8,128)(2,1)S(1)}, bf16[512,2048]{1,0:T(8,128)(2,1)S(1)}, u32[]{:S(2)}, u32[]{:S(2)}) %collective-permute-start.58) | collective-permute-done | bytes 2097184 | tf_op jit(solution)/shard_map/ppermute | solution.py:149
  809.1 10.1 shard_map.256
  826.8 14.5 %multiply_reduce_fusion = (f32[2,4,512]{2,1,0:T(4,128)S(1)}, f32[2,4,512,1024]{3,2,1,0:T(8,128)}) fusion(f32[2,4,512,1024]{3,2,1,0:T(8,128)} %copy-done.3, f32[2,4,512]{2,1,0:T(4,128)S(1)} %bitcast.239, bf16[2,512,4,128]{1,3,2,0:T(8,128)(2,1)} %copy.52, bf16[2,512,4,128]{1,3,2,0:T(8,128)(2,1)} %copy.40, bf16[2,512,4,128]{1,3,2,0:T(8,128)(2,1)} %copy.39), kind=kOutput, calls=%fused_computation.11 | convolution fusion | flops 1090514944 | bytes 36732928 | tf_op jit(solution)/shard_map/bqhd,bkhd->bhqk/dot_general | solution.py:346
  841.3 11.0 convert_bitcast_fusion
  852.4 10.5 multiply_convert_fusion
  862.9 8.1 fusion.101
  957.4 42.1 %collective-permute-start.73 = (bf16[256,1024]{1,0:T(8,128)(2,1)S(1)}, bf16[256,1024]{1,0:T(8,128)(2,1)S(1)}, u32[]{:S(2)}, u32[]{:S(2)}) collective-permute-start(bf16[256,1024]{1,0:T(8,128)(2,1)S(1)} %fusion.165), channel_id=1, source_target_pairs={{0,2},{8,10},{2,4},{10,12},{4,6},{12,14},{6,22},{14,30},{22,20},{3... | collective-permute-start | bytes 1572872 | tf_op jit(solution)/shard_map/ppermute | solution.py:177
  1003.0 8.9 collective-permute-done.73
  1015.6 26.4 %collective-permute-done.65 = bf16[1024,1024]{1,0:T(8,128)(2,1)S(1)} collective-permute-done((bf16[1024,1024]{1,0:T(8,128)(2,1)S(1)}, bf16[1024,1024]{1,0:T(8,128)(2,1)S(1)}, u32[]{:S(2)}, u32[]{:S(2)}) %collective-permute-start.65) | collective-permute-done | bytes 2097184 | tf_op jit(solution)/shard_map/ppermute | solution.py:375
  1049.0 7.0 add_add_fusion
  1058.5 13.7 %collective-permute-start.78 = (bf16[256,1024]{1,0:T(8,128)(2,1)S(1)}, bf16[256,1024]{1,0:T(8,128)(2,1)S(1)}, u32[]{:S(2)}, u32[]{:S(2)}) collective-permute-start(bf16[256,1024]{1,0:T(8,128)(2,1)S(1)} %fusion.166), channel_id=1, source_target_pairs={{2,0},{10,8},{4,2},{12,10},{6,4},{14,12},{22,6},{30,14},{20,22},{2... | collective-permute-start | bytes 1572872 | tf_op jit(solution)/shard_map/ppermute | solution.py:182
  1078.6 15.9 %collective-permute-done.85 = bf16[256,1024]{1,0:T(8,128)(2,1)S(1)} collective-permute-done((bf16[256,1024]{1,0:T(8,128)(2,1)S(1)}, bf16[256,1024]{1,0:T(8,128)(2,1)S(1)}, u32[]{:S(2)}, u32[]{:S(2)}) %collective-permute-start.85) | collective-permute-done | bytes 524320 | tf_op jit(solution)/shard_map/ppermute | solution.py:182
  1113.1 40.9 %collective-permute-done.67 = bf16[512,2048]{1,0:T(8,128)(2,1)S(1)} collective-permute-done((bf16[512,2048]{1,0:T(8,128)(2,1)S(1)}, bf16[512,2048]{1,0:T(8,128)(2,1)S(1)}, u32[]{:S(2)}, u32[]{:S(2)}) %collective-permute-start.67) | collective-permute-done | bytes 2097184 | tf_op jit(solution)/shard_map/ppermute | solution.py:149
  1175.4 10.1 shard_map.258
  (755 shorter events, 571.5 us)
Async XLA Ops:
  2.9 54.9 %collective-permute-start.25 = (bf16[128,1024]{1,0:T(8,128)(2,1)}, bf16[128,1024]{1,0:T(8,128)(2,1)}, u32[]{:S(2)}, u32[]{:S(2)}) collective-permute-start(bf16[128,1024]{1,0:T(8,128)(2,1)} %get-tuple-element.87), channel_id=1, source_target_pairs={{0,8},{8,0},{2,10},{10,2},{4,12},{12,4},{6,14},{14,6},{22,30},{30,... | collective-permute-start | bytes 786440 | tf_op jit(solution)/shard_map/ppermute | solution.py:146
  3.3 75.1 %collective-permute-start.41 = (bf16[128,1024]{1,0:T(8,128)(2,1)}, bf16[128,1024]{1,0:T(8,128)(2,1)}, u32[]{:S(2)}, u32[]{:S(2)}) collective-permute-start(bf16[128,1024]{1,0:T(8,128)(2,1)} %get-tuple-element.88), channel_id=1, source_target_pairs={{0,8},{8,0},{2,10},{10,2},{4,12},{12,4},{6,14},{14,6},{22,30},{30,... | collective-permute-start | bytes 786440 | tf_op jit(solution)/shard_map/ppermute | solution.py:146
  5.4 43.6 %collective-permute-start.5 = (bf16[128,1024]{1,0:T(8,128)(2,1)}, bf16[128,1024]{1,0:T(8,128)(2,1)}, u32[]{:S(2)}, u32[]{:S(2)}) collective-permute-start(bf16[128,1024]{1,0:T(8,128)(2,1)} %broadcast_select_fusion.36), channel_id=1, source_target_pairs={{0,8},{8,0},{2,10},{10,2},{4,12},{12,4},{6,14},{14,6},{22,30},{30,... | collective-permute-start | bytes 786440 | tf_op jit(solution)/shard_map/ppermute | solution.py:146
  7.8 45.8 %collective-permute-start.14 = (bf16[128,1024]{1,0:T(8,128)(2,1)}, bf16[128,1024]{1,0:T(8,128)(2,1)}, u32[]{:S(2)}, u32[]{:S(2)}) collective-permute-start(bf16[128,1024]{1,0:T(8,128)(2,1)} %broadcast_select_fusion.32), channel_id=1, source_target_pairs={{0,8},{8,0},{2,10},{10,2},{4,12},{12,4},{6,14},{14,6},{22,30},{30,... | collective-permute-start | bytes 786440 | tf_op jit(solution)/shard_map/ppermute | solution.py:146
  8.9 34.2 %collective-permute-start = (bf16[256,2048]{1,0:T(8,128)(2,1)}, bf16[256,2048]{1,0:T(8,128)(2,1)}, u32[]{:S(2)}, u32[]{:S(2)}) collective-permute-start(bf16[256,2048]{1,0:T(8,128)(2,1)} %slice_select_fusion), channel_id=1, source_target_pairs={{0,2},{1,3},{8,10},{9,11},{16,18},{17,19},{24,26},{25,27}} | collective-permute-start | bytes 3145736 | tf_op jit(solution)/shard_map/ppermute | solution.py:230
  49.0 74.2 %collective-permute-start.33 = (bf16[128,1024]{1,0:T(8,128)(2,1)}, bf16[128,1024]{1,0:T(8,128)(2,1)S(1)}, u32[]{:S(2)}, u32[]{:S(2)}) collective-permute-start(bf16[128,1024]{1,0:T(8,128)(2,1)} %get-tuple-element.81), channel_id=1, source_target_pairs={{0,8},{8,0},{2,10},{10,2},{4,12},{12,4},{6,14},{14,6},{22,30},{30,... | collective-permute-start | bytes 786440 | tf_op jit(solution)/shard_map/ppermute | solution.py:146
  51.7 33.3 %collective-permute-start.6 = (bf16[256,1024]{1,0:T(8,128)(2,1)S(1)}, bf16[256,1024]{1,0:T(8,128)(2,1)S(1)}, u32[]{:S(2)}, u32[]{:S(2)}) collective-permute-start(bf16[256,1024]{1,0:T(8,128)(2,1)S(1)} %pad_maximum_fusion.32), channel_id=1, source_target_pairs={{2,0},{10,8},{4,2},{12,10},{6,4},{14,12},{22,6},{30,14},{20,22},{2... | collective-permute-start | bytes 1572872 | tf_op jit(solution)/shard_map/ppermute | solution.py:164
  53.6 53.2 %collective-permute-start.3 = (bf16[256,2048]{1,0:T(8,128)(2,1)S(1)}, bf16[256,2048]{1,0:T(8,128)(2,1)S(1)}, u32[]{:S(2)}, u32[]{:S(2)}) collective-permute-start(bf16[256,2048]{1,0:T(8,128)(2,1)S(1)} %select_select_fusion), channel_id=1, source_target_pairs={{0,1},{1,0},{2,3},{3,2},{4,5},{5,4},{6,7},{7,6},{8,9},{9,8},{10,11... | collective-permute-start | bytes 3145736 | tf_op jit(solution)/shard_map/ppermute | solution.py:149
  57.8 65.5 %collective-permute-start.10 = (bf16[256,1024]{1,0:T(8,128)(2,1)S(1)}, bf16[256,1024]{1,0:T(8,128)(2,1)}, u32[]{:S(2)}, u32[]{:S(2)}) collective-permute-start(bf16[256,1024]{1,0:T(8,128)(2,1)S(1)} %pad_maximum_fusion.32), channel_id=1, source_target_pairs={{0,2},{8,10},{2,4},{10,12},{4,6},{12,14},{6,22},{14,30},{22,20},{3... | collective-permute-start | bytes 1572872 | tf_op jit(solution)/shard_map/ppermute | solution.py:161
  78.4 47.4 %collective-permute-start.15 = (bf16[256,1024]{1,0:T(8,128)(2,1)S(1)}, bf16[256,1024]{1,0:T(8,128)(2,1)}, u32[]{:S(2)}, u32[]{:S(2)}) collective-permute-start(bf16[256,1024]{1,0:T(8,128)(2,1)S(1)} %pad_maximum_fusion.33), channel_id=1, source_target_pairs={{2,0},{10,8},{4,2},{12,10},{6,4},{14,12},{22,6},{30,14},{20,22},{2... | collective-permute-start | bytes 1572872 | tf_op jit(solution)/shard_map/ppermute | solution.py:164
  85.1 51.9 %collective-permute-start.18 = (bf16[256,1024]{1,0:T(8,128)(2,1)S(1)}, bf16[256,1024]{1,0:T(8,128)(2,1)}, u32[]{:S(2)}, u32[]{:S(2)}) collective-permute-start(bf16[256,1024]{1,0:T(8,128)(2,1)S(1)} %pad_maximum_fusion.33), channel_id=1, source_target_pairs={{0,2},{8,10},{2,4},{10,12},{4,6},{12,14},{6,22},{14,30},{22,20},{3... | collective-permute-start | bytes 1572872 | tf_op jit(solution)/shard_map/ppermute | solution.py:161
  106.8 30.2 %collective-permute-start.7 = (bf16[256,1024]{1,0:T(8,128)(2,1)S(1)}, bf16[256,1024]{1,0:T(8,128)(2,1)}, u32[]{:S(2)}, u32[]{:S(2)}) collective-permute-start(bf16[256,1024]{1,0:T(8,128)(2,1)S(1)} %collective-permute-done.6), channel_id=1, source_target_pairs={{2,0},{10,8},{4,2},{12,10},{6,4},{14,12},{22,6},{30,14},{20,22},{2... | collective-permute-start | bytes 1572872 | tf_op jit(solution)/shard_map/ppermute | solution.py:164
  123.2 28.7 %collective-permute-start.49 = (bf16[128,1024]{1,0:T(8,128)(2,1)}, bf16[128,1024]{1,0:T(8,128)(2,1)S(1)}, u32[]{:S(2)}, u32[]{:S(2)}) collective-permute-start(bf16[128,1024]{1,0:T(8,128)(2,1)} %get-tuple-element.82), channel_id=1, source_target_pairs={{0,8},{8,0},{2,10},{10,2},{4,12},{12,4},{6,14},{14,6},{22,30},{30,... | collective-permute-start | bytes 786440 | tf_op jit(solution)/shard_map/ppermute | solution.py:146
  123.3 40.5 %collective-permute-start.11 = (bf16[256,1024]{1,0:T(8,128)(2,1)}, bf16[256,1024]{1,0:T(8,128)(2,1)S(1)}, u32[]{:S(2)}, u32[]{:S(2)}) collective-permute-start(bf16[256,1024]{1,0:T(8,128)(2,1)} %collective-permute-done.10), channel_id=1, source_target_pairs={{0,2},{8,10},{2,4},{10,12},{4,6},{12,14},{6,22},{14,30},{22,20},{3... | collective-permute-start | bytes 1572872 | tf_op jit(solution)/shard_map/ppermute | solution.py:161
  151.9 47.8 %collective-permute-start.13 = (bf16[512,2048]{1,0:T(8,128)(2,1)S(1)}, bf16[512,2048]{1,0:T(8,128)(2,1)}, u32[]{:S(2)}, u32[]{:S(2)}) collective-permute-start(bf16[512,2048]{1,0:T(8,128)(2,1)S(1)} %get-tuple-element.111), channel_id=1, source_target_pairs={{0,8},{8,0},{2,10},{10,2},{4,12},{12,4},{6,14},{14,6},{22,30},{30,... | collective-permute-start | bytes 6291464 | tf_op jit(solution)/shard_map/ppermute | solution.py:146
  163.7 47.5 %collective-permute-start.4 = (bf16[512,2048]{1,0:T(8,128)(2,1)}, bf16[512,2048]{1,0:T(8,128)(2,1)}, u32[]{:S(2)}, u32[]{:S(2)}) collective-permute-start(bf16[512,2048]{1,0:T(8,128)(2,1)} %get-tuple-element.110), channel_id=1, source_target_pairs={{0,8},{8,0},{2,10},{10,2},{4,12},{12,4},{6,14},{14,6},{22,30},{30,... | collective-permute-start | bytes 6291464 | tf_op jit(solution)/shard_map/ppermute | solution.py:146
  182.7 103.3 %collective-permute-start.42 = (bf16[256,1024]{1,0:T(8,128)(2,1)}, bf16[256,1024]{1,0:T(8,128)(2,1)}, u32[]{:S(2)}, u32[]{:S(2)}) collective-permute-start(bf16[256,1024]{1,0:T(8,128)(2,1)} %pad_maximum_fusion.36), channel_id=1, source_target_pairs={{2,0},{10,8},{4,2},{12,10},{6,4},{14,12},{22,6},{30,14},{20,22},{2... | collective-permute-start | bytes 1572872 | tf_op jit(solution)/shard_map/ppermute | solution.py:164
  187.2 100.9 %collective-permute-start.46 = (bf16[256,1024]{1,0:T(8,128)(2,1)}, bf16[256,1024]{1,0:T(8,128)(2,1)}, u32[]{:S(2)}, u32[]{:S(2)}) collective-permute-start(bf16[256,1024]{1,0:T(8,128)(2,1)} %pad_maximum_fusion.36), channel_id=1, source_target_pairs={{0,2},{8,10},{2,4},{10,12},{4,6},{12,14},{6,22},{14,30},{22,20},{3... | collective-permute-start | bytes 1572872 | tf_op jit(solution)/shard_map/ppermute | solution.py:161
  279.2 67.6 %collective-permute-start.22 = (bf16[512,2048]{1,0:T(8,128)(2,1)}, bf16[512,2048]{1,0:T(8,128)(2,1)}, u32[]{:S(2)}, u32[]{:S(2)}) collective-permute-start(bf16[512,2048]{1,0:T(8,128)(2,1)} %slice.1099), channel_id=1, source_target_pairs={{0,8},{8,0},{2,10},{10,2},{4,12},{12,4},{6,14},{14,6},{22,30},{30,... | collective-permute-start | bytes 6291464 | tf_op jit(solution)/shard_map/ppermute | solution.py:146
  344.8 31.6 %collective-permute-start.44 = (bf16[256,1024]{1,0:T(8,128)(2,1)}, bf16[256,1024]{1,0:T(8,128)(2,1)S(1)}, u32[]{:S(2)}, u32[]{:S(2)}) collective-permute-start(bf16[256,1024]{1,0:T(8,128)(2,1)} %collective-permute-done.43), channel_id=1, source_target_pairs={{2,0},{10,8},{4,2},{12,10},{6,4},{14,12},{22,6},{30,14},{20,22},{2... | collective-permute-start | bytes 1572872 | tf_op jit(solution)/shard_map/ppermute | solution.py:164
  346.8 40.8 %collective-permute-start.52 = (bf16[256,1024]{1,0:T(8,128)(2,1)}, bf16[256,1024]{1,0:T(8,128)(2,1)S(1)}, u32[]{:S(2)}, u32[]{:S(2)}) collective-permute-start(bf16[256,1024]{1,0:T(8,128)(2,1)} %collective-permute-done.51), channel_id=1, source_target_pairs={{2,0},{10,8},{4,2},{12,10},{6,4},{14,12},{22,6},{30,14},{20,22},{2... | collective-permute-start | bytes 1572872 | tf_op jit(solution)/shard_map/ppermute | solution.py:164
  353.9 44.9 %collective-permute-start.28 = (bf16[256,1024]{1,0:T(8,128)(2,1)S(1)}, bf16[256,1024]{1,0:T(8,128)(2,1)S(1)}, u32[]{:S(2)}, u32[]{:S(2)}) collective-permute-start(bf16[256,1024]{1,0:T(8,128)(2,1)S(1)} %collective-permute-done.27), channel_id=1, source_target_pairs={{2,0},{10,8},{4,2},{12,10},{6,4},{14,12},{22,6},{30,14},{20,22},{2... | collective-permute-start | bytes 1572872 | tf_op jit(solution)/shard_map/ppermute | solution.py:164
  355.9 85.2 %collective-permute-start.23 = (bf16[512,2048]{1,0:T(8,128)(2,1)S(1)}, bf16[512,2048]{1,0:T(8,128)(2,1)S(1)}, u32[]{:S(2)}, u32[]{:S(2)}) collective-permute-start(bf16[512,2048]{1,0:T(8,128)(2,1)S(1)} %fusion.47), channel_id=1, source_target_pairs={{0,1},{1,0},{2,3},{3,2},{4,5},{5,4},{6,7},{7,6},{8,9},{9,8},{10,11... | collective-permute-start | bytes 6291464 | tf_op jit(solution)/shard_map/ppermute | solution.py:149
  365.1 37.5 %collective-permute-start.38 = (bf16[256,1024]{1,0:T(8,128)(2,1)S(1)}, bf16[256,1024]{1,0:T(8,128)(2,1)S(1)}, u32[]{:S(2)}, u32[]{:S(2)}) collective-permute-start(bf16[256,1024]{1,0:T(8,128)(2,1)S(1)} %collective-permute-done.37), channel_id=1, source_target_pairs={{0,2},{8,10},{2,4},{10,12},{4,6},{12,14},{6,22},{14,30},{22,20},{3... | collective-permute-start | bytes 1572872 | tf_op jit(solution)/shard_map/ppermute | solution.py:161
  426.7 45.1 %collective-permute-start.59 = (bf16[512,2048]{1,0:T(8,128)(2,1)S(1)}, bf16[512,2048]{1,0:T(8,128)(2,1)S(1)}, u32[]{:S(2)}, u32[]{:S(2)}) collective-permute-start(bf16[512,2048]{1,0:T(8,128)(2,1)S(1)} %copy-done.2), channel_id=1, source_target_pairs={{0,8},{8,0},{2,10},{10,2},{4,12},{12,4},{6,14},{14,6},{22,30},{30,... | collective-permute-start | bytes 6291464 | tf_op jit(solution)/shard_map/ppermute | solution.py:146
  520.4 156.7 %collective-permute-start.60 = (bf16[512,2048]{1,0:T(8,128)(2,1)S(1)}, bf16[512,2048]{1,0:T(8,128)(2,1)S(1)}, u32[]{:S(2)}, u32[]{:S(2)}) collective-permute-start(bf16[512,2048]{1,0:T(8,128)(2,1)S(1)} %slice.1097), channel_id=1, source_target_pairs={{0,8},{8,0},{2,10},{10,2},{4,12},{12,4},{6,14},{14,6},{22,30},{30,... | collective-permute-start | bytes 6291464 | tf_op jit(solution)/shard_map/ppermute | solution.py:146
  540.8 139.6 %collective-permute-start.57 = (bf16[512,2048]{1,0:T(8,128)(2,1)S(1)}, bf16[512,2048]{1,0:T(8,128)(2,1)S(1)}, u32[]{:S(2)}, u32[]{:S(2)}) collective-permute-start(bf16[512,2048]{1,0:T(8,128)(2,1)S(1)} %slice.1098), channel_id=1, source_target_pairs={{0,8},{8,0},{2,10},{10,2},{4,12},{12,4},{6,14},{14,6},{22,30},{30,... | collective-permute-start | bytes 6291464 | tf_op jit(solution)/shard_map/ppermute | solution.py:146
  635.0 39.3 %collective-permute-start.102 = (bf16[256,1024]{1,0:T(8,128)(2,1)S(1)}, bf16[256,1024]{1,0:T(8,128)(2,1)S(1)}, u32[]{:S(2)}, u32[]{:S(2)}) collective-permute-start(bf16[256,1024]{1,0:T(8,128)(2,1)S(1)} %fusion.113), channel_id=1, source_target_pairs={{0,2},{8,10},{2,4},{10,12},{4,6},{12,14},{6,22},{14,30},{22,20},{3... | collective-permute-start | bytes 1572872 | tf_op jit(solution)/shard_map/ppermute | solution.py:177
  674.6 33.6 %collective-permute-start.114 = (bf16[256,1024]{1,0:T(8,128)(2,1)S(1)}, bf16[256,1024]{1,0:T(8,128)(2,1)S(1)}, u32[]{:S(2)}, u32[]{:S(2)}) collective-permute-start(bf16[256,1024]{1,0:T(8,128)(2,1)S(1)} %fusion.121), channel_id=1, source_target_pairs={{2,0},{10,8},{4,2},{12,10},{6,4},{14,12},{22,6},{30,14},{20,22},{2... | collective-permute-start | bytes 1572872 | tf_op jit(solution)/shard_map/ppermute | solution.py:182
  700.4 48.6 %collective-permute-start.61 = (bf16[512,2048]{1,0:T(8,128)(2,1)S(1)}, bf16[512,2048]{1,0:T(8,128)(2,1)S(1)}, u32[]{:S(2)}, u32[]{:S(2)}) collective-permute-start(bf16[512,2048]{1,0:T(8,128)(2,1)S(1)} %fusion.45), channel_id=1, source_target_pairs={{0,1},{1,0},{2,3},{3,2},{4,5},{5,4},{6,7},{7,6},{8,9},{9,8},{10,11... | collective-permute-start | bytes 6291464 | tf_op jit(solution)/shard_map/ppermute | solution.py:149
  702.8 82.6 %collective-permute-start.58 = (bf16[512,2048]{1,0:T(8,128)(2,1)S(1)}, bf16[512,2048]{1,0:T(8,128)(2,1)S(1)}, u32[]{:S(2)}, u32[]{:S(2)}) collective-permute-start(bf16[512,2048]{1,0:T(8,128)(2,1)S(1)} %fusion.46), channel_id=1, source_target_pairs={{0,1},{1,0},{2,3},{3,2},{4,5},{5,4},{6,7},{7,6},{8,9},{9,8},{10,11... | collective-permute-start | bytes 6291464 | tf_op jit(solution)/shard_map/ppermute | solution.py:149
  708.8 88.6 %collective-permute-start.123 = (f32[128,1024]{1,0:T(8,128)}, f32[128,1024]{1,0:T(8,128)}, u32[]{:S(2)}, u32[]{:S(2)}) collective-permute-start(f32[128,1024]{1,0:T(8,128)} %slice_select_fusion.1), channel_id=1, source_target_pairs={{0,8},{8,0},{2,10},{10,2},{4,12},{12,4},{6,14},{14,6},{22,30},{30,... | collective-permute-start | bytes 1572872 | tf_op jit(solution)/shard_map/ppermute | solution.py:146
  710.5 91.3 %collective-permute-start.115 = (f32[128,1024]{1,0:T(8,128)}, f32[128,1024]{1,0:T(8,128)}, u32[]{:S(2)}, u32[]{:S(2)}) collective-permute-start(f32[128,1024]{1,0:T(8,128)} %slice_select_fusion.3), channel_id=1, source_target_pairs={{0,8},{8,0},{2,10},{10,2},{4,12},{12,4},{6,14},{14,6},{22,30},{30,... | collective-permute-start | bytes 1572872 | tf_op jit(solution)/shard_map/ppermute | solution.py:146
  791.4 29.1 %collective-permute-start.62 = (bf16[512,2048]{1,0:T(8,128)(2,1)S(1)}, bf16[512,2048]{1,0:T(8,128)(2,1)}, u32[]{:S(2)}, u32[]{:S(2)}) collective-permute-start(bf16[512,2048]{1,0:T(8,128)(2,1)S(1)} %get-tuple-element.25), channel_id=1, source_target_pairs={{0,8},{8,0},{2,10},{10,2},{4,12},{12,4},{6,14},{14,6},{22,30},{30,... | collective-permute-start | bytes 6291464 | tf_op jit(solution)/shard_map/ppermute | solution.py:146
  900.9 37.3 %collective-permute-start.63 = (bf16[1024,1024]{1,0:T(8,128)(2,1)}, bf16[1024,1024]{1,0:T(8,128)(2,1)S(1)}, u32[]{:S(2)}, u32[]{:S(2)}) collective-permute-start(bf16[1024,1024]{1,0:T(8,128)(2,1)} %copy-done.20), channel_id=1, source_target_pairs={{6,4},{7,5},{14,12},{15,13},{22,20},{23,21},{30,28},{31,29}} | collective-permute-start | bytes 6291464 | tf_op jit(solution)/shard_map/ppermute | solution.py:375
  903.4 96.2 %collective-permute-start.76 = (bf16[256,1024]{1,0:T(8,128)(2,1)S(1)}, bf16[256,1024]{1,0:T(8,128)(2,1)S(1)}, u32[]{:S(2)}, u32[]{:S(2)}) collective-permute-start(bf16[256,1024]{1,0:T(8,128)(2,1)S(1)} %pad_maximum_fusion.39), channel_id=1, source_target_pairs={{2,0},{10,8},{4,2},{12,10},{6,4},{14,12},{22,6},{30,14},{20,22},{2... | collective-permute-start | bytes 1572872 | tf_op jit(solution)/shard_map/ppermute | solution.py:182
  905.7 51.5 %collective-permute-start.72 = (bf16[256,1024]{1,0:T(8,128)(2,1)S(1)}, bf16[256,1024]{1,0:T(8,128)(2,1)S(1)}, u32[]{:S(2)}, u32[]{:S(2)}) collective-permute-start(bf16[256,1024]{1,0:T(8,128)(2,1)S(1)} %pad_maximum_fusion.38), channel_id=1, source_target_pairs={{0,2},{8,10},{2,4},{10,12},{4,6},{12,14},{6,22},{14,30},{22,20},{3... | collective-permute-start | bytes 1572872 | tf_op jit(solution)/shard_map/ppermute | solution.py:177
  908.5 91.3 %collective-permute-start.83 = (bf16[256,1024]{1,0:T(8,128)(2,1)S(1)}, bf16[256,1024]{1,0:T(8,128)(2,1)S(1)}, u32[]{:S(2)}, u32[]{:S(2)}) collective-permute-start(bf16[256,1024]{1,0:T(8,128)(2,1)S(1)} %pad_maximum_fusion.43), channel_id=1, source_target_pairs={{2,0},{10,8},{4,2},{12,10},{6,4},{14,12},{22,6},{30,14},{20,22},{2... | collective-permute-start | bytes 1572872 | tf_op jit(solution)/shard_map/ppermute | solution.py:182
  910.9 91.1 %collective-permute-start.80 = (bf16[256,1024]{1,0:T(8,128)(2,1)S(1)}, bf16[256,1024]{1,0:T(8,128)(2,1)S(1)}, u32[]{:S(2)}, u32[]{:S(2)}) collective-permute-start(bf16[256,1024]{1,0:T(8,128)(2,1)S(1)} %pad_maximum_fusion.42), channel_id=1, source_target_pairs={{0,2},{8,10},{2,4},{10,12},{4,6},{12,14},{6,22},{14,30},{22,20},{3... | collective-permute-start | bytes 1572872 | tf_op jit(solution)/shard_map/ppermute | solution.py:177
  952.3 89.8 %collective-permute-start.65 = (bf16[1024,1024]{1,0:T(8,128)(2,1)S(1)}, bf16[1024,1024]{1,0:T(8,128)(2,1)S(1)}, u32[]{:S(2)}, u32[]{:S(2)}) collective-permute-start(bf16[1024,1024]{1,0:T(8,128)(2,1)S(1)} %fusion.28), channel_id=1, source_target_pairs={{2,0},{3,1},{10,8},{11,9},{18,16},{19,17},{26,24},{27,25}} | collective-permute-start | bytes 6291464 | tf_op jit(solution)/shard_map/ppermute | solution.py:375
  957.4 54.5 %collective-permute-start.73 = (bf16[256,1024]{1,0:T(8,128)(2,1)S(1)}, bf16[256,1024]{1,0:T(8,128)(2,1)S(1)}, u32[]{:S(2)}, u32[]{:S(2)}) collective-permute-start(bf16[256,1024]{1,0:T(8,128)(2,1)S(1)} %fusion.165), channel_id=1, source_target_pairs={{0,2},{8,10},{2,4},{10,12},{4,6},{12,14},{6,22},{14,30},{22,20},{3... | collective-permute-start | bytes 1572872 | tf_op jit(solution)/shard_map/ppermute | solution.py:177
  999.7 56.8 %collective-permute-start.77 = (bf16[256,1024]{1,0:T(8,128)(2,1)S(1)}, bf16[256,1024]{1,0:T(8,128)(2,1)}, u32[]{:S(2)}, u32[]{:S(2)}) collective-permute-start(bf16[256,1024]{1,0:T(8,128)(2,1)S(1)} %fusion.167), channel_id=1, source_target_pairs={{2,0},{10,8},{4,2},{12,10},{6,4},{14,12},{22,6},{30,14},{20,22},{2... | collective-permute-start | bytes 1572872 | tf_op jit(solution)/shard_map/ppermute | solution.py:182
  1000.7 71.4 %collective-permute-start.84 = (bf16[256,1024]{1,0:T(8,128)(2,1)}, bf16[256,1024]{1,0:T(8,128)(2,1)}, u32[]{:S(2)}, u32[]{:S(2)}) collective-permute-start(bf16[256,1024]{1,0:T(8,128)(2,1)} %fusion.173), channel_id=1, source_target_pairs={{2,0},{10,8},{4,2},{12,10},{6,4},{14,12},{22,6},{30,14},{20,22},{2... | collective-permute-start | bytes 1572872 | tf_op jit(solution)/shard_map/ppermute | solution.py:182
  1002.1 76.2 %collective-permute-start.81 = (bf16[256,1024]{1,0:T(8,128)(2,1)S(1)}, bf16[256,1024]{1,0:T(8,128)(2,1)S(1)}, u32[]{:S(2)}, u32[]{:S(2)}) collective-permute-start(bf16[256,1024]{1,0:T(8,128)(2,1)S(1)} %fusion.170), channel_id=1, source_target_pairs={{0,2},{8,10},{2,4},{10,12},{4,6},{12,14},{6,22},{14,30},{22,20},{3... | collective-permute-start | bytes 1572872 | tf_op jit(solution)/shard_map/ppermute | solution.py:177
  1012.9 62.6 %collective-permute-start.74 = (bf16[256,1024]{1,0:T(8,128)(2,1)}, bf16[256,1024]{1,0:T(8,128)(2,1)}, u32[]{:S(2)}, u32[]{:S(2)}) collective-permute-start(bf16[256,1024]{1,0:T(8,128)(2,1)} %fusion.164), channel_id=1, source_target_pairs={{0,2},{8,10},{2,4},{10,12},{4,6},{12,14},{6,22},{14,30},{22,20},{3... | collective-permute-start | bytes 1572872 | tf_op jit(solution)/shard_map/ppermute | solution.py:177
  1056.4 51.2 %collective-permute-start.66 = (bf16[512,2048]{1,0:T(8,128)(2,1)S(1)}, bf16[512,2048]{1,0:T(8,128)(2,1)S(1)}, u32[]{:S(2)}, u32[]{:S(2)}) collective-permute-start(bf16[512,2048]{1,0:T(8,128)(2,1)S(1)} %slice.1096), channel_id=1, source_target_pairs={{0,8},{8,0},{2,10},{10,2},{4,12},{12,4},{6,14},{14,6},{22,30},{30,... | collective-permute-start | bytes 6291464 | tf_op jit(solution)/shard_map/ppermute | solution.py:146
  1058.5 38.7 %collective-permute-start.78 = (bf16[256,1024]{1,0:T(8,128)(2,1)S(1)}, bf16[256,1024]{1,0:T(8,128)(2,1)S(1)}, u32[]{:S(2)}, u32[]{:S(2)}) collective-permute-start(bf16[256,1024]{1,0:T(8,128)(2,1)S(1)} %fusion.166), channel_id=1, source_target_pairs={{2,0},{10,8},{4,2},{12,10},{6,4},{14,12},{22,6},{30,14},{20,22},{2... | collective-permute-start | bytes 1572872 | tf_op jit(solution)/shard_map/ppermute | solution.py:182
  1108.4 45.6 %collective-permute-start.67 = (bf16[512,2048]{1,0:T(8,128)(2,1)S(1)}, bf16[512,2048]{1,0:T(8,128)(2,1)S(1)}, u32[]{:S(2)}, u32[]{:S(2)}) collective-permute-start(bf16[512,2048]{1,0:T(8,128)(2,1)S(1)} %fusion.44), channel_id=1, source_target_pairs={{0,1},{1,0},{2,3},{3,2},{4,5},{5,4},{6,7},{7,6},{8,9},{9,8},{10,11... | collective-permute-start | bytes 6291464 | tf_op jit(solution)/shard_map/ppermute | solution.py:149
  (199 other events, 3720.7 us)

commit v2 on v1

--- a/solution.py
+++ b/solution.py
@@ -1,3 +1,4 @@
+import functools
 import math
 
 import jax
@@ -101,7 +102,1711 @@
     )(order, rows)
 
 
-def per_device(
+MESH = pl.DeviceIdType.MESH
+CHUNK = 256
+
+
+def any_spec():
+    return pl.BlockSpec(memory_space=pl.ANY)
+
+
+def vmem_spec():
+    return pl.BlockSpec(memory_space=pltpu.VMEM)
+
+
+class Place:
+    def __init__(self, dp_size, sol_size):
+        self.sol_size = sol_size
+        self.count = dp_size // 2 * sol_size
+        dp, self.z = lax.axis_index("dp"), lax.axis_index("sol")
+        self.y = lax.axis_index("tensor")
+        self.x, self.core = dp // 2, dp % 2
+        self.dp = dp
+        turned = jnp.where(self.x % 2 == 0, self.z, sol_size - 1 - self.z)
+        self.at = self.x * sol_size + turned
+        self.next = self._chip((self.at + 1) % self.count)
+        self.prev = self._chip((self.at + self.count - 1) % self.count)
+        self.sibling = (dp + 1 - 2 * self.core, self.z, self.y)
+        self.across = (dp, self.z, 1 - self.y)
+
+    def _coords(self, position):
+        x, turned = position // self.sol_size, position % self.sol_size
+        return x, jnp.where(x % 2 == 0, turned, self.sol_size - 1 - turned)
+
+    def _chip(self, position):
+        x, z = self._coords(position)
+        return (x * 2 + self.core, z, self.y)
+
+    def along(self, step):
+        return (self.dp, self.z + step, self.y)
+
+    def blocks(self):
+        result = []
+        for j in range(self.count):
+            x, z = self._coords((self.at + j) % self.count)
+            result += [(x * 2) * self.sol_size + z, (x * 2 + 1) * self.sol_size + z]
+        return result
+
+    def greet(self):
+        barrier = pltpu.get_barrier_semaphore()
+        peers = (self.next, self.prev, self.sibling, self.across)
+        for peer in peers:
+            pl.semaphore_signal(barrier, inc=1, device_id=peer, device_id_type=MESH)
+        pl.semaphore_wait(barrier, len(peers))
+
+
+def remote(src, dst, send_sem, recv_sem, device):
+    return pltpu.make_async_remote_copy(
+        src_ref=src,
+        dst_ref=dst,
+        send_sem=send_sem,
+        recv_sem=recv_sem,
+        device_id=device,
+        device_id_type=MESH,
+    )
+
+
+def norm_rows(values, gain, shift):
+    row_mean = jnp.mean(values, axis=-1, keepdims=True)
+    centered = values - row_mean
+    variance = jnp.mean(centered * centered, axis=-1, keepdims=True)
+    return centered * lax.rsqrt(variance + EPSILON) * gain + shift
+
+
+def forward_kernel(
+    dp_size,
+    sol_size,
+    x_ref,
+    vectors_ref,
+    up_bias_ref,
+    live_ref,
+    cot_hbm,
+    query_ref,
+    key_ref,
+    value_ref,
+    out_ref,
+    up_ref,
+    down_ref,
+    weights,
+    normed_out,
+    cot_out,
+    query_out,
+    key_out,
+    value_out,
+    probs_out,
+    mixed_out,
+    hidden_out,
+    normed_two_out,
+    slope_out,
+    active_out,
+    w_v,
+    normed_v,
+    query_v,
+    key_v,
+    value_v,
+    probs_v,
+    mixed_v,
+    hidden_v,
+    normed_two_v,
+    slope_v,
+    active_v,
+    core_send_v,
+    core_recv_v,
+    cross_send_v,
+    cross_recv_v,
+    ring_send,
+    ring_recv,
+    swap_local,
+    swap_send,
+    swap_recv,
+    prefix_send,
+    prefix_recv,
+    pair_send,
+    pair_recv,
+    sum_send,
+    sum_recv,
+    cot_sem,
+    load_sem,
+    probs_sem,
+    store_sem,
+):
+    here = Place(dp_size, sol_size)
+    count, core = here.count, here.core
+    rows, width = x_ref.shape
+    prefix_v = slope_v
+    shard = query_ref.shape[0]
+    head_cols = query_ref.shape[1] // 2
+    ff = up_ref.shape[1] // 2
+    half = width // 2
+    local_heads = head_cols // HEAD_DIM
+    scale = 1.0 / math.sqrt(HEAD_DIM)
+    blocks = here.blocks()
+    far = count // 2
+    own_class, other_class = core, 1 - core
+
+    here.greet()
+
+    def slot(j, which):
+        return pl.ds(pl.multiple_of((2 * j + which) * shard, shard), shard)
+
+    shards = (
+        (0, 0, query_ref, head_cols),
+        (0, head_cols, key_ref, head_cols),
+        (0, 2 * head_cols, value_ref, head_cols),
+        (0, 3 * head_cols, out_ref, head_cols),
+        (1, 0, up_ref, ff),
+        (2, 0, down_ref, ff),
+    )
+
+    def swap_copies(i):
+        matrix, start, source, size = shards[i]
+        target = weights.at[matrix, slot(0, own_class), pl.ds(start, size)]
+
+        def columns(which):
+            return source.at[:, pl.ds(pl.multiple_of(which * size, size), size)]
+
+        return (
+            pltpu.make_async_copy(columns(core), target, swap_local.at[i]),
+            remote(columns(1 - core), target, swap_send.at[i], swap_recv.at[i], here.sibling),
+        )
+
+    def start_swap(matrix):
+        for i in range(len(shards)):
+            if shards[i][0] == matrix:
+                for copy in swap_copies(i):
+                    copy.start()
+
+    def hops(matrix, k, sub):
+        which = own_class if sub == 0 else other_class
+        ahead_cols = pl.ds(0, half if k == far else width)
+        back_cols = pl.ds(half if k == far else 0, half if k == far else width)
+        return (
+            remote(
+                weights.at[matrix, slot((count - k + 1) % count, which), ahead_cols],
+                weights.at[matrix, slot(count - k, which), ahead_cols],
+                ring_send.at[matrix, 0, k - 1, sub],
+                ring_recv.at[matrix, 0, k - 1, sub],
+                here.next,
+            ),
+            remote(
+                weights.at[matrix, slot(k - 1, which), back_cols],
+                weights.at[matrix, slot(k, which), back_cols],
+                ring_send.at[matrix, 1, k - 1, sub],
+                ring_recv.at[matrix, 1, k - 1, sub],
+                here.prev,
+            ),
+        )
+
+    def start_ring(matrix, sub):
+        for i in range(len(shards)):
+            if shards[i][0] == matrix:
+                if sub == 0:
+                    swap_copies(i)[0].wait()
+                else:
+                    swap_copies(i)[1].wait_recv()
+        for copy in hops(matrix, 1, sub):
+            copy.start()
+
+    def pump(matrix, k, sub):
+        came = hops(matrix, k, sub)
+        if k < far:
+            further = hops(matrix, k + 1, sub)
+        for i in range(2):
+            came[i].wait_recv()
+            if k < far:
+                further[i].start()
+        if k == far - 1 and matrix < 2:
+            start_ring(matrix + 1, sub)
+
+    steps = [
+        (matrix, k, sub) for matrix in range(3) for k in range(1, far + 1) for sub in range(2)
+    ]
+    done = [0]
+
+    def pump_to(number):
+        while done[0] < min(number, len(steps)):
+            pump(*steps[done[0]])
+            done[0] += 1
+
+    y_rows = rows // 2
+    part = y_rows // 2
+
+    def prefix_rows(which_half, i):
+        return pl.ds(pl.multiple_of(which_half * y_rows + i * part, part), part)
+
+    def prefix_hop(i, from_input):
+        at = prefix_rows(here.y, i)
+        return remote(
+            x_ref.at[at] if from_input else prefix_v.at[at],
+            prefix_v.at[at],
+            prefix_send.at[0, i],
+            prefix_recv.at[0, i],
+            here.along(1),
+        )
+
+    def prefix_cross(i, from_input):
+        at = prefix_rows(here.y, i)
+        return remote(
+            x_ref.at[at] if from_input else prefix_v.at[at],
+            prefix_v.at[at],
+            prefix_send.at[1, i],
+            prefix_recv.at[1, i],
+            here.across,
+        )
+
+    def prefix_stage(stage, i):
+        @pl.when(here.z == stage)
+        def _():
+            if stage == 0:
+                prefix_hop(i, True).start()
+                prefix_cross(i, True).start()
+            else:
+                prefix_hop(i, False).wait_recv()
+                if stage < sol_size - 1:
+                    prefix_hop(i, False).start()
+                prefix_cross(i, False).start()
+
+    def prefix_finish():
+        for i in range(2):
+            prefix_cross(i, False).wait_recv()
+
+        @pl.when(here.z == 0)
+        def _():
+            for i in range(2):
+                at = prefix_rows(here.y, i)
+                prefix_v[at, :] = x_ref[at, :]
+
+    cot_load = pltpu.make_async_copy(cot_hbm, active_v.at[pl.ds(0, rows)], cot_sem.at[1])
+    start_swap(0)
+    for i in range(2):
+        prefix_stage(0, i)
+    start_swap(1)
+    start_swap(2)
+    cot_load.start()
+
+    start_ring(0, 0)
+    start_ring(0, 1)
+
+    def ordered(ref, at):
+        return jnp.concatenate(
+            [ref[at, pl.ds(pl.multiple_of(b * shard, shard), shard)] for b in blocks], axis=1
+        ).astype(WIDE)
+
+    gain, shift = vectors_ref[0:1, :], vectors_ref[1:2, :]
+    gain_two, shift_two = vectors_ref[2:3, :], vectors_ref[3:4, :]
+
+    def norm_into(ref, start):
+        @pl.loop(0, rows // 128)
+        def _(t):
+            at = pl.ds(pl.multiple_of(t * 128, 128), 128)
+            to = pl.ds(pl.multiple_of(start + t * 128, 128), 128)
+            normed_v[to, :] = norm_rows(ordered(ref, at), gain, shift).astype(LOW)
+
+    normed_pair = remote(
+        normed_v.at[pl.ds(0, rows)],
+        normed_v.at[pl.ds(rows, rows)],
+        pair_send.at[1],
+        pair_recv.at[1],
+        here.sibling,
+    )
+    prefix_pair = remote(
+        normed_v.at[pl.ds(2 * rows, rows)],
+        normed_v.at[pl.ds(3 * rows, rows)],
+        pair_send.at[2],
+        pair_recv.at[2],
+        here.sibling,
+    )
+    norm_into(x_ref, 0)
+    normed_pair.start()
+    pump_to(1)
+    for stage in range(1, sol_size + 1):
+        if stage < sol_size:
+            prefix_stage(stage, 0)
+        if stage > 1:
+            prefix_stage(stage - 1, 1)
+        pump_to(1 + stage)
+    pump_to(2 * far)
+
+    cot_pair = remote(
+        core_send_v,
+        cot_out.at[pl.ds(rows, rows)],
+        pair_send.at[0],
+        pair_recv.at[0],
+        here.sibling,
+    )
+    cot_own = pltpu.make_async_copy(core_send_v, cot_out.at[pl.ds(0, rows)], cot_sem.at[0])
+
+    cot_load.wait()
+
+    @pl.loop(0, rows // 128)
+    def _(t):
+        at = pl.ds(pl.multiple_of(t * 128, 128), 128)
+        core_send_v[at, :] = ordered(active_v, at).astype(LOW)
+
+    cot_pair.start()
+    cot_own.start()
+
+    load_first = pltpu.make_async_copy(weights.at[0], w_v, load_sem.at[0])
+    load_first.start()
+    normed_pair.wait_recv()
+    load_first.wait()
+
+    def row_tile(t):
+        return pl.ds(pl.multiple_of(t * CHUNK, CHUNK), CHUNK)
+
+    def project(first, last, with_queries):
+        @pl.loop(first, last)
+        def _(t):
+            at = row_tile(t)
+            tile = normed_v[at, :]
+            kv = dot_plain(tile, w_v[:, head_cols : 3 * head_cols])
+            key_v[at, :] = kv[:, :head_cols].astype(LOW)
+            value_v[at, :] = kv[:, head_cols:].astype(LOW)
+            if with_queries:
+                query_v[at, :] = dot_plain(tile, w_v[:, :head_cols]).astype(LOW)
+
+    tiles = rows // CHUNK
+    project(0, 2 * tiles, True)
+    pump_to(2 * far + 1)
+    prefix_finish()
+    norm_into(prefix_v, 2 * rows)
+    prefix_pair.start()
+    pump_to(2 * far + 2)
+    prefix_pair.wait_recv()
+    project(2 * tiles, 4 * tiles, False)
+    pump_to(2 * far + 3)
+
+    stores = []
+
+    def store(src, dst):
+        copy = pltpu.make_async_copy(src, dst, store_sem.at[len(stores)])
+        copy.start()
+        stores.append(copy)
+
+    store(normed_v, normed_out)
+    store(query_v, query_out)
+    store(key_v, key_out)
+    store(value_v, value_out)
+
+    def probs_copy(unit):
+        return pltpu.make_async_copy(
+            probs_v.at[unit % 2], probs_out.at[unit], probs_sem.at[unit % 2]
+        )
+
+    def attend(unit):
+        block, head = unit // local_heads, unit % local_heads
+        cols = pl.ds(pl.multiple_of(head * HEAD_DIM, HEAD_DIM), HEAD_DIM)
+        place = jnp.where(block == 0, here.dp, here.dp + 1 - 2 * core)
+        own_live = live_ref[place * sol_size + here.z]
+        prefix_live = jnp.where(here.z == 0, 0, live_ref[place * sol_size])
+        own_at = pl.ds(pl.multiple_of(block * rows, rows), rows)
+        prefix_at = pl.ds(pl.multiple_of((2 + block) * rows, rows), rows)
+
+        @pl.when(unit >= 2)
+        def _():
+            probs_copy(unit - 2).wait()
+
+        for t in range(tiles):
+            at = pl.ds(pl.multiple_of(block * rows + t * CHUNK, CHUNK), CHUNK)
+            queries = query_v[at, cols]
+            col = lax.broadcasted_iota(jnp.int32, (CHUNK, rows), 1)
+            row = lax.broadcasted_iota(jnp.int32, (CHUNK, rows), 0) + t * CHUNK
+            first = dot_right_t(queries, key_v[prefix_at, cols]) * scale
+            second = dot_right_t(queries, key_v[own_at, cols]) * scale
+            first = jnp.where(col < prefix_live, first, NEG_FILL)
+            second = jnp.where(
+                jnp.logical_and(col <= row, col < own_live), second, NEG_FILL
+            )
+            peak = jnp.maximum(
+                jnp.max(first, axis=-1, keepdims=True), jnp.max(second, axis=-1, keepdims=True)
+            )
+            first = jnp.exp(first - peak)
+            second = jnp.exp(second - peak)
+            total = jnp.sum(first, axis=-1, keepdims=True) + jnp.sum(
+                second, axis=-1, keepdims=True
+            )
+            inverse = 1.0 / total
+            first = (first * inverse).astype(LOW)
+            second = (second * inverse).astype(LOW)
+            probs_v[unit % 2, pl.ds(t * CHUNK, CHUNK), pl.ds(0, rows)] = first
+            probs_v[unit % 2, pl.ds(t * CHUNK, CHUNK), pl.ds(rows, rows)] = second
+            mixed_v[at, cols] = (
+                dot_plain(first, value_v[prefix_at, cols])
+                + dot_plain(second, value_v[own_at, cols])
+            ).astype(LOW)
+        probs_copy(unit).start()
+
+    units = 2 * local_heads
+    for quarter in range(4):
+        pl.loop(quarter * units // 4, (quarter + 1) * units // 4)(attend)
+        pump_to(2 * far + 4 + quarter)
+    for unit in (units - 2, units - 1):
+        probs_copy(unit).wait()
+    store(mixed_v, mixed_out)
+
+    out_cols = slice(3 * head_cols, 4 * head_cols)
+
+    def core_copy(t):
+        at = pl.ds(t * CHUNK, CHUNK)
+        return remote(
+            core_send_v.at[at], core_recv_v.at[at], sum_send.at[0, t], sum_recv.at[0, t], here.sibling
+        )
+
+    def cross_copy(t):
+        at = pl.ds(t * CHUNK, CHUNK)
+        return remote(
+            cross_send_v.at[at], cross_recv_v.at[at], sum_send.at[1, t], sum_recv.at[1, t], here.across
+        )
+
+    def two_copy(t):
+        return remote(
+            normed_two_v.at[pl.ds(t * CHUNK, CHUNK)],
+            normed_two_v.at[pl.ds(rows + t * CHUNK, CHUNK)],
+            sum_send.at[2, t],
+            sum_recv.at[2, t],
+            here.sibling,
+        )
+
+    def hidden_store(t):
+        return pltpu.make_async_copy(
+            hidden_v, hidden_out.at[pl.ds(t * CHUNK, CHUNK)], load_sem.at[1]
+        )
+
+    cot_own.wait()
+    cot_pair.wait_send()
+    for t in range(tiles):
+        core_send_v[pl.ds(t * CHUNK, CHUNK), :] = dot_right_t(
+            mixed_v[pl.ds(rows + t * CHUNK, CHUNK), :], w_v[:, out_cols]
+        ).astype(LOW)
+        core_copy(t).start()
+    for t in range(tiles):
+        at = pl.ds(t * CHUNK, CHUNK)
+        partial = dot_right_t(mixed_v[at, :], w_v[:, out_cols])
+        core_copy(t).wait_recv()
+        cross_send_v[at, :] = (partial + core_recv_v[at, :].astype(WIDE)).astype(LOW)
+        cross_copy(t).start()
+    pump_to(4 * far)
+    load_second = pltpu.make_async_copy(weights.at[1], w_v, load_sem.at[0])
+    load_second.start()
+    for t in range(tiles):
+        at = pl.ds(t * CHUNK, CHUNK)
+        cross_copy(t).wait_recv()
+        hidden = (
+            ordered(x_ref, at)
+            + cross_send_v[at, :].astype(WIDE)
+            + cross_recv_v[at, :].astype(WIDE)
+        )
+        if t > 0:
+            hidden_store(t - 1).wait()
+        hidden_v[...] = hidden
+        hidden_store(t).start()
+        normed_two_v[at, :] = norm_rows(hidden, gain_two, shift_two).astype(LOW)
+        two_copy(t).start()
+    hidden_store(tiles - 1).wait()
+    load_second.wait()
+    for t in range(tiles):
+        two_copy(t).wait_recv()
+    pump_to(4 * far + 1)
+    store(normed_two_v, normed_two_out)
+
+    bend = math.sqrt(2.0 / math.pi)
+    spans = ff // half
+
+    def feed(i):
+        at = row_tile(i // spans)
+        cols = pl.ds(pl.multiple_of((i % spans) * half, half), half)
+        upward = dot_plain(normed_two_v[at, :], w_v[:, cols]) + up_bias_ref[:, cols]
+        square = upward * upward
+        curve = jnp.tanh(bend * (upward + 0.044715 * (upward * square)))
+        active_v[at, cols] = (0.5 * upward * (1.0 + curve)).astype(LOW)
+        slope_v[at, cols] = (
+            0.5 * (1.0 + curve)
+            + 0.5 * upward * (1.0 - curve * curve) * (bend + (3.0 * 0.044715 * bend) * square)
+        ).astype(LOW)
+
+    for i in range(2):
+
+        @pl.when(here.z < sol_size - 1)
+        def _():
+            prefix_hop(i, False).wait_send()
+
+        prefix_cross(i, False).wait_send()
+
+    feeds = 2 * tiles * spans
+    for quarter in range(4):
+        pl.loop(quarter * feeds // 4, (quarter + 1) * feeds // 4)(feed)
+        pump_to(4 * far + 2 + quarter)
+    store(active_v, active_out)
+    store(slope_v, slope_out)
+
+    pump_to(len(steps))
+    cot_pair.wait_recv()
+    normed_pair.wait_send()
+    prefix_pair.wait_send()
+    for i in range(len(shards)):
+        swap_copies(i)[1].wait_send()
+    for step in steps:
+        for copy in hops(*step):
+            copy.wait_send()
+    for t in range(tiles):
+        core_copy(t).wait_send()
+        cross_copy(t).wait_send()
+        two_copy(t).wait_send()
+    for copy in stores:
+        copy.wait()
+
+
+def run_forward(dp_size, sol_size, x, vectors, up_bias, live_rows, cot, matrices):
+    rows, width = x.shape
+    head_cols = matrices[0].shape[1] // 2
+    ff = matrices[4].shape[1] // 2
+    heads = head_cols // HEAD_DIM
+    count = dp_size // 2 * sol_size
+    far = count // 2
+
+    def shape(*dims, dtype=LOW):
+        return jax.ShapeDtypeStruct(dims, dtype)
+
+    outs = [
+        shape(3, width, width),
+        shape(4 * rows, width),
+        shape(2 * rows, width),
+        shape(2 * rows, head_cols),
+        shape(4 * rows, head_cols),
+        shape(4 * rows, head_cols),
+        shape(2 * heads, rows, 2 * rows),
+        shape(2 * rows, head_cols),
+        shape(rows, width, dtype=WIDE),
+        shape(2 * rows, width),
+        shape(2 * rows, ff),
+        shape(2 * rows, ff),
+    ]
+    dma = pltpu.SemaphoreType.DMA
+    return pl.pallas_call(
+        functools.partial(forward_kernel, dp_size, sol_size),
+        out_shape=outs,
+        in_specs=[
+            vmem_spec(),
+            vmem_spec(),
+            vmem_spec(),
+            pl.BlockSpec(memory_space=pltpu.SMEM),
+        ]
+        + [any_spec()]
+        + [vmem_spec()] * 6,
+        out_specs=[any_spec()] * len(outs),
+        scratch_shapes=[
+            pltpu.VMEM((width, width), LOW),
+            pltpu.VMEM((4 * rows, width), LOW),
+            pltpu.VMEM((2 * rows, head_cols), LOW),
+            pltpu.VMEM((4 * rows, head_cols), LOW),
+            pltpu.VMEM((4 * rows, head_cols), LOW),
+            pltpu.VMEM((2, rows, 2 * rows), LOW),
+            pltpu.VMEM((2 * rows, head_cols), LOW),
+            pltpu.VMEM((CHUNK, width), WIDE),
+            pltpu.VMEM((2 * rows, width), LOW),
+            pltpu.VMEM((2 * rows, ff), LOW),
+            pltpu.VMEM((2 * rows, ff), LOW),
+        ]
+        + [pltpu.VMEM((rows, width), LOW)] * 4
+        + [
+            dma((3, 2, far, 2)),
+            dma((3, 2, far, 2)),
+            dma((6,)),
+            dma((6,)),
+            dma((6,)),
+            dma((2, 2)),
+            dma((2, 2)),
+            dma((3,)),
+            dma((3,)),
+            dma((3, rows // CHUNK)),
+            dma((3, rows // CHUNK)),
+            dma((2,)),
+            dma((2,)),
+            dma((2,)),
+            dma((16,)),
+        ],
+        compiler_params=pltpu.CompilerParams(
+            collective_id=0, has_side_effects=True, vmem_limit_bytes=60 * 2**20
+        ),
+    )(x, vectors, up_bias, live_rows, cot, *matrices)
+
+
+class RingSum:
+    def __init__(self, here, chunk, send_v, recv_v, stage_v, sems, target):
+        self.here, self.chunk = here, chunk
+        self.send_v, self.recv_v, self.stage_v = send_v, recv_v, stage_v
+        self.send_sem, self.recv_sem, self.end_sem = sems
+        self.target = target
+        self.far = here.count // 2
+        self.cols = stage_v.shape[2]
+        self.steps = [(t, sub) for t in range(1, self.far + 1) for sub in range(2)]
+        self.done = 0
+
+    def _class(self, sub):
+        return self.here.core if sub == 0 else 1 - self.here.core
+
+    def _columns(self, t, way):
+        if t > 1:
+            return pl.ds(0, self.cols)
+        return pl.ds(way * (self.cols // 2), self.cols // 2)
+
+    def _copy(self, t, way, sub):
+        at = self._columns(t, way)
+        return remote(
+            self.send_v.at[way, sub, :, at],
+            self.recv_v.at[(t - 1) % 3, way, sub, :, at],
+            self.send_sem.at[t - 1, way, sub],
+            self.recv_sem.at[t - 1, way, sub],
+            self.here.prev if way else self.here.next,
+        )
+
+    def _event(self, t, sub):
+        far, count = self.far, self.here.count
+        half = self.cols // 2
+        if t == 1:
+            value = self.chunk(far, self._class(sub))
+            self.send_v[0, sub, :, :half] = value[:, :half].astype(LOW)
+            self.send_v[1, sub, :, half:] = value[:, half:].astype(LOW)
+            for way in range(2):
+                self._copy(1, way, sub).start()
+            return
+        for way in range(2):
+            j = far + 1 - t if way == 0 else count - (far + 1 - t)
+            value = self.chunk(j, self._class(sub))
+            self._copy(t - 1, way, sub).wait()
+            if t == 2:
+                near = slice(0, half) if way == 0 else slice(half, 2 * half)
+                rest = slice(half, 2 * half) if way == 0 else slice(0, half)
+                self.send_v[way, sub, :, near] = (
+                    value[:, near] + self.recv_v[0, way, sub, :, near].astype(WIDE)
+                ).astype(LOW)
+                self.send_v[way, sub, :, rest] = value[:, rest].astype(LOW)
+            else:
+                self.send_v[way, sub] = (
+                    value + self.recv_v[(t - 2) % 3, way, sub].astype(WIDE)
+                ).astype(LOW)
+            self._copy(t, way, sub).start()
+
+    def _last(self, sub):
+        value = self.chunk(0, self._class(sub))
+        for way in range(2):
+            self._copy(self.far, way, sub).wait()
+        value = value + self.recv_v[(self.far - 1) % 3, 0, sub].astype(WIDE)
+        self.stage_v[sub] = value + self.recv_v[(self.far - 1) % 3, 1, sub].astype(WIDE)
+        for copy in self._results(sub):
+            copy.start()
+
+    def _results(self, sub):
+        copies = []
+        core = self.here.core
+        for i, (ref, start, size) in enumerate(self.target):
+            to = ref.at[:, pl.ds(pl.multiple_of(core * size, size), size)]
+            source = self.stage_v.at[sub, :, pl.ds(start, size)]
+            if sub == 0:
+                copies.append(pltpu.make_async_copy(source, to, self.end_sem.at[0, i]))
+            else:
+                copies.append(
+                    remote(
+                        source, to, self.end_sem.at[1, i], self.end_sem.at[2, i], self.here.sibling
+                    )
+                )
+        return copies
+
+    def to(self, number):
+        while self.done < min(number, len(self.steps) + 2):
+            if self.done < len(self.steps):
+                self._event(*self.steps[self.done])
+            else:
+                self._last(self.done - len(self.steps))
+            self.done += 1
+
+    def finish(self):
+        self.to(len(self.steps) + 2)
+        for sub in range(2):
+            for copy in self._results(sub):
+                copy.wait()
+
+
+def ring_sum_scratch(far, shard, cols, results):
+    dma = pltpu.SemaphoreType.DMA
+    return [
+        pltpu.VMEM((2, 2, shard, cols), LOW),
+        pltpu.VMEM((3, 2, 2, shard, cols), LOW),
+        pltpu.VMEM((2, shard, cols), WIDE),
+        dma((far, 2, 2)),
+        dma((far, 2, 2)),
+        dma((3, results)),
+    ]
+
+
+def norm_back(values, gain, grad):
+    row_mean = jnp.mean(values, axis=-1, keepdims=True)
+    centered = values - row_mean
+    variance = jnp.mean(centered * centered, axis=-1, keepdims=True)
+    inverse = lax.rsqrt(variance + EPSILON)
+    unit = centered * inverse
+    scaled = grad * gain
+    terms = grad * unit
+    along = jnp.mean(scaled * unit, axis=-1, keepdims=True)
+    level = jnp.mean(scaled, axis=-1, keepdims=True)
+    return (
+        (scaled - level - unit * along) * inverse,
+        jnp.sum(terms, axis=0, keepdims=True),
+        jnp.sum(grad, axis=0, keepdims=True),
+    )
+
+
+def tile_rows(t):
+    return pl.ds(t * CHUNK, CHUNK)
+
+
+def down_kernel(
+    dp_size,
+    sol_size,
+    vectors_ref,
+    weights,
+    cot_hbm,
+    active_hbm,
+    slope_hbm,
+    hidden_hbm,
+    grad_up_out,
+    branch_out,
+    grad_hidden_out,
+    mlp_low_out,
+    down_grad_out,
+    sums_ref,
+    cot_v,
+    active_v,
+    slope_v,
+    down_v,
+    up_v,
+    hidden_v,
+    core_send_v,
+    core_recv_v,
+    second_recv_v,
+    cross_send_v,
+    cross_recv_v,
+    ring_send_v,
+    ring_recv_v,
+    stage_v,
+    ring_send,
+    ring_recv,
+    ring_end,
+    load_sem,
+    store_sem,
+    sum_send,
+    sum_recv,
+):
+    here = Place(dp_size, sol_size)
+    rows, width = core_send_v.shape
+    shard = stage_v.shape[1]
+    ff = active_v.shape[1]
+    tiles = rows // CHUNK
+    halves = (pl.ds(0, width // 2), pl.ds(width // 2, width // 2))
+    loads = [
+        pltpu.make_async_copy(src, dst, load_sem.at[i])
+        for i, (src, dst) in enumerate(
+            (
+                (cot_hbm, cot_v),
+                (active_hbm, active_v),
+                (weights.at[2], down_v),
+                (slope_hbm, slope_v),
+                (weights.at[1], up_v),
+            )
+        )
+    ]
+    for copy in loads:
+        copy.start()
+    here.greet()
+
+    def chunk(j, which):
+        at = pl.ds(pl.multiple_of((2 * j + which) * shard, shard), shard)
+        return dot_left_t(cot_v[:, at], active_v[...])
+
+    ring = RingSum(
+        here,
+        chunk,
+        ring_send_v,
+        ring_recv_v,
+        stage_v,
+        (ring_send, ring_recv, ring_end),
+        ((down_grad_out, 0, ff),),
+    )
+    loads[0].wait()
+    loads[1].wait()
+    ring.to(2)
+    loads[2].wait()
+    loads[3].wait()
+
+    sums_ref[...] = jnp.zeros_like(sums_ref)
+    spans = 2
+
+    def back_feed(i):
+        at = pl.ds(pl.multiple_of(i // spans * CHUNK, CHUNK), CHUNK)
+        cols = pl.ds(pl.multiple_of(i % spans * (ff // spans), ff // spans), ff // spans)
+        grad = dot_plain(cot_v[at, :], down_v[:, cols]) * slope_v[at, cols].astype(WIDE)
+        low = grad.astype(LOW)
+        slope_v[at, cols] = low
+        sums_ref[3:4, cols] += jnp.sum(low.astype(WIDE), axis=0, keepdims=True)
+
+    pl.loop(0, tiles * spans)(back_feed)
+    ring.to(3)
+    pl.loop(tiles * spans, 2 * tiles * spans)(back_feed)
+    ring.to(4)
+    loads[4].wait()
+    stores = [pltpu.make_async_copy(slope_v, grad_up_out, store_sem.at[0])]
+    stores[0].start()
+
+    def core_copy(t):
+        return remote(
+            core_send_v.at[tile_rows(t)],
+            core_recv_v.at[tile_rows(t)],
+            sum_send.at[0, t],
+            sum_recv.at[0, t],
+            here.sibling,
+        )
+
+    def cross_copy(t):
+        return remote(
+            cross_send_v.at[tile_rows(t)],
+            cross_recv_v.at[tile_rows(t)],
+            sum_send.at[1, t],
+            sum_recv.at[1, t],
+            here.across,
+        )
+
+    def second_copy(t):
+        return remote(
+            core_send_v.at[tile_rows(t)],
+            second_recv_v.at[tile_rows(t)],
+            sum_send.at[2, t],
+            sum_recv.at[2, t],
+            here.sibling,
+        )
+
+    def branch_copy(t):
+        return remote(
+            core_recv_v.at[tile_rows(t)],
+            branch_out.at[pl.ds(rows + t * CHUNK, CHUNK)],
+            sum_send.at[3, t],
+            sum_recv.at[3, t],
+            here.sibling,
+        )
+
+    for t in range(tiles):
+        for cols in halves:
+            core_send_v[tile_rows(t), cols] = dot_right_t(
+                slope_v[pl.ds(rows + t * CHUNK, CHUNK), :], up_v[cols, :]
+            ).astype(LOW)
+        core_copy(t).start()
+    for t in range(tiles):
+        at = tile_rows(t)
+        core_copy(t).wait_recv()
+        for cols in halves:
+            cross_send_v[at, cols] = (
+                dot_right_t(slope_v[at, :], up_v[cols, :]) + core_recv_v[at, cols].astype(WIDE)
+            ).astype(LOW)
+        cross_copy(t).start()
+    ring.to(5)
+
+    for t in range(tiles):
+        core_copy(t).wait_send()
+        for cols in halves:
+            core_send_v[tile_rows(t), cols] = dot_right_t(
+                active_v[pl.ds(rows + t * CHUNK, CHUNK), :], down_v[cols, :]
+            ).astype(LOW)
+        second_copy(t).start()
+    ring.to(6)
+    for t in range(tiles):
+        at = tile_rows(t)
+        second_copy(t).wait_recv()
+        for cols in halves:
+            second_recv_v[at, cols] = (
+                dot_right_t(active_v[at, :], down_v[cols, :])
+                + second_recv_v[at, cols].astype(WIDE)
+            ).astype(LOW)
+    stores.append(pltpu.make_async_copy(second_recv_v, mlp_low_out, store_sem.at[1]))
+    stores[1].start()
+    ring.to(8)
+
+    gain = vectors_ref[2:3, :]
+
+    def hidden_load(t):
+        return pltpu.make_async_copy(hidden_hbm.at[tile_rows(t)], hidden_v, load_sem.at[0])
+
+    def hidden_store(t):
+        return pltpu.make_async_copy(hidden_v, grad_hidden_out.at[tile_rows(t)], store_sem.at[2])
+
+    hidden_load(0).start()
+    for t in range(tiles):
+        at = tile_rows(t)
+        hidden_load(t).wait()
+        cross_copy(t).wait_recv()
+        for part in range(2):
+            inner = pl.ds(part * (CHUNK // 2), CHUNK // 2)
+            here_at = pl.ds(t * CHUNK + part * (CHUNK // 2), CHUNK // 2)
+            grad = cross_send_v[here_at, :].astype(WIDE) + cross_recv_v[here_at, :].astype(WIDE)
+            back, gain_terms, shift_terms = norm_back(hidden_v[inner, :], gain, grad)
+            cot = cot_v[here_at, :].astype(WIDE)
+            sums_ref[0:1, :] += gain_terms
+            sums_ref[1:2, :] += shift_terms
+            sums_ref[2:3, :] += jnp.sum(cot, axis=0, keepdims=True)
+            back = back + cot
+            hidden_v[inner, :] = back
+            core_recv_v[here_at, :] = back.astype(LOW)
+        branch_copy(t).start()
+        hidden_store(t).start()
+        if t == 0:
+            ring.to(9)
+        hidden_store(t).wait()
+        if t + 1 < tiles:
+            hidden_load(t + 1).start()
+    stores.append(
+        pltpu.make_async_copy(core_recv_v, branch_out.at[pl.ds(0, rows)], store_sem.at[3])
+    )
+    stores[2].start()
+    ring.finish()
+    for t in range(tiles):
+        cross_copy(t).wait_send()
+        second_copy(t).wait_send()
+        branch_copy(t).wait()
+    for copy in stores:
+        copy.wait()
+
+
+def run_down(dp_size, sol_size, shard, vectors, weights, cot, active, slope, hidden):
+    rows, width = hidden.shape
+    ff = active.shape[1]
+    count = dp_size // 2 * sol_size
+    tiles = rows // CHUNK
+    dma = pltpu.SemaphoreType.DMA
+
+    def shape(*dims, dtype=LOW):
+        return jax.ShapeDtypeStruct(dims, dtype)
+
+    outs = [
+        shape(2 * rows, ff),
+        shape(2 * rows, width),
+        shape(rows, width, dtype=WIDE),
+        shape(rows, width),
+        shape(shard, 2 * ff, dtype=WIDE),
+        shape(8, width, dtype=WIDE),
+    ]
+    return pl.pallas_call(
+        functools.partial(down_kernel, dp_size, sol_size),
+        out_shape=outs,
+        in_specs=[vmem_spec()] + [any_spec()] * 5,
+        out_specs=[any_spec()] * 5 + [vmem_spec()],
+        scratch_shapes=[
+            pltpu.VMEM((2 * rows, width), LOW),
+            pltpu.VMEM((2 * rows, ff), LOW),
+            pltpu.VMEM((2 * rows, ff), LOW),
+            pltpu.VMEM((width, ff), LOW),
+            pltpu.VMEM((width, ff), LOW),
+            pltpu.VMEM((CHUNK, width), WIDE),
+        ]
+        + [pltpu.VMEM((rows, width), LOW)] * 5
+        + ring_sum_scratch(count // 2, shard, ff, 1)
+        + [
+            dma((5,)),
+            dma((4,)),
+            dma((4, tiles)),
+            dma((4, tiles)),
+        ],
+        compiler_params=pltpu.CompilerParams(
+            collective_id=1, has_side_effects=True, vmem_limit_bytes=60 * 2**20
+        ),
+    )(vectors, weights, cot, active, slope, hidden)
+
+
+def read_ordered(ref, at, blocks, part):
+    return jnp.concatenate(
+        [ref[at, pl.ds(pl.multiple_of(b * part, part), part)] for b in blocks], axis=1
+    ).astype(WIDE)
+
+
+def write_ordered(ref, at, blocks, part, values):
+    for j, b in enumerate(blocks):
+        ref[at, pl.ds(pl.multiple_of(b * part, part), part)] = values[
+            :, j * part : (j + 1) * part
+        ].astype(ref.dtype)
+
+
+def attend_back_kernel(
+    dp_size,
+    sol_size,
+    vectors_ref,
+    weights,
+    normed_two_hbm,
+    grad_up_hbm,
+    branch_hbm,
+    query_hbm,
+    key_hbm,
+    value_hbm,
+    probs_hbm,
+    mlp_low_hbm,
+    hidden_hbm,
+    query_grad_out,
+    kv_grad_out,
+    own_low_out,
+    prefix_half_out,
+    up_grad_out,
+    outputs_out,
+    mlp_recv_out,
+    normed_two_v,
+    grad_up_v,
+    branch_v,
+    w_v,
+    query_v,
+    key_v,
+    value_v,
+    mixed_grad_v,
+    probs_v,
+    query_grad_v,
+    kv_grad_v,
+    core_recv_v,
+    second_recv_v,
+    half_recv_v,
+    mlp_low_v,
+    mlp_recv_v,
+    hidden_v,
+    ring_send_v,
+    ring_recv_v,
+    stage_v,
+    ring_send,
+    ring_recv,
+    ring_end,
+    load_sem,
+    probs_sem,
+    tile_sem,
+    store_sem,
+    sum_send,
+    sum_recv,
+    cross_send,
+    cross_recv,
+):
+    here = Place(dp_size, sol_size)
+    rows, width = core_recv_v.shape
+    core_send_v = branch_v.at[pl.ds(0, rows)]
+    half_send_v = branch_v.at[pl.ds(rows, CHUNK)]
+    half_keep_v = branch_v.at[pl.ds(rows + CHUNK, CHUNK)]
+    shard = stage_v.shape[1]
+    ff = grad_up_v.shape[1]
+    head_cols = query_v.shape[1]
+    local_heads = head_cols // HEAD_DIM
+    scale = 1.0 / math.sqrt(HEAD_DIM)
+    tiles = rows // CHUNK
+    blocks = here.blocks()
+    halves = (pl.ds(0, width // 2), pl.ds(width // 2, width // 2))
+    loads = [
+        pltpu.make_async_copy(src, dst, load_sem.at[i])
+        for i, (src, dst) in enumerate(
+            (
+                (normed_two_hbm, normed_two_v),
+                (grad_up_hbm, grad_up_v),
+                (branch_hbm, branch_v),
+                (weights.at[0], w_v),
+                (query_hbm, query_v),
+                (key_hbm, key_v),
+                (value_hbm, value_v),
+            )
+        )
+    ]
+    for copy in loads:
+        copy.start()
+
+    def probs_load(unit):
+        return pltpu.make_async_copy(
+            probs_hbm.at[unit], probs_v.at[unit % 2], probs_sem.at[unit % 2]
+        )
+
+    probs_load(0).start()
+    here.greet()
+    mlp_cross = remote(
+        mlp_low_hbm, mlp_recv_out, cross_send.at[0], cross_recv.at[0], here.across
+    )
+    mlp_cross.start()
+
+    def chunk(j, which):
+        at = pl.ds(pl.multiple_of((2 * j + which) * shard, shard), shard)
+        return dot_left_t(normed_two_v[:, at], grad_up_v[...])
+
+    ring = RingSum(
+        here,
+        chunk,
+        ring_send_v,
+        ring_recv_v,
+        stage_v,
+        (ring_send, ring_recv, ring_end),
+        ((up_grad_out, 0, ff),),
+    )
+    loads[0].wait()
+    loads[1].wait()
+    ring.to(2)
+    loads[2].wait()
+    loads[3].wait()
+
+    @pl.loop(0, 2 * tiles)
+    def _(t):
+        at = pl.ds(pl.multiple_of(t * CHUNK, CHUNK), CHUNK)
+        mixed_grad_v[at, :] = dot_plain(
+            branch_v[at, :], w_v[:, 3 * head_cols : 4 * head_cols]
+        ).astype(LOW)
+
+    for i in range(4, 7):
+        loads[i].wait()
+
+    units = 2 * local_heads
+
+    def back(unit):
+        block, head = unit // local_heads, unit % local_heads
+        cols = pl.ds(pl.multiple_of(head * HEAD_DIM, HEAD_DIM), HEAD_DIM)
+        value_cols = pl.ds(
+            pl.multiple_of(head_cols + head * HEAD_DIM, HEAD_DIM), HEAD_DIM
+        )
+        own_at = pl.ds(pl.multiple_of(block * rows, rows), rows)
+        prefix_at = pl.ds(pl.multiple_of((2 + block) * rows, rows), rows)
+        probs_load(unit).wait()
+
+        @pl.when(unit + 1 < units)
+        def _():
+            probs_load(unit + 1).start()
+
+        sums = None
+        for t in range(tiles):
+            at = pl.ds(pl.multiple_of(block * rows + t * CHUNK, CHUNK), CHUNK)
+            grad = mixed_grad_v[at, cols]
+            queries = query_v[at, cols]
+            inner = pl.ds(t * CHUNK, CHUNK)
+            first_low = probs_v[unit % 2, inner, pl.ds(0, rows)]
+            second_low = probs_v[unit % 2, inner, pl.ds(rows, rows)]
+            first, second = first_low.astype(WIDE), second_low.astype(WIDE)
+            first_grad = dot_right_t(grad, value_v[prefix_at, cols])
+            second_grad = dot_right_t(grad, value_v[own_at, cols])
+            delta = jnp.sum(first * first_grad, axis=-1, keepdims=True) + jnp.sum(
+                second * second_grad, axis=-1, keepdims=True
+            )
+            first_scores = (first * (first_grad - delta)).astype(LOW)
+            second_scores = (second * (second_grad - delta)).astype(LOW)
+            query_grad_v[at, cols] = (
+                (
+                    dot_plain(first_scores, key_v[prefix_at, cols])
+                    + dot_plain(second_scores, key_v[own_at, cols])
+                )
+                * scale
+            ).astype(LOW)
+            terms = [
+                dot_left_t(second_scores, queries),
+                dot_left_t(second_low, grad),
+                dot_left_t(first_scores, queries),
+                dot_left_t(first_low, grad),
+            ]
+            sums = terms if sums is None else [a + b for a, b in zip(sums, terms)]
+        kv_grad_v[own_at, cols] = (sums[0] * scale).astype(LOW)
+        kv_grad_v[own_at, value_cols] = sums[1].astype(LOW)
+        kv_grad_v[prefix_at, cols] = (sums[2] * scale).astype(LOW)
+        kv_grad_v[prefix_at, value_cols] = sums[3].astype(LOW)
+
+    for quarter in range(4):
+        pl.loop(quarter * units // 4, (quarter + 1) * units // 4)(back)
+        ring.to(3 + quarter)
+    stores = []
+
+    def store(src, dst):
+        copy = pltpu.make_async_copy(src, dst, store_sem.at[len(stores)])
+        copy.start()
+        stores.append(copy)
+
+    store(query_grad_v, query_grad_out)
+    store(kv_grad_v, kv_grad_out)
+
+    def core_copy(t):
+        return remote(
+            core_send_v.at[tile_rows(t)],
+            core_recv_v.at[tile_rows(t)],
+            sum_send.at[0, t],
+            sum_recv.at[0, t],
+            here.sibling,
+        )
+
+    def second_copy(t):
+        return remote(
+            core_send_v.at[tile_rows(t)],
+            second_recv_v.at[tile_rows(t)],
+            sum_send.at[1, t],
+            sum_recv.at[1, t],
+            here.sibling,
+        )
+
+    half_copy = remote(half_send_v, half_recv_v, cross_send.at[1], cross_recv.at[1], here.across)
+    kv_cols = pl.ds(head_cols, 2 * head_cols)
+
+    def prefix_terms(at, cols):
+        return dot_right_t(kv_grad_v[at, :], w_v[cols, kv_cols])
+
+    for t in range(tiles):
+        for cols in halves:
+            core_send_v[tile_rows(t), cols] = prefix_terms(
+                pl.ds(3 * rows + t * CHUNK, CHUNK), cols
+            ).astype(LOW)
+        second_copy(t).start()
+    for t in range(tiles):
+        second_copy(t).wait_recv()
+    for keep in range(2):
+        which = here.y if keep else 1 - here.y
+        at = pl.ds(pl.multiple_of(2 * rows + which * CHUNK, CHUNK), CHUNK)
+        came = pl.ds(pl.multiple_of(which * CHUNK, CHUNK), CHUNK)
+        for cols in halves:
+            value = prefix_terms(at, cols) + second_recv_v[came, cols].astype(WIDE)
+            if keep:
+                half_keep_v[:, cols] = value.astype(LOW)
+            else:
+                half_send_v[:, cols] = value.astype(LOW)
+        if not keep:
+            half_copy.start()
+    ring.to(7)
+
+    def own_terms(at, cols):
+        return dot_right_t(query_grad_v[at, :], w_v[cols, 0:head_cols]) + dot_right_t(
+            kv_grad_v[at, :], w_v[cols, kv_cols]
+        )
+
+    for t in range(tiles):
+        second_copy(t).wait_send()
+        for cols in halves:
+            core_send_v[tile_rows(t), cols] = own_terms(
+                pl.ds(rows + t * CHUNK, CHUNK), cols
+            ).astype(LOW)
+        core_copy(t).start()
+    for t in range(tiles):
+        at = tile_rows(t)
+        core_copy(t).wait_recv()
+        for cols in halves:
+            core_recv_v[at, cols] = (
+                own_terms(at, cols) + core_recv_v[at, cols].astype(WIDE)
+            ).astype(LOW)
+    store(core_recv_v, own_low_out)
+    ring.to(8)
+
+    half_copy.wait()
+    write_ordered(
+        half_send_v,
+        slice(None),
+        blocks,
+        shard,
+        half_keep_v[...].astype(WIDE) + half_recv_v[...].astype(WIDE),
+    )
+    store(half_send_v, prefix_half_out)
+
+    small = mlp_low_v.shape[0]
+    pieces = rows // small
+
+    def piece_rows(t):
+        return pl.ds(t * small, small)
+
+    def tile_loads(t):
+        return (
+            pltpu.make_async_copy(hidden_hbm.at[piece_rows(t)], hidden_v, tile_sem.at[0]),
+            pltpu.make_async_copy(mlp_low_hbm.at[piece_rows(t)], mlp_low_v, tile_sem.at[1]),
+            pltpu.make_async_copy(mlp_recv_out.at[piece_rows(t)], mlp_recv_v, tile_sem.at[2]),
+        )
+
+    def tile_store(t):
+        return pltpu.make_async_copy(
+            half_keep_v.at[pl.ds(t % 2 * small, small)],
+            outputs_out.at[piece_rows(t)],
+            tile_sem.at[3 + t % 2],
+        )
+
+    mlp_cross.wait()
+    for copy in tile_loads(0):
+        copy.start()
+    for t in range(pieces):
+        for copy in tile_loads(t):
+            copy.wait()
+        value = (
+            hidden_v[...]
+            + mlp_low_v[...].astype(WIDE)
+            + mlp_recv_v[...].astype(WIDE)
+            + vectors_ref[4:5, :]
+        )
+        if t > 1:
+            tile_store(t - 2).wait()
+        write_ordered(half_keep_v, pl.ds(t % 2 * small, small), blocks, shard, value)
+        tile_store(t).start()
+        if t + 1 < pieces:
+            for copy in tile_loads(t + 1):
+                copy.start()
+    for t in (pieces - 2, pieces - 1):
+        tile_store(t).wait()
+    ring.finish()
+    for t in range(tiles):
+        core_copy(t).wait_send()
+    for copy in stores:
+        copy.wait()
+
+
+def run_attend_back(
+    dp_size,
+    sol_size,
+    shard,
+    vectors,
+    weights,
+    normed_two,
+    grad_up,
+    branch,
+    query_rows,
+    key_rows,
+    value_rows,
+    probs,
+    mlp_low,
+    hidden,
+):
+    rows, width = hidden.shape
+    ff = grad_up.shape[1]
+    head_cols = query_rows.shape[1]
+    count = dp_size // 2 * sol_size
+    tiles = rows // CHUNK
+    dma = pltpu.SemaphoreType.DMA
+
+    def shape(*dims, dtype=LOW):
+        return jax.ShapeDtypeStruct(dims, dtype)
+
+    def low(*dims):
+        return pltpu.VMEM(dims, LOW)
+
+    outs = [
+        shape(2 * rows, head_cols),
+        shape(4 * rows, 2 * head_cols),
+        shape(rows, width),
+        shape(rows // 2, width),
+        shape(shard, 2 * ff, dtype=WIDE),
+        shape(rows, width),
+        shape(rows, width),
+    ]
+    return pl.pallas_call(
+        functools.partial(attend_back_kernel, dp_size, sol_size),
+        out_shape=outs,
+        in_specs=[vmem_spec()] + [any_spec()] * 10,
+        out_specs=[any_spec()] * len(outs),
+        scratch_shapes=[
+            low(2 * rows, width),
+            low(2 * rows, ff),
+            low(2 * rows, width),
+            low(width, width),
+            low(2 * rows, head_cols),
+            low(4 * rows, head_cols),
+            low(4 * rows, head_cols),
+            low(2 * rows, head_cols),
+            low(2, rows, 2 * rows),
+            low(2 * rows, head_cols),
+            low(4 * rows, 2 * head_cols),
+            low(rows, width),
+            low(rows, width),
+            low(CHUNK, width),
+            low(CHUNK // 2, width),
+            low(CHUNK // 2, width),
+            pltpu.VMEM((CHUNK // 2, width), WIDE),
+        ]
+        + ring_sum_scratch(count // 2, shard, ff, 1)
+        + [
+            dma((7,)),
+            dma((2,)),
+            dma((5,)),
+            dma((4,)),
+            dma((2, tiles)),
+            dma((2, tiles)),
+            dma((2,)),
+            dma((2,)),
+        ],
+        compiler_params=pltpu.CompilerParams(
+            collective_id=2, has_side_effects=True, vmem_limit_bytes=60 * 2**20
+        ),
+    )(
+        vectors,
+        weights,
+        normed_two,
+        grad_up,
+        branch,
+        query_rows,
+        key_rows,
+        value_rows,
+        probs,
+        mlp_low,
+        hidden,
+    )
+
+
+def last_kernel(
+    dp_size,
+    sol_size,
+    x_ref,
+    vectors_ref,
+    normed_hbm,
+    branch_hbm,
+    query_grad_hbm,
+    kv_grad_hbm,
+    mixed_hbm,
+    own_low_hbm,
+    prefix_half_hbm,
+    grad_hidden_hbm,
+    query_out,
+    key_out,
+    value_out,
+    out_out,
+    input_grad_out,
+    sums_ref,
+    normed_v,
+    branch_v,
+    query_grad_v,
+    kv_grad_v,
+    mixed_v,
+    own_low_v,
+    own_recv_v,
+    half_v,
+    half_recv_v,
+    prefix_v,
+    grad_hidden_v,
+    out_v,
+    ring_send_v,
+    ring_recv_v,
+    stage_v,
+    ring_send,
+    ring_recv,
+    ring_end,
+    load_sem,
+    tile_sem,
+    cross_send,
+    cross_recv,
+    chain_send,
+    chain_recv,
+):
+    here = Place(dp_size, sol_size)
+    rows, width = x_ref.shape
+    shard = stage_v.shape[1]
+    head_cols = query_grad_v.shape[1]
+    tiles = rows // CHUNK
+    blocks = here.blocks()
+    loads = [
+        pltpu.make_async_copy(src, dst, load_sem.at[i])
+        for i, (src, dst) in enumerate(
+            (
+                (query_grad_hbm, query_grad_v),
+                (kv_grad_hbm, kv_grad_v),
+                (mixed_hbm, mixed_v),
+                (prefix_half_hbm, half_v),
+                (normed_hbm, normed_v),
+                (branch_hbm, branch_v),
+                (own_low_hbm, own_low_v),
+            )
+        )
+    ]
+    for copy in loads:
+        copy.start()
+    here.greet()
+    own_cross = remote(own_low_hbm, own_recv_v, cross_send.at[0], cross_recv.at[0], here.across)
+    own_cross.start()
+
+    def chunk(j, which):
+        at = pl.ds(pl.multiple_of((2 * j + which) * shard, shard), shard)
+        return jnp.concatenate(
+            [
+                dot_left_t(normed_v[: 2 * rows, at], query_grad_v[...]),
+                dot_left_t(normed_v[:, at], kv_grad_v[...]),
+                dot_left_t(branch_v[:, at], mixed_v[...]),
+            ],
+            axis=1,
+        )
+
+    ring = RingSum(
+        here,
+        chunk,
+        ring_send_v,
+        ring_recv_v,
+        stage_v,
+        (ring_send, ring_recv, ring_end),
+        tuple(
+            (ref, i * head_cols, head_cols)
+            for i, ref in enumerate((query_out, key_out, value_out, out_out))
+        ),
+    )
+
+    part = CHUNK // 2
+
+    def chain_copy(i):
+        at = pl.ds(i * part, part)
+        return remote(
+            half_v.at[at], half_recv_v.at[at], chain_send.at[i], chain_recv.at[i], here.along(-1)
+        )
+
+    def chain(stage, i):
+        at = pl.ds(i * part, part)
+
+        @pl.when(here.z == stage)
+        def _():
+            if stage < sol_size - 1:
+                chain_copy(i).wait_recv()
+                if stage > 0:
+                    half_v[at, :] = (
+                        half_v[at, :].astype(WIDE) + half_recv_v[at, :].astype(WIDE)
+                    ).astype(LOW)
+            if stage > 0:
+                chain_copy(i).start()
+
+    loads[3].wait()
+    for i in range(2):
+        chain(sol_size - 1, i)
+    for i in (0, 1, 2, 4, 5):
+        loads[i].wait()
+    ring.to(2)
+    for step in range(sol_size):
+        if step < sol_size - 1:
+            chain(sol_size - 2 - step, 0)
+        if step > 0:
+            chain(sol_size - 1 - step, 1)
+        ring.to(3 + step)
+
+    mine = pl.ds(pl.multiple_of(here.y * CHUNK, CHUNK), CHUNK)
+    half_cross = remote(
+        half_recv_v, prefix_v.at[mine], cross_send.at[1], cross_recv.at[1], here.across
+    )
+
+    @pl.when(here.z == 0)
+    def _():
+        half_cross.start()
+        prefix_v[mine, :] = half_recv_v[...]
+
+    @pl.when(here.z > 0)
+    def _():
+        prefix_v[...] = jnp.zeros_like(prefix_v)
+
+    ring.to(7)
+    loads[6].wait()
+    own_cross.wait()
+
+    @pl.when(here.z == 0)
+    def _():
+        half_cross.wait()
+
+    gain = vectors_ref[0:1, :]
+    sums_ref[...] = jnp.zeros_like(sums_ref)
+
+    def tile_load(t):
+        return pltpu.make_async_copy(
+            grad_hidden_hbm.at[tile_rows(t)], grad_hidden_v, tile_sem.at[0]
+        )
+
+    def tile_store(t):
+        return pltpu.make_async_copy(out_v, input_grad_out.at[tile_rows(t)], tile_sem.at[1])
+
+    tile_load(0).start()
+    for t in range(tiles):
+        tile_load(t).wait()
+        if t > 0:
+            tile_store(t - 1).wait()
+        for piece in range(2):
+            at = pl.ds(t * CHUNK + piece * part, part)
+            inner = pl.ds(piece * part, part)
+            grad = (
+                own_low_v[at, :].astype(WIDE)
+                + own_recv_v[at, :].astype(WIDE)
+                + read_ordered(prefix_v, at, blocks, shard)
+            )
+            back, gain_terms, shift_terms = norm_back(
+                read_ordered(x_ref, at, blocks, shard), gain, grad
+            )
+            sums_ref[0:1, :] += gain_terms
+            sums_ref[1:2, :] += shift_terms
+            write_ordered(out_v, inner, blocks, shard, back + grad_hidden_v[inner, :])
+        tile_store(t).start()
+        if t + 1 < tiles:
+            tile_load(t + 1).start()
+        ring.to(8 + t)
+    tile_store(tiles - 1).wait()
+    ring.finish()
+    for i in range(2):
+
+        @pl.when(here.z > 0)
+        def _():
+            chain_copy(i).wait_send()
+
+
+def run_last(
+    dp_size,
+    sol_size,
+    shard,
+    x,
+    vectors,
+    normed,
+    branch,
+    query_grad,
+    kv_grad,
+    mixed,
+    own_low,
+    prefix_half,
+    grad_hidden,
+):
+    rows, width = x.shape
+    head_cols = query_grad.shape[1]
+    count = dp_size // 2 * sol_size
+    dma = pltpu.SemaphoreType.DMA
+
+    def shape(*dims, dtype=LOW):
+        return jax.ShapeDtypeStruct(dims, dtype)
+
+    def low(*dims):
+        return pltpu.VMEM(dims, LOW)
+
+    outs = [shape(shard, 2 * head_cols, dtype=WIDE)] * 4 + [
+        shape(rows, width),
+        shape(8, width, dtype=WIDE),
+    ]
+    return pl.pallas_call(
+        functools.partial(last_kernel, dp_size, sol_size),
+        out_shape=outs,
+        in_specs=[vmem_spec()] * 2 + [any_spec()] * 8,
+        out_specs=[any_spec()] * 5 + [vmem_spec()],
+        scratch_shapes=[
+            low(4 * rows, width),
+            low(2 * rows, width),
+            low(2 * rows, head_cols),
+            low(4 * rows, 2 * head_cols),
+            low(2 * rows, head_cols),
+            low(rows, width),
+            low(rows, width),
+            low(CHUNK, width),
+            low(CHUNK, width),
+            low(rows, width),
+            pltpu.VMEM((CHUNK, width), WIDE),
+            low(CHUNK, width),
+        ]
+        + ring_sum_scratch(count // 2, shard, 4 * head_cols, 4)
+        + [
+            dma((7,)),
+            dma((2,)),
+            dma((2,)),
+            dma((2,)),
+            dma((2,)),
+            dma((2,)),
+        ],
+        compiler_params=pltpu.CompilerParams(
+            collective_id=3, has_side_effects=True, vmem_limit_bytes=60 * 2**20
+        ),
+    )(
+        x,
+        vectors,
+        normed,
+        branch,
+        query_grad,
+        kv_grad,
+        mixed,
+        own_low,
+        prefix_half,
+        grad_hidden,
+    )
+
+
+def ring_program(
     inputs,
     cotangent,
     attn_gain,
@@ -468,6 +2173,151 @@
         early[3 * width :],
         jnp.concatenate(down_low + down_high, axis=1),
         early[2 * width : 3 * width],
+    )
+
+
+def per_device(*arrays):
+    inputs, query_weight, up_weight = arrays[0], arrays[4], arrays[10]
+    fits = (
+        query_weight.shape[0] % 128 == 0
+        and inputs.shape[0] % (2 * CHUNK) == 0
+        and up_weight.shape[1] // 2 % inputs.shape[1] == 0
+        and query_weight.shape[1] * 2 == inputs.shape[1]
+    )
+    return kernel_program(*arrays) if fits else ring_program(*arrays)
+
+
+def kernel_program(
+    inputs,
+    cotangent,
+    attn_gain,
+    attn_shift,
+    query_weight,
+    key_weight,
+    value_weight,
+    out_weight,
+    mlp_gain,
+    mlp_shift,
+    up_weight,
+    up_bias,
+    down_weight,
+    down_bias,
+    live_rows,
+):
+    width = inputs.shape[1]
+    shard_rows = query_weight.shape[0]
+    ff_cols = up_weight.shape[1] // 2
+    dp_size, sol_size = lax.axis_size("dp"), lax.axis_size("sol")
+    count, _, _, cores = ring_pairs(dp_size, sol_size)
+    here = Place(dp_size, sol_size)
+    core = here.core
+    first_core = core == 0
+    order = jnp.stack(here.blocks()).astype(jnp.int32)
+    back_order = jnp.argsort(order).astype(jnp.int32)
+    vectors = jnp.stack([attn_gain, attn_shift, mlp_gain, mlp_shift, down_bias])
+    vectors = jnp.take(vectors.reshape(5, 2 * count, shard_rows), order, axis=1).reshape(5, width)
+    up_bias_c = jnp.where(first_core, up_bias[:ff_cols], up_bias[ff_cols:])[None]
+    (
+        weights,
+        normed_all,
+        cot_pair,
+        query_rows,
+        key_rows,
+        value_rows,
+        probs,
+        mixed_low,
+        hidden,
+        normed_two,
+        slope,
+        active,
+    ) = run_forward(
+        dp_size,
+        sol_size,
+        inputs,
+        vectors,
+        up_bias_c,
+        live_rows,
+        cotangent,
+        (query_weight, key_weight, value_weight, out_weight, up_weight, down_weight),
+    )
+    grad_up, grad_branch, grad_hidden, mlp_low, down_grad, early_sums = run_down(
+        dp_size, sol_size, shard_rows, vectors, weights, cot_pair, active, slope, hidden
+    )
+    query_grad, kv_grad, own_low, prefix_half, up_grad, outputs, _ = run_attend_back(
+        dp_size,
+        sol_size,
+        shard_rows,
+        vectors,
+        weights,
+        normed_two,
+        grad_up,
+        grad_branch,
+        query_rows,
+        key_rows,
+        value_rows,
+        probs,
+        mlp_low,
+        hidden,
+    )
+    query_grads, key_grads, value_grads, out_grads, input_grad, late_sums = run_last(
+        dp_size,
+        sol_size,
+        shard_rows,
+        inputs,
+        vectors,
+        normed_all,
+        grad_branch,
+        query_grad,
+        kv_grad,
+        mixed_low,
+        own_low,
+        prefix_half,
+        grad_hidden,
+    )
+
+    def to_core(value):
+        return lax.ppermute(value, ROWS_AXES, cores)
+
+    def reorder_rows(table, by):
+        return jnp.take(
+            table.reshape(table.shape[0], 2 * count, shard_rows), by, axis=1
+        ).reshape(table.shape)
+
+    small = reorder_rows(jnp.concatenate([early_sums[:3], late_sums[:2]]), back_order)
+    up_bias_grad = early_sums[3]
+    up_bias_both = jnp.concatenate(
+        [jnp.where(first_core, up_bias_grad, 0.0), jnp.where(first_core, 0.0, up_bias_grad)]
+    )
+
+    def sum_rows_axes(vector):
+        vector = vector + to_core(vector)
+        step = 1
+        while step < sol_size:
+            vector = vector + lax.ppermute(vector, "sol", [(i, i ^ step) for i in range(sol_size)])
+            step *= 2
+        step = 2
+        while step < dp_size:
+            vector = vector + lax.ppermute(vector, "dp", [(i, i ^ step) for i in range(dp_size)])
+            step *= 2
+        return vector
+
+    total = sum_rows_axes(jnp.concatenate([small.reshape(-1), up_bias_both]))
+    parts = total[: 5 * width].reshape(5, width)
+    return (
+        outputs,
+        input_grad,
+        parts[3],
+        parts[4],
+        query_grads,
+        key_grads,
+        value_grads,
+        out_grads,
+        parts[0],
+        parts[1],
+        up_grad,
+        total[5 * width :],
+        down_grad,
+        parts[2],
     )
 
 

time: 1200 us -> 653 us (0.54)
  Pallas kernels: 50.7 us -> 612 us
  waiting for transfers between devices: 438 us -> 13.9 us
  matrix products: 249 us -> 0 us
  starting transfers between devices: 220 us -> 1.39 us
  other arithmetic: 119 us -> 4.31 us
  local copies, waits for them, and re-layouts: 106 us -> 15.6 us
    pallas_call x5 -> x4, Pallas kernels: 50.7 us -> 612 us  [the longest x1 313 us: run_forward(): pl.pallas_call(functools.partial(forward_kernel, dp_size, sol_size), out_...]
    ppermute x95 -> x0, waiting for transfers between devices: 424 us -> none  [the longest x21 111 us: gather_ring(): moving_b = lax.ppermute(moving_b, ROWS_AXES, back)]
    dot_general x88 -> x0, matrix products: 249 us -> none  [the longest x64 79.5 us: dot_left_t(): lax.dot_general(left_side, right_side, (((0,), (0,)), ((), ())), preferre...]
    ppermute x95 -> x0, starting transfers between devices: 211 us -> none  [the longest x21 51.1 us: scatter_ring(): carried_a = lax.ppermute(value.astype(LOW), ROWS_AXES, ahead)]
    convert_element_type x21 -> x0, other arithmetic: 43.9 us -> none  [the longest x1 10.5 us: per_device(): grad_scores = (attn_probs * (grad_probs - row_delta)).astype(LOW)]
    unnamed x285 -> x24, local copies, waits for them, and re-layouts: 38.7 us -> 10.6 us
    reshape x10 -> x0, local copies, waits for them, and re-layouts: 19.9 us -> none  [heads_of(): return rows.reshape(2, -1, local_heads, HEAD_DIM)]
    reduce_sum x9 -> x0, other arithmetic: 19.5 us -> none  [the longest x3 5.99 us: norm_stats(): row_mean = jnp.mean(features, axis=-1, keepdims=True)]
  transfers between devices with their start and end apart: 124 -> 4, of which waited for: 58 -> 4; matrix products, arithmetic and copies ran while one was open for 28% -> 0% of each run, Pallas kernels for 4% -> 0%
where the time goes in v2:
time: 653 us; the launch traced here: 649 us
  Pallas kernels  612 us (94%)
  local copies, waits for them, and re-layouts  15.6 us (2%)
  waiting for transfers between devices  13.9 us (2%)
    pallas_call x1, Pallas kernels, run_forward(): pl.pallas_call(functools.partial(forward_kernel, dp_size, sol_size), out_...  313 us
    pallas_call x1, Pallas kernels, run_last(): pl.pallas_call(functools.partial(last_kernel, dp_size, sol_size), out_sha...  121 us
    pallas_call x1, Pallas kernels, run_attend_back(): pl.pallas_call(functools.partial(attend_back_kernel, dp_size, sol_size),...  89.8 us
    pallas_call x1, Pallas kernels, run_down(): pl.pallas_call(functools.partial(down_kernel, dp_size, sol_size), out_sha...  89.1 us
  transfers between devices with their start and end apart: 4, of which 4 were waited for; matrix products, arithmetic and copies ran while one was open for 0% of the time, Pallas kernels for 0%

profile of v2, /device:TPU:0, one launch (start us, length us, event | category | flops | bytes accessed | tf_op | source)
XLA Modules:
  0.0 648.8 jit_solution(1957606444591064663)
XLA Ops:
  1.3 0.1 stack.91
  1.4 1.2 sort.17
  2.7 0.8 stack.74
  3.5 0.6 gather_fusion
  4.1 0.7 select_bitcast_fusion.1.vectors_ref
  4.8 1.3 slice_select_fusion
  6.1 312.5 %shard_map.254 = (bf16[3,2048,2048]{2,1,0:T(8,128)(2,1)}, bf16[2048,2048]{1,0:T(8,128)(2,1)}, bf16[1024,2048]{1,0:T(8,128)(2,1)}, bf16[1024,512]{1,0:T(8,128)(2,...) custom-call(bf16[512,2048]{1,0:T(8,128)(2,1)} %x_ref.3, ...), custom_call_target="tpu_custom_call" | custom-call | tf_op jit(solution)/shard_map/pallas_call | solution.py:685
  318.7 89.1 %shard_map.255 = (bf16[1024,2048]{1,0:T(8,128)(2,1)}, bf16[1024,2048]{1,0:T(8,128)(2,1)}, f32[512,2048]{1,0:T(8,128)}, bf16[512,2048]{1,0:T(8,128)(2,1)}, f32[128,4096]{1,0:T(8,128)}, /*index=5*/f32[8,2048]{1,0:T(8,128)}) custom-call(f32[5,2048]{1,0:T(8,128)} %select_bitcast_fusion.1.vectors_ref, bf16[3,2048,2048]{2,1,0:T(8,128)(2,1)} %get-tuple-element.46.weights, ...), custom_call_target="tpu_custom_call" | custom-call | tf_op jit(solution)/shard_map/pallas_call | solution.py:1095
  407.7 0.8 slice.46
  408.6 0.9 broadcast_select_fusion.1
  409.4 89.8 %shard_map.256 = (bf16[1024,512]{1,0:T(8,128)(2,1)}, bf16[2048,1024]{1,0:T(8,128)(2,1)}, bf16[512,2048]{1,0:T(8,128)(2,1)}, bf16[256,2048]{1,0:T(8,128)(2,1)}, f...) custom-call(f32[5,2048]{1,0:T(8,128)} %select_bitcast_fusion.1.vectors_ref, ...), custom_call_target="tpu_custom_call" | custom-call | tf_op jit(solution)/shard_map/pallas_call | solution.py:1487
  499.2 0.0 copy-start.2
  499.2 120.6 %shard_map.257 = (f32[128,1024]{1,0:T(8,128)}, f32[128,1024]{1,0:T(8,128)}, f32[128,1024]{1,0:T(8,128)}, f32[128,1024]{1,0:T(8,128)}, bf16[512,2048]{1,0:T(8,128)(2,1)}, /*index=5*/f32[8,2048]{1,0:T(8,128)}) custom-call(bf16[512,2048]{1,0:T(8,128)(2,1)} %x_ref.3, f32[5,2048]{1,0:T(8,128)} %select_bitcast_fusion.1.vectors_ref, ...), custom_call_target="tpu_custom_call" | custom-call | tf_op jit(solution)/shard_map/pallas_call | solution.py:1764
  619.8 0.8 slice.47
  620.7 0.6 gather_fusion.1
  621.3 0.1 select_bitcast_fusion
  621.4 0.4 collective-permute-start
  621.8 0.9 collective-permute-done
  622.7 0.2 collective-permute-start.1
  623.0 4.0 collective-permute-done.1
  627.0 0.1 collective-permute-start.2
  627.1 5.4 collective-permute-done.2
  632.5 0.6 collective-permute-start.3
  633.1 3.6 collective-permute-done.3
  636.7 0.6 fusion.1
  637.3 0.6 slice.63
  638.0 0.0 copy-done.2
  638.0 0.0 copy-start.3
  638.0 1.3 copy.40
  639.3 1.0 copy-done.3
  640.3 0.0 copy-start.7
  640.3 0.0 copy-start.6
  640.3 0.0 copy-start.5
  640.3 1.3 copy.41
  641.6 0.0 copy-done.7
  641.7 0.0 copy-start.4
  641.7 0.0 copy-start.1
  641.7 0.8 copy.42
  642.5 0.0 copy-done.6
  642.5 0.8 copy.43
  643.3 0.0 copy-done.5
  643.3 0.8 copy.44
  644.1 0.0 copy-done.4
  644.1 0.8 copy.45
  644.9 0.0 copy-done.1
  644.9 1.3 copy.46
  646.2 1.0 copy-done
  647.2 1.3 copy.47
  (15 shorter events, 0.1 us)
Async XLA Ops:
  499.2 138.7 %copy-start.2 = (bf16[512,2048]{1,0:T(8,128)(2,1)S(1)}, bf16[512,2048]{1,0:T(8,128)(2,1)}, u32[]{:S(2)}) copy-start(bf16[512,2048]{1,0:T(8,128)(2,1)} %get-tuple-element.98) | copy-start | bytes 6291460
  621.4 1.3 collective-permute-start
  622.7 4.2 collective-permute-start.1
  627.0 5.5 collective-permute-start.2
  632.5 4.2 collective-permute-start.3
  638.0 2.3 copy-start.3
  640.3 1.4 copy-start.7
  640.3 2.2 copy-start.6
  640.3 3.0 copy-start.5
  641.7 2.4 copy-start.4
  641.7 3.2 copy-start.1
  644.9 2.3 copy-start

commit v3 on v2

--- a/solution.py
+++ b/solution.py
@@ -116,7 +116,7 @@
 
 class Place:
     def __init__(self, dp_size, sol_size):
-        self.sol_size = sol_size
+        self.dp_size, self.sol_size = dp_size, sol_size
         self.count = dp_size // 2 * sol_size
         dp, self.z = lax.axis_index("dp"), lax.axis_index("sol")
         self.y = lax.axis_index("tensor")
@@ -147,9 +147,25 @@
             result += [(x * 2) * self.sol_size + z, (x * 2 + 1) * self.sol_size + z]
         return result
 
-    def greet(self):
+    def partners(self):
+        result = [self.sibling]
+        step = 1
+        while step < self.sol_size:
+            result.append((self.dp, self._flip(self.z, step), self.y))
+            step *= 2
+        step = 2
+        while step < self.dp_size:
+            result.append((self._flip(self.dp, step), self.z, self.y))
+            step *= 2
+        return result
+
+    @staticmethod
+    def _flip(place, step):
+        return jnp.where(place // step % 2 == 0, place + step, place - step)
+
+    def greet(self, others=()):
         barrier = pltpu.get_barrier_semaphore()
-        peers = (self.next, self.prev, self.sibling, self.across)
+        peers = (self.next, self.prev, self.sibling, self.across) + tuple(others)
         for peer in peers:
             pl.semaphore_signal(barrier, inc=1, device_id=peer, device_id_type=MESH)
         pl.semaphore_wait(barrier, len(peers))
@@ -329,7 +345,8 @@
             done[0] += 1
 
     y_rows = rows // 2
-    part = y_rows // 2
+    parts = 4
+    part = y_rows // parts
 
     def prefix_rows(which_half, i):
         return pl.ds(pl.multiple_of(which_half * y_rows + i * part, part), part)
@@ -367,18 +384,18 @@
                 prefix_cross(i, False).start()
 
     def prefix_finish():
-        for i in range(2):
+        for i in range(parts):
             prefix_cross(i, False).wait_recv()
 
         @pl.when(here.z == 0)
         def _():
-            for i in range(2):
+            for i in range(parts):
                 at = prefix_rows(here.y, i)
                 prefix_v[at, :] = x_ref[at, :]
 
     cot_load = pltpu.make_async_copy(cot_hbm, active_v.at[pl.ds(0, rows)], cot_sem.at[1])
     start_swap(0)
-    for i in range(2):
+    for i in range(parts):
         prefix_stage(0, i)
     start_swap(1)
     start_swap(2)
@@ -419,12 +436,11 @@
     norm_into(x_ref, 0)
     normed_pair.start()
     pump_to(1)
-    for stage in range(1, sol_size + 1):
-        if stage < sol_size:
-            prefix_stage(stage, 0)
-        if stage > 1:
-            prefix_stage(stage - 1, 1)
-        pump_to(1 + stage)
+    for step in range(1, sol_size + parts - 1):
+        for i in range(parts):
+            if 1 <= step - i < sol_size:
+                prefix_stage(step - i, i)
+        pump_to(1 + step)
     pump_to(2 * far)
 
     cot_pair = remote(
@@ -474,7 +490,6 @@
     pump_to(2 * far + 2)
     prefix_pair.wait_recv()
     project(2 * tiles, 4 * tiles, False)
-    pump_to(2 * far + 3)
 
     stores = []
 
@@ -539,7 +554,7 @@
     units = 2 * local_heads
     for quarter in range(4):
         pl.loop(quarter * units // 4, (quarter + 1) * units // 4)(attend)
-        pump_to(2 * far + 4 + quarter)
+        pump_to(2 * far + (2, 3, 4, 4)[quarter])
     for unit in (units - 2, units - 1):
         probs_copy(unit).wait()
     store(mixed_v, mixed_out)
@@ -590,6 +605,8 @@
     load_second.start()
     for t in range(tiles):
         at = pl.ds(t * CHUNK, CHUNK)
+        if t > 0:
+            pump_to(4 * far + 2)
         cross_copy(t).wait_recv()
         hidden = (
             ordered(x_ref, at)
@@ -606,7 +623,6 @@
     load_second.wait()
     for t in range(tiles):
         two_copy(t).wait_recv()
-    pump_to(4 * far + 1)
     store(normed_two_v, normed_two_out)
 
     bend = math.sqrt(2.0 / math.pi)
@@ -624,7 +640,7 @@
             + 0.5 * upward * (1.0 - curve * curve) * (bend + (3.0 * 0.044715 * bend) * square)
         ).astype(LOW)
 
-    for i in range(2):
+    for i in range(parts):
 
         @pl.when(here.z < sol_size - 1)
         def _():
@@ -635,7 +651,7 @@
     feeds = 2 * tiles * spans
     for quarter in range(4):
         pl.loop(quarter * feeds // 4, (quarter + 1) * feeds // 4)(feed)
-        pump_to(4 * far + 2 + quarter)
+        pump_to(4 * far + 3 + quarter)
     store(active_v, active_out)
     store(slope_v, slope_out)
 
@@ -714,8 +730,8 @@
             dma((6,)),
             dma((6,)),
             dma((6,)),
-            dma((2, 2)),
-            dma((2, 2)),
+            dma((2, 4)),
+            dma((2, 4)),
             dma((3,)),
             dma((3,)),
             dma((3, rows // CHUNK)),
@@ -1542,6 +1558,7 @@
     sol_size,
     x_ref,
     vectors_ref,
+    early_ref,
     normed_hbm,
     branch_hbm,
     query_grad_hbm,
@@ -1568,6 +1585,8 @@
     prefix_v,
     grad_hidden_v,
     out_v,
+    table_v,
+    table_recv_v,
     ring_send_v,
     ring_recv_v,
     stage_v,
@@ -1580,6 +1599,8 @@
     cross_recv,
     chain_send,
     chain_recv,
+    table_send,
+    table_recv,
 ):
     here = Place(dp_size, sol_size)
     rows, width = x_ref.shape
@@ -1603,7 +1624,8 @@
     ]
     for copy in loads:
         copy.start()
-    here.greet()
+    partners = here.partners()
+    here.greet(partners[1:])
     own_cross = remote(own_low_hbm, own_recv_v, cross_send.at[0], cross_recv.at[0], here.across)
     own_cross.start()
 
@@ -1631,7 +1653,8 @@
         ),
     )
 
-    part = CHUNK // 2
+    parts = chain_send.shape[0]
+    part = CHUNK // parts
 
     def chain_copy(i):
         at = pl.ds(i * part, part)
@@ -1639,6 +1662,18 @@
             half_v.at[at], half_recv_v.at[at], chain_send.at[i], chain_recv.at[i], here.along(-1)
         )
 
+    def mine(i):
+        return pl.ds(pl.multiple_of(here.y * CHUNK + i * part, part), part)
+
+    def half_cross(i):
+        return remote(
+            half_recv_v.at[pl.ds(i * part, part)],
+            prefix_v.at[mine(i)],
+            cross_send.at[1 + i],
+            cross_recv.at[1 + i],
+            here.across,
+        )
+
     def chain(stage, i):
         at = pl.ds(i * part, part)
 
@@ -1646,50 +1681,42 @@
         def _():
             if stage < sol_size - 1:
                 chain_copy(i).wait_recv()
-                if stage > 0:
-                    half_v[at, :] = (
-                        half_v[at, :].astype(WIDE) + half_recv_v[at, :].astype(WIDE)
-                    ).astype(LOW)
+            if 0 < stage < sol_size - 1:
+                half_v[at, :] = (
+                    half_v[at, :].astype(WIDE) + half_recv_v[at, :].astype(WIDE)
+                ).astype(LOW)
             if stage > 0:
                 chain_copy(i).start()
+            else:
+                half_cross(i).start()
+                prefix_v[mine(i), :] = half_recv_v[at, :]
 
     loads[3].wait()
-    for i in range(2):
+    for i in range(parts):
         chain(sol_size - 1, i)
+
+    @pl.when(here.z > 0)
+    def _():
+        prefix_v[...] = jnp.zeros_like(prefix_v)
+
     for i in (0, 1, 2, 4, 5):
         loads[i].wait()
     ring.to(2)
-    for step in range(sol_size):
-        if step < sol_size - 1:
-            chain(sol_size - 2 - step, 0)
-        if step > 0:
-            chain(sol_size - 1 - step, 1)
-        ring.to(3 + step)
-
-    mine = pl.ds(pl.multiple_of(here.y * CHUNK, CHUNK), CHUNK)
-    half_cross = remote(
-        half_recv_v, prefix_v.at[mine], cross_send.at[1], cross_recv.at[1], here.across
-    )
+    for step in range(1, sol_size + parts - 1):
+        for i in range(parts):
+            if 1 <= step - i < sol_size:
+                chain(sol_size - 1 - (step - i), i)
+        ring.to(2 + step)
+
+    loads[6].wait()
+    own_cross.wait()
 
     @pl.when(here.z == 0)
     def _():
-        half_cross.start()
-        prefix_v[mine, :] = half_recv_v[...]
-
-    @pl.when(here.z > 0)
-    def _():
-        prefix_v[...] = jnp.zeros_like(prefix_v)
-
-    ring.to(7)
-    loads[6].wait()
-    own_cross.wait()
-
-    @pl.when(here.z == 0)
-    def _():
-        half_cross.wait()
+        for i in range(parts):
+            half_cross(i).wait()
 
     gain = vectors_ref[0:1, :]
-    sums_ref[...] = jnp.zeros_like(sums_ref)
 
     def tile_load(t):
         return pltpu.make_async_copy(
@@ -1700,13 +1727,15 @@
         return pltpu.make_async_copy(out_v, input_grad_out.at[tile_rows(t)], tile_sem.at[1])
 
     tile_load(0).start()
+    totals = [jnp.zeros((1, width), WIDE)] * 2
+    small = CHUNK // 2
     for t in range(tiles):
         tile_load(t).wait()
         if t > 0:
             tile_store(t - 1).wait()
         for piece in range(2):
-            at = pl.ds(t * CHUNK + piece * part, part)
-            inner = pl.ds(piece * part, part)
+            at = pl.ds(t * CHUNK + piece * small, small)
+            inner = pl.ds(piece * small, small)
             grad = (
                 own_low_v[at, :].astype(WIDE)
                 + own_recv_v[at, :].astype(WIDE)
@@ -1715,16 +1744,41 @@
             back, gain_terms, shift_terms = norm_back(
                 read_ordered(x_ref, at, blocks, shard), gain, grad
             )
-            sums_ref[0:1, :] += gain_terms
-            sums_ref[1:2, :] += shift_terms
+            totals = [totals[0] + gain_terms, totals[1] + shift_terms]
             write_ordered(out_v, inner, blocks, shard, back + grad_hidden_v[inner, :])
         tile_store(t).start()
         if t + 1 < tiles:
             tile_load(t + 1).start()
-        ring.to(8 + t)
+
+    for row in range(2):
+        write_ordered(table_v.at[0], pl.ds(row, 1), blocks, shard, totals[row])
+    for row in range(3):
+        write_ordered(
+            table_v.at[0], pl.ds(2 + row, 1), blocks, shard, early_ref[row : row + 1, :]
+        )
+    bias = early_ref[3:4, :]
+    table_v[0, 5:6, :] = jnp.where(here.core == 0, bias, 0.0)
+    table_v[0, 6:7, :] = jnp.where(here.core == 0, 0.0, bias)
+    table_v[0, 7:8, :] = jnp.zeros((1, width), WIDE)
+
+    def table_copy(k):
+        return remote(
+            table_v.at[k], table_recv_v.at[k], table_send.at[k], table_recv.at[k], partners[k]
+        )
+
+    for k in range(len(partners)):
+        table_copy(k).start()
+        ring.to(9 + k)
+        table_copy(k).wait_recv()
+        if k + 1 < len(partners):
+            table_v[k + 1] = table_v[k] + table_recv_v[k]
+        else:
+            sums_ref[...] = table_v[k] + table_recv_v[k]
     tile_store(tiles - 1).wait()
     ring.finish()
-    for i in range(2):
+    for k in range(len(partners)):
+        table_copy(k).wait_send()
+    for i in range(parts):
 
         @pl.when(here.z > 0)
         def _():
@@ -1737,6 +1791,7 @@
     shard,
     x,
     vectors,
+    early,
     normed,
     branch,
     query_grad,
@@ -1749,6 +1804,7 @@
     rows, width = x.shape
     head_cols = query_grad.shape[1]
     count = dp_size // 2 * sol_size
+    bits = (dp_size * sol_size).bit_length() - 1
     dma = pltpu.SemaphoreType.DMA
 
     def shape(*dims, dtype=LOW):
@@ -1764,7 +1820,7 @@
     return pl.pallas_call(
         functools.partial(last_kernel, dp_size, sol_size),
         out_shape=outs,
-        in_specs=[vmem_spec()] * 2 + [any_spec()] * 8,
+        in_specs=[vmem_spec()] * 3 + [any_spec()] * 8,
         out_specs=[any_spec()] * 5 + [vmem_spec()],
         scratch_shapes=[
             low(4 * rows, width),
@@ -1779,15 +1835,19 @@
             low(rows, width),
             pltpu.VMEM((CHUNK, width), WIDE),
             low(CHUNK, width),
+            pltpu.VMEM((bits, 8, width), WIDE),
+            pltpu.VMEM((bits, 8, width), WIDE),
         ]
         + ring_sum_scratch(count // 2, shard, 4 * head_cols, 4)
         + [
             dma((7,)),
             dma((2,)),
-            dma((2,)),
-            dma((2,)),
-            dma((2,)),
-            dma((2,)),
+            dma((5,)),
+            dma((5,)),
+            dma((4,)),
+            dma((4,)),
+            dma((bits,)),
+            dma((bits,)),
         ],
         compiler_params=pltpu.CompilerParams(
             collective_id=3, has_side_effects=True, vmem_limit_bytes=60 * 2**20
@@ -1795,6 +1855,7 @@
     )(
         x,
         vectors,
+        early,
         normed,
         branch,
         query_grad,
@@ -2178,11 +2239,15 @@
 
 def per_device(*arrays):
     inputs, query_weight, up_weight = arrays[0], arrays[4], arrays[10]
+    width = inputs.shape[1]
     fits = (
         query_weight.shape[0] % 128 == 0
-        and inputs.shape[0] % (2 * CHUNK) == 0
-        and up_weight.shape[1] // 2 % inputs.shape[1] == 0
-        and query_weight.shape[1] * 2 == inputs.shape[1]
+        and inputs.shape[0] == 2 * CHUNK
+        and up_weight.shape[1] == 2 * width
+        and query_weight.shape[1] * 2 == width
+        and lax.axis_size("dp") % 2 == 0
+        and lax.axis_size("dp") * lax.axis_size("sol") == 16
+        and lax.axis_size("tensor") == 2
     )
     return kernel_program(*arrays) if fits else ring_program(*arrays)
 
@@ -2208,14 +2273,12 @@
     shard_rows = query_weight.shape[0]
     ff_cols = up_weight.shape[1] // 2
     dp_size, sol_size = lax.axis_size("dp"), lax.axis_size("sol")
-    count, _, _, cores = ring_pairs(dp_size, sol_size)
     here = Place(dp_size, sol_size)
     core = here.core
     first_core = core == 0
     order = jnp.stack(here.blocks()).astype(jnp.int32)
-    back_order = jnp.argsort(order).astype(jnp.int32)
     vectors = jnp.stack([attn_gain, attn_shift, mlp_gain, mlp_shift, down_bias])
-    vectors = jnp.take(vectors.reshape(5, 2 * count, shard_rows), order, axis=1).reshape(5, width)
+    vectors = jnp.take(vectors.reshape(5, here.count * 2, shard_rows), order, axis=1).reshape(5, width)
     up_bias_c = jnp.where(first_core, up_bias[:ff_cols], up_bias[ff_cols:])[None]
     (
         weights,
@@ -2259,12 +2322,13 @@
         mlp_low,
         hidden,
     )
-    query_grads, key_grads, value_grads, out_grads, input_grad, late_sums = run_last(
+    query_grads, key_grads, value_grads, out_grads, input_grad, sums = run_last(
         dp_size,
         sol_size,
         shard_rows,
         inputs,
         vectors,
+        early_sums,
         normed_all,
         grad_branch,
         query_grad,
@@ -2275,49 +2339,21 @@
         grad_hidden,
     )
 
-    def to_core(value):
-        return lax.ppermute(value, ROWS_AXES, cores)
-
-    def reorder_rows(table, by):
-        return jnp.take(
-            table.reshape(table.shape[0], 2 * count, shard_rows), by, axis=1
-        ).reshape(table.shape)
-
-    small = reorder_rows(jnp.concatenate([early_sums[:3], late_sums[:2]]), back_order)
-    up_bias_grad = early_sums[3]
-    up_bias_both = jnp.concatenate(
-        [jnp.where(first_core, up_bias_grad, 0.0), jnp.where(first_core, 0.0, up_bias_grad)]
-    )
-
-    def sum_rows_axes(vector):
-        vector = vector + to_core(vector)
-        step = 1
-        while step < sol_size:
-            vector = vector + lax.ppermute(vector, "sol", [(i, i ^ step) for i in range(sol_size)])
-            step *= 2
-        step = 2
-        while step < dp_size:
-            vector = vector + lax.ppermute(vector, "dp", [(i, i ^ step) for i in range(dp_size)])
-            step *= 2
-        return vector
-
-    total = sum_rows_axes(jnp.concatenate([small.reshape(-1), up_bias_both]))
-    parts = total[: 5 * width].reshape(5, width)
     return (
         outputs,
         input_grad,
-        parts[3],
-        parts[4],
+        sums[0],
+        sums[1],
         query_grads,
         key_grads,
         value_grads,
         out_grads,
-        parts[0],
-        parts[1],
+        sums[2],
+        sums[3],
         up_grad,
-        total[5 * width :],
+        sums[5:7].reshape(-1),
         down_grad,
-        parts[2],
+        sums[4],
     )
 
 

time: 653 us -> 613 us (0.939)
  Pallas kernels: 612 us -> 590 us
  waiting for transfers between devices: 13.9 us -> 0 us
    pallas_call x1, Pallas kernels: 313 us -> 274 us  [run_forward(): pl.pallas_call(functools.partial(forward_kernel, dp_size, sol_size), out_...]
    ppermute x4 -> x0, waiting for transfers between devices: 13.9 us -> none  [the longest x2 9.4 us: sum_rows_axes(): lax.ppermute(vector, 'sol', [(i, i ^ step) for i in range(sol_size)])]
    pallas_call x1, Pallas kernels: 121 us -> 131 us  [run_last(): pl.pallas_call(functools.partial(last_kernel, dp_size, sol_size), out_sha...]
    pallas_call x1, Pallas kernels: 89.1 us -> 95.7 us  [run_down(): pl.pallas_call(functools.partial(down_kernel, dp_size, sol_size), out_sha...]
  transfers between devices with their start and end apart: 4 -> 0, of which waited for: 4 -> 0; matrix products, arithmetic and copies ran while one was open for 0% -> 0% of each run, Pallas kernels for 0% -> 0%
where the time goes in v3:
time: 613 us; the launch traced here: 609 us
  Pallas kernels  590 us (96%)
  local copies, waits for them, and re-layouts  15.4 us (3%)
    pallas_call x1, Pallas kernels, run_forward(): pl.pallas_call(functools.partial(forward_kernel, dp_size, sol_size), out_...  274 us
    pallas_call x1, Pallas kernels, run_last(): pl.pallas_call(functools.partial(last_kernel, dp_size, sol_size), out_sha...  131 us
    pallas_call x1, Pallas kernels, run_down(): pl.pallas_call(functools.partial(down_kernel, dp_size, sol_size), out_sha...  95.7 us
    pallas_call x1, Pallas kernels, run_attend_back(): pl.pallas_call(functools.partial(attend_back_kernel, dp_size, sol_size),...  89.6 us

profile of v3, /device:TPU:0, one launch (start us, length us, event | category | flops | bytes accessed | tf_op | source)
XLA Modules:
  0.0 608.8 jit_solution(14958068675388399190)
XLA Ops:
  1.2 0.1 stack.119
  1.3 0.1 stack.142
  1.5 0.1 broadcast_bitcast_fusion
  1.5 1.3 slice_select_fusion
  2.9 0.8 stack.125
  3.7 0.6 gather_fusion
  4.3 0.6 bitcast_select_fusion.vectors_ref
  4.9 273.7 %shard_map.254 = (bf16[3,2048,2048]{2,1,0:T(8,128)(2,1)}, bf16[2048,2048]{1,0:T(8,128)(2,1)}, bf16[1024,2048]{1,0:T(8,128)(2,1)}, bf16[1024,512]{1,0:T(8,128)(2,...) custom-call(bf16[512,2048]{1,0:T(8,128)(2,1)} %x_ref.3, ...), custom_call_target="tpu_custom_call" | custom-call | tf_op jit(solution)/shard_map/pallas_call | solution.py:701
  278.6 95.7 %shard_map.255 = (bf16[1024,2048]{1,0:T(8,128)(2,1)}, bf16[1024,2048]{1,0:T(8,128)(2,1)}, f32[512,2048]{1,0:T(8,128)}, bf16[512,2048]{1,0:T(8,128)(2,1)}, f32[128,4096]{1,0:T(8,128)}, /*index=5*/f32[8,2048]{1,0:T(8,128)}) custom-call(f32[5,2048]{1,0:T(8,128)} %bitcast_select_fusion.vectors_ref, bf16[3,2048,2048]{2,1,0:T(8,128)(2,1)} %get-tuple-element.44.weights, ...), custom_call_target="tpu_custom_call" | custom-call | tf_op jit(solution)/shard_map/pallas_call | solution.py:1111
  374.3 89.6 %shard_map.256 = (bf16[1024,512]{1,0:T(8,128)(2,1)}, bf16[2048,1024]{1,0:T(8,128)(2,1)}, bf16[512,2048]{1,0:T(8,128)(2,1)}, bf16[256,2048]{1,0:T(8,128)(2,1)}, f...) custom-call(f32[5,2048]{1,0:T(8,128)} %bitcast_select_fusion.vectors_ref, ...), custom_call_target="tpu_custom_call" | custom-call | tf_op jit(solution)/shard_map/pallas_call | solution.py:1503
  463.9 0.0 copy-start.2
  463.9 131.0 %shard_map.257 = (f32[128,1024]{1,0:T(8,128)}, f32[128,1024]{1,0:T(8,128)}, f32[128,1024]{1,0:T(8,128)}, f32[128,1024]{1,0:T(8,128)}, bf16[512,2048]{1,0:T(8,128)(2,1)}, /*index=5*/f32[8,2048]{1,0:T(8,128)}) custom-call(bf16[512,2048]{1,0:T(8,128)(2,1)} %x_ref.3, f32[5,2048]{1,0:T(8,128)} %bitcast_select_fusion.vectors_ref, ...), custom_call_target="tpu_custom_call" | custom-call | tf_op jit(solution)/shard_map/pallas_call | solution.py:1820
  594.9 0.8 slice_bitcast_fusion
  595.8 1.7 fusion.1
  597.4 0.6 copy.29
  598.0 0.0 copy-done.2
  598.0 0.0 copy-start.3
  598.0 1.3 copy.38
  599.3 1.0 copy-done.3
  600.4 0.0 copy-start.7
  600.4 0.0 copy-start.6
  600.4 0.0 copy-start.5
  600.4 1.3 copy.39
  601.7 0.0 copy-done.7
  601.7 0.0 copy-start.4
  601.8 0.0 copy-start.1
  601.8 0.8 copy.40
  602.5 0.0 copy-done.6
  602.5 0.8 copy.41
  603.3 0.0 copy-done.5
  603.3 0.8 copy.42
  604.1 0.0 copy-done.4
  604.1 0.8 copy.43
  604.9 0.0 copy-done.1
  604.9 0.0 copy-start
  604.9 1.3 copy.44
  606.3 1.0 copy-done
  607.3 1.3 copy.45
  (3 shorter events, 0.0 us)
Async XLA Ops:
  463.9 134.1 %copy-start.2 = (bf16[512,2048]{1,0:T(8,128)(2,1)S(1)}, bf16[512,2048]{1,0:T(8,128)(2,1)}, u32[]{:S(2)}) copy-start(bf16[512,2048]{1,0:T(8,128)(2,1)} %get-tuple-element.93) | copy-start | bytes 6291460
  598.0 2.3 copy-start.3
  600.4 1.4 copy-start.7
  600.4 2.2 copy-start.6
  600.4 3.0 copy-start.5
  601.7 2.4 copy-start.4
  601.8 3.2 copy-start.1
  604.9 2.3 copy-start

commit v4 on v3

--- a/solution.py
+++ b/solution.py
@@ -136,6 +136,10 @@
     def _chip(self, position):
         x, z = self._coords(position)
         return (x * 2 + self.core, z, self.y)
+
+    def up_ahead(self, step=0):
+        x, z = self._coords((self.at + step + self.count) % self.count)
+        return (x % 2 == 0) == (z > 0)
 
     def along(self, step):
         return (self.dp, self.z + step, self.y)
@@ -748,8 +752,14 @@
 
 
 class RingSum:
-    def __init__(self, here, chunk, send_v, recv_v, stage_v, sems, target):
+    def __init__(self, here, chunk, send_v, recv_v, stage_v, sems, target, upward=False):
         self.here, self.chunk = here, chunk
+        self.prepared = False
+        self.upward = upward
+        if upward:
+            mine = here.up_ahead()
+            self.sends = (mine, jnp.logical_not(mine))
+            self.gets = (here.up_ahead(-1), jnp.logical_not(here.up_ahead(1)))
         self.send_v, self.recv_v, self.stage_v = send_v, recv_v, stage_v
         self.send_sem, self.recv_sem, self.end_sem = sems
         self.target = target
@@ -762,7 +772,7 @@
         return self.here.core if sub == 0 else 1 - self.here.core
 
     def _columns(self, t, way):
-        if t > 1:
+        if t > 1 or self.upward:
             return pl.ds(0, self.cols)
         return pl.ds(way * (self.cols // 2), self.cols // 2)
 
@@ -779,6 +789,12 @@
     def _event(self, t, sub):
         far, count = self.far, self.here.count
         half = self.cols // 2
+        if t == 1 and self.upward:
+            value = self.chunk(far, self._class(sub)).astype(LOW)
+            for way in range(2):
+                self.send_v[way, sub] = value
+                pl.when(self.sends[way])(self._copy(1, way, sub).start)
+            return
         if t == 1:
             value = self.chunk(far, self._class(sub))
             self.send_v[0, sub, :, :half] = value[:, :half].astype(LOW)
@@ -789,6 +805,15 @@
         for way in range(2):
             j = far + 1 - t if way == 0 else count - (far + 1 - t)
             value = self.chunk(j, self._class(sub))
+            if t == 2 and self.upward:
+                pl.when(self.sends[way])(self._copy(1, way, sub).wait_send)
+                pl.when(self.gets[way])(self._copy(1, way, sub).wait_recv)
+                came = self.recv_v[0, way, sub].astype(WIDE)
+                self.send_v[way, sub] = (
+                    value + jnp.where(self.gets[way], came, 0.0)
+                ).astype(LOW)
+                self._copy(t, way, sub).start()
+                continue
             self._copy(t - 1, way, sub).wait()
             if t == 2:
                 near = slice(0, half) if way == 0 else slice(half, 2 * half)
@@ -803,11 +828,15 @@
                 ).astype(LOW)
             self._copy(t, way, sub).start()
 
+    def prepare(self):
+        for sub in range(2):
+            self.stage_v[sub] = self.chunk(0, self._class(sub))
+        self.prepared = True
+
     def _last(self, sub):
-        value = self.chunk(0, self._class(sub))
         for way in range(2):
             self._copy(self.far, way, sub).wait()
-        value = value + self.recv_v[(self.far - 1) % 3, 0, sub].astype(WIDE)
+        value = self.stage_v[sub] + self.recv_v[(self.far - 1) % 3, 0, sub].astype(WIDE)
         self.stage_v[sub] = value + self.recv_v[(self.far - 1) % 3, 1, sub].astype(WIDE)
         for copy in self._results(sub):
             copy.start()
@@ -919,6 +948,19 @@
     ff = active_v.shape[1]
     tiles = rows // CHUNK
     halves = (pl.ds(0, width // 2), pl.ds(width // 2, width // 2))
+    def chunk(j, which):
+        at = pl.ds(pl.multiple_of((2 * j + which) * shard, shard), shard)
+        return dot_left_t(cot_v[:, at], active_v[...])
+
+    ring = RingSum(
+        here,
+        chunk,
+        ring_send_v,
+        ring_recv_v,
+        stage_v,
+        (ring_send, ring_recv, ring_end),
+        ((down_grad_out, 0, ff),),
+    )
     loads = [
         pltpu.make_async_copy(src, dst, load_sem.at[i])
         for i, (src, dst) in enumerate(
@@ -935,43 +977,23 @@
         copy.start()
     here.greet()
 
-    def chunk(j, which):
-        at = pl.ds(pl.multiple_of((2 * j + which) * shard, shard), shard)
-        return dot_left_t(cot_v[:, at], active_v[...])
-
-    ring = RingSum(
-        here,
-        chunk,
-        ring_send_v,
-        ring_recv_v,
-        stage_v,
-        (ring_send, ring_recv, ring_end),
-        ((down_grad_out, 0, ff),),
-    )
     loads[0].wait()
     loads[1].wait()
-    ring.to(2)
-    loads[2].wait()
-    loads[3].wait()
+    ring.to(1)
 
     sums_ref[...] = jnp.zeros_like(sums_ref)
     spans = 2
 
-    def back_feed(i):
-        at = pl.ds(pl.multiple_of(i // spans * CHUNK, CHUNK), CHUNK)
-        cols = pl.ds(pl.multiple_of(i % spans * (ff // spans), ff // spans), ff // spans)
-        grad = dot_plain(cot_v[at, :], down_v[:, cols]) * slope_v[at, cols].astype(WIDE)
-        low = grad.astype(LOW)
-        slope_v[at, cols] = low
-        sums_ref[3:4, cols] += jnp.sum(low.astype(WIDE), axis=0, keepdims=True)
-
-    pl.loop(0, tiles * spans)(back_feed)
-    ring.to(3)
-    pl.loop(tiles * spans, 2 * tiles * spans)(back_feed)
-    ring.to(4)
-    loads[4].wait()
-    stores = [pltpu.make_async_copy(slope_v, grad_up_out, store_sem.at[0])]
-    stores[0].start()
+    def back_feed(tile):
+        at = pl.ds(tile * CHUNK, CHUNK)
+
+        @pl.loop(0, spans)
+        def _(i):
+            cols = pl.ds(pl.multiple_of(i * (ff // spans), ff // spans), ff // spans)
+            grad = dot_plain(cot_v[at, :], down_v[:, cols]) * slope_v[at, cols].astype(WIDE)
+            low = grad.astype(LOW)
+            slope_v[at, cols] = low
+            sums_ref[3:4, cols] += jnp.sum(low.astype(WIDE), axis=0, keepdims=True)
 
     def core_copy(t):
         return remote(
@@ -1009,13 +1031,14 @@
             here.sibling,
         )
 
-    for t in range(tiles):
+    def sibling_terms(t):
         for cols in halves:
             core_send_v[tile_rows(t), cols] = dot_right_t(
                 slope_v[pl.ds(rows + t * CHUNK, CHUNK), :], up_v[cols, :]
             ).astype(LOW)
         core_copy(t).start()
-    for t in range(tiles):
+
+    def own_terms(t):
         at = tile_rows(t)
         core_copy(t).wait_recv()
         for cols in halves:
@@ -1023,17 +1046,16 @@
                 dot_right_t(slope_v[at, :], up_v[cols, :]) + core_recv_v[at, cols].astype(WIDE)
             ).astype(LOW)
         cross_copy(t).start()
-    ring.to(5)
-
-    for t in range(tiles):
+
+    def sibling_output(t):
         core_copy(t).wait_send()
         for cols in halves:
             core_send_v[tile_rows(t), cols] = dot_right_t(
                 active_v[pl.ds(rows + t * CHUNK, CHUNK), :], down_v[cols, :]
             ).astype(LOW)
         second_copy(t).start()
-    ring.to(6)
-    for t in range(tiles):
+
+    def own_output(t):
         at = tile_rows(t)
         second_copy(t).wait_recv()
         for cols in halves:
@@ -1041,9 +1063,6 @@
                 dot_right_t(active_v[at, :], down_v[cols, :])
                 + second_recv_v[at, cols].astype(WIDE)
             ).astype(LOW)
-    stores.append(pltpu.make_async_copy(second_recv_v, mlp_low_out, store_sem.at[1]))
-    stores[1].start()
-    ring.to(8)
 
     gain = vectors_ref[2:3, :]
 
@@ -1053,9 +1072,7 @@
     def hidden_store(t):
         return pltpu.make_async_copy(hidden_v, grad_hidden_out.at[tile_rows(t)], store_sem.at[2])
 
-    hidden_load(0).start()
-    for t in range(tiles):
-        at = tile_rows(t)
+    def norm_tile(t):
         hidden_load(t).wait()
         cross_copy(t).wait_recv()
         for part in range(2):
@@ -1072,15 +1089,47 @@
             core_recv_v[here_at, :] = back.astype(LOW)
         branch_copy(t).start()
         hidden_store(t).start()
-        if t == 0:
-            ring.to(9)
-        hidden_store(t).wait()
-        if t + 1 < tiles:
-            hidden_load(t + 1).start()
-    stores.append(
-        pltpu.make_async_copy(core_recv_v, branch_out.at[pl.ds(0, rows)], store_sem.at[3])
-    )
-    stores[2].start()
+
+    stores = []
+
+    def store(src, dst, i):
+        copy = pltpu.make_async_copy(src, dst, store_sem.at[i])
+        copy.start()
+        stores.append(copy)
+
+    loads[2].wait()
+    loads[3].wait()
+    ring.to(2)
+    hidden_load(0).start()
+    back_feed(0)
+    ring.to(3)
+    back_feed(tiles)
+    loads[4].wait()
+    sibling_terms(0)
+    ring.to(4)
+    own_terms(0)
+    back_feed(1)
+    ring.to(5)
+    back_feed(tiles + 1)
+    store(slope_v, grad_up_out, 0)
+    sibling_terms(1)
+    ring.to(6)
+    own_terms(1)
+    sibling_output(0)
+    ring.to(7)
+    own_output(0)
+    sibling_output(1)
+    ring.to(8)
+    norm_tile(0)
+    own_output(1)
+    store(second_recv_v, mlp_low_out, 1)
+    hidden_store(0).wait()
+    hidden_load(1).start()
+    ring.prepare()
+    ring.to(9)
+    norm_tile(1)
+    store(core_recv_v, branch_out.at[pl.ds(0, rows)], 3)
+    hidden_store(1).wait()
     ring.finish()
     for t in range(tiles):
         cross_copy(t).wait_send()
@@ -1090,7 +1139,9 @@
         copy.wait()
 
 
-def run_down(dp_size, sol_size, shard, vectors, weights, cot, active, slope, hidden):
+def run_down(
+    dp_size, sol_size, shard, vectors, weights, cot, active, slope, hidden
+):
     rows, width = hidden.shape
     ff = active.shape[1]
     count = dp_size // 2 * sol_size
@@ -1125,7 +1176,7 @@
         + ring_sum_scratch(count // 2, shard, ff, 1)
         + [
             dma((5,)),
-            dma((4,)),
+            dma((6,)),
             dma((4, tiles)),
             dma((4, tiles)),
         ],
@@ -1403,6 +1454,7 @@
             ).astype(LOW)
     store(core_recv_v, own_low_out)
     ring.to(8)
+    ring.prepare()
 
     half_copy.wait()
     write_ordered(
@@ -1651,6 +1703,7 @@
             (ref, i * head_cols, head_cols)
             for i, ref in enumerate((query_out, key_out, value_out, out_out))
         ),
+        upward=True,
     )
 
     parts = chain_send.shape[0]
@@ -1707,6 +1760,8 @@
             if 1 <= step - i < sol_size:
                 chain(sol_size - 1 - (step - i), i)
         ring.to(2 + step)
+        if step == 4:
+            ring.prepare()
 
     loads[6].wait()
     own_cross.wait()
@@ -1768,7 +1823,6 @@
 
     for k in range(len(partners)):
         table_copy(k).start()
-        ring.to(9 + k)
         table_copy(k).wait_recv()
         if k + 1 < len(partners):
             table_v[k + 1] = table_v[k] + table_recv_v[k]
@@ -1867,6 +1921,40 @@
     )
 
 
+def finish_kernel(*refs):
+    count = (len(refs) - 2) // 3
+    ins, outs, rooms = refs[:count], refs[count : 2 * count], refs[2 * count : 3 * count]
+    in_sem, out_sem = refs[3 * count :]
+    loads = [
+        pltpu.make_async_copy(src, room, in_sem.at[i])
+        for i, (src, room) in enumerate(zip(ins, rooms))
+    ]
+    stores = [
+        pltpu.make_async_copy(room, dst, out_sem.at[i])
+        for i, (room, dst) in enumerate(zip(rooms, outs))
+    ]
+    for copy in loads:
+        copy.start()
+    for load, store in zip(loads, stores):
+        load.wait()
+        store.start()
+    for copy in stores:
+        copy.wait()
+
+
+def run_finish(arrays):
+    dma = pltpu.SemaphoreType.DMA
+    return pl.pallas_call(
+        finish_kernel,
+        out_shape=[jax.ShapeDtypeStruct(a.shape, a.dtype) for a in arrays],
+        in_specs=[any_spec()] * len(arrays),
+        out_specs=[any_spec()] * len(arrays),
+        scratch_shapes=[pltpu.VMEM(a.shape, a.dtype) for a in arrays]
+        + [dma((len(arrays),)), dma((len(arrays),))],
+        compiler_params=pltpu.CompilerParams(vmem_limit_bytes=60 * 2**20),
+    )(*arrays)
+
+
 def ring_program(
     inputs,
     cotangent,
@@ -2339,6 +2427,27 @@
         grad_hidden,
     )
 
+    (
+        outputs,
+        input_grad,
+        query_grads,
+        key_grads,
+        value_grads,
+        out_grads,
+        up_grad,
+        down_grad,
+    ) = run_finish(
+        [
+            outputs,
+            input_grad,
+            query_grads,
+            key_grads,
+            value_grads,
+            out_grads,
+            up_grad,
+            down_grad,
+        ]
+    )
     return (
         outputs,
         input_grad,

time: 613 us -> 602 us (0.982)
  local copies, waits for them, and re-layouts: 15.4 us -> 2.93 us
    unnamed x26 -> x4, local copies, waits for them, and re-layouts: 12 us -> 0.62 us
    pallas_call x1, Pallas kernels: 131 us -> 122 us  [run_last(): pl.pallas_call(functools.partial(last_kernel, dp_size, sol_size), out_sha...]
    pallas_call x0 -> x1, Pallas kernels: none -> 7.79 us  [run_finish(): pl.pallas_call(finish_kernel, out_shape=[jax.ShapeDtypeStruct(a.shape, a....]
where the time goes in v4:
time: 602 us; the launch traced here: 594 us
  Pallas kernels  587 us (98%)
    pallas_call x1, Pallas kernels, run_forward(): pl.pallas_call(functools.partial(forward_kernel, dp_size, sol_size), out_...  273 us
    pallas_call x1, Pallas kernels, run_last(): pl.pallas_call(functools.partial(last_kernel, dp_size, sol_size), out_sha...  122 us
    pallas_call x1, Pallas kernels, run_down(): pl.pallas_call(functools.partial(down_kernel, dp_size, sol_size), out_sha...  96.2 us
    pallas_call x1, Pallas kernels, run_attend_back(): pl.pallas_call(functools.partial(attend_back_kernel, dp_size, sol_size),...  88.3 us

profile of v4, /device:TPU:0, one launch (start us, length us, event | category | flops | bytes accessed | tf_op | source)
XLA Modules:
  0.0 593.7 jit_solution(2816559014701914119)
XLA Ops:
  1.2 0.1 stack.119
  1.3 0.1 stack.142
  1.5 0.1 broadcast_bitcast_fusion
  1.5 1.3 slice_select_fusion
  2.9 0.8 stack.125
  3.7 0.6 gather_fusion
  4.3 0.6 bitcast_select_fusion.vectors_ref
  4.9 272.7 %shard_map.254 = (bf16[3,2048,2048]{2,1,0:T(8,128)(2,1)}, bf16[2048,2048]{1,0:T(8,128)(2,1)}, bf16[1024,2048]{1,0:T(8,128)(2,1)}, bf16[1024,512]{1,0:T(8,128)(2,...) custom-call(bf16[512,2048]{1,0:T(8,128)(2,1)} %x_ref.3, ...), custom_call_target="tpu_custom_call" | custom-call | tf_op jit(solution)/shard_map/pallas_call | solution.py:705
  277.6 96.2 %shard_map.255 = (bf16[1024,2048]{1,0:T(8,128)(2,1)}, bf16[1024,2048]{1,0:T(8,128)(2,1)}, f32[512,2048]{1,0:T(8,128)}, bf16[512,2048]{1,0:T(8,128)(2,1)}, f32[128,4096]{1,0:T(8,128)}, /*index=5*/f32[8,2048]{1,0:T(8,128)}) custom-call(f32[5,2048]{1,0:T(8,128)} %bitcast_select_fusion.vectors_ref, bf16[3,2048,2048]{2,1,0:T(8,128)(2,1)} %get-tuple-element.52.weights, ...), custom_call_target="tpu_custom_call" | custom-call | tf_op jit(solution)/shard_map/pallas_call | solution.py:1162
  373.7 88.3 %shard_map.256 = (bf16[1024,512]{1,0:T(8,128)(2,1)}, bf16[2048,1024]{1,0:T(8,128)(2,1)}, bf16[512,2048]{1,0:T(8,128)(2,1)}, bf16[256,2048]{1,0:T(8,128)(2,1)}, f...) custom-call(f32[5,2048]{1,0:T(8,128)} %bitcast_select_fusion.vectors_ref, ...), custom_call_target="tpu_custom_call" | custom-call | tf_op jit(solution)/shard_map/pallas_call | solution.py:1555
  462.1 122.2 %shard_map.257 = (f32[128,1024]{1,0:T(8,128)}, f32[128,1024]{1,0:T(8,128)}, f32[128,1024]{1,0:T(8,128)}, f32[128,1024]{1,0:T(8,128)}, bf16[512,2048]{1,0:T(8,128)(2,1)}, /*index=5*/f32[8,2048]{1,0:T(8,128)}) custom-call(bf16[512,2048]{1,0:T(8,128)(2,1)} %x_ref.3, f32[5,2048]{1,0:T(8,128)} %bitcast_select_fusion.vectors_ref, ...), custom_call_target="tpu_custom_call" | custom-call | tf_op jit(solution)/shard_map/pallas_call | solution.py:1874
  584.3 0.0 copy-start
  584.3 7.8 %shard_map.258 = (bf16[512,2048]{1,0:T(8,128)(2,1)}, bf16[512,2048]{1,0:T(8,128)(2,1)}, f32[128,1024]{1,0:T(8,128)}, f32[128,1024]{1,0:T(8,128)}, f32[128,1024]{...) custom-call(bf16[512,2048]{1,0:T(8,128)(2,1)} %get-tuple-element.65.refs_0_, ...), custom_call_target="tpu_custom_call" | custom-call | tf_op jit(solution)/shard_map/pallas_call | solution.py:1947
  592.1 0.0 copy-done
  592.2 0.6 fusion.1
  592.8 0.6 copy.29
  (4 shorter events, 0.0 us)
Async XLA Ops:
  584.3 7.8 %copy-start = (f32[8,2048]{1,0:T(8,128)S(1)}, f32[8,2048]{1,0:T(8,128)}, u32[]{:S(2)}) copy-start(f32[8,2048]{1,0:T(8,128)} %get-tuple-element.83) | copy-start | bytes 196612

commit v5 on v4

--- a/solution.py
+++ b/solution.py
@@ -197,7 +197,10 @@
     dp_size,
     sol_size,
     x_ref,
-    vectors_ref,
+    attn_gain_ref,
+    attn_shift_ref,
+    mlp_gain_ref,
+    mlp_shift_ref,
     up_bias_ref,
     live_ref,
     cot_hbm,
@@ -298,8 +301,9 @@
 
     def hops(matrix, k, sub):
         which = own_class if sub == 0 else other_class
-        ahead_cols = pl.ds(0, half if k == far else width)
-        back_cols = pl.ds(half if k == far else 0, half if k == far else width)
+        halved = k == far and matrix > 0
+        ahead_cols = pl.ds(0, half if halved else width)
+        back_cols = pl.ds(half if halved else 0, half if halved else width)
         return (
             remote(
                 weights.at[matrix, slot((count - k + 1) % count, which), ahead_cols],
@@ -327,14 +331,25 @@
         for copy in hops(matrix, 1, sub):
             copy.start()
 
+    def only_when(matrix, k, condition, action):
+        if matrix == 0 and k == far:
+            pl.when(condition)(action)
+        else:
+            action()
+
+    came_ahead = jnp.logical_not(here.up_ahead())
+    goes = (jnp.logical_not(here.up_ahead(1)), here.up_ahead(-1))
+
     def pump(matrix, k, sub):
         came = hops(matrix, k, sub)
         if k < far:
             further = hops(matrix, k + 1, sub)
         for i in range(2):
-            came[i].wait_recv()
+            only_when(
+                matrix, k, came_ahead if i == 0 else jnp.logical_not(came_ahead), came[i].wait_recv
+            )
             if k < far:
-                further[i].start()
+                only_when(matrix, k + 1, goes[i], further[i].start)
         if k == far - 1 and matrix < 2:
             start_ring(matrix + 1, sub)
 
@@ -399,8 +414,6 @@
 
     cot_load = pltpu.make_async_copy(cot_hbm, active_v.at[pl.ds(0, rows)], cot_sem.at[1])
     start_swap(0)
-    for i in range(parts):
-        prefix_stage(0, i)
     start_swap(1)
     start_swap(2)
     cot_load.start()
@@ -413,8 +426,10 @@
             [ref[at, pl.ds(pl.multiple_of(b * shard, shard), shard)] for b in blocks], axis=1
         ).astype(WIDE)
 
-    gain, shift = vectors_ref[0:1, :], vectors_ref[1:2, :]
-    gain_two, shift_two = vectors_ref[2:3, :], vectors_ref[3:4, :]
+    gain, shift, gain_two, shift_two = [
+        ordered(ref, pl.ds(0, 1))
+        for ref in (attn_gain_ref, attn_shift_ref, mlp_gain_ref, mlp_shift_ref)
+    ]
 
     def norm_into(ref, start):
         @pl.loop(0, rows // 128)
@@ -439,12 +454,14 @@
     )
     norm_into(x_ref, 0)
     normed_pair.start()
-    pump_to(1)
+    pump_to(2)
+    for i in range(parts):
+        prefix_stage(0, i)
     for step in range(1, sol_size + parts - 1):
         for i in range(parts):
             if 1 <= step - i < sol_size:
                 prefix_stage(step - i, i)
-        pump_to(1 + step)
+        pump_to(2 + step)
     pump_to(2 * far)
 
     cot_pair = remote(
@@ -635,7 +652,8 @@
     def feed(i):
         at = row_tile(i // spans)
         cols = pl.ds(pl.multiple_of((i % spans) * half, half), half)
-        upward = dot_plain(normed_two_v[at, :], w_v[:, cols]) + up_bias_ref[:, cols]
+        bias_cols = pl.ds(pl.multiple_of(core * ff + (i % spans) * half, half), half)
+        upward = dot_plain(normed_two_v[at, :], w_v[:, cols]) + up_bias_ref[:, bias_cols]
         square = upward * upward
         curve = jnp.tanh(bend * (upward + 0.044715 * (upward * square)))
         active_v[at, cols] = (0.5 * upward * (1.0 + curve)).astype(LOW)
@@ -666,8 +684,8 @@
     for i in range(len(shards)):
         swap_copies(i)[1].wait_send()
     for step in steps:
-        for copy in hops(*step):
-            copy.wait_send()
+        for i, copy in enumerate(hops(*step)):
+            only_when(step[0], step[1], goes[i], copy.wait_send)
     for t in range(tiles):
         core_copy(t).wait_send()
         cross_copy(t).wait_send()
@@ -676,7 +694,7 @@
         copy.wait()
 
 
-def run_forward(dp_size, sol_size, x, vectors, up_bias, live_rows, cot, matrices):
+def run_forward(dp_size, sol_size, x, vectors, live_rows, cot, matrices):
     rows, width = x.shape
     head_cols = matrices[0].shape[1] // 2
     ff = matrices[4].shape[1] // 2
@@ -706,6 +724,9 @@
         functools.partial(forward_kernel, dp_size, sol_size),
         out_shape=outs,
         in_specs=[
+            vmem_spec(),
+            vmem_spec(),
+            vmem_spec(),
             vmem_spec(),
             vmem_spec(),
             vmem_spec(),
@@ -748,7 +769,7 @@
         compiler_params=pltpu.CompilerParams(
             collective_id=0, has_side_effects=True, vmem_limit_bytes=60 * 2**20
         ),
-    )(x, vectors, up_bias, live_rows, cot, *matrices)
+    )(x, *vectors, live_rows, cot, *matrices)
 
 
 class RingSum:
@@ -908,7 +929,7 @@
 def down_kernel(
     dp_size,
     sol_size,
-    vectors_ref,
+    gain_ref,
     weights,
     cot_hbm,
     active_hbm,
@@ -1064,7 +1085,7 @@
                 + second_recv_v[at, cols].astype(WIDE)
             ).astype(LOW)
 
-    gain = vectors_ref[2:3, :]
+    gain = read_ordered(gain_ref, pl.ds(0, 1), here.blocks(), shard)
 
     def hidden_load(t):
         return pltpu.make_async_copy(hidden_hbm.at[tile_rows(t)], hidden_v, load_sem.at[0])
@@ -1140,7 +1161,7 @@
 
 
 def run_down(
-    dp_size, sol_size, shard, vectors, weights, cot, active, slope, hidden
+    dp_size, sol_size, shard, gain, weights, cot, active, slope, hidden
 ):
     rows, width = hidden.shape
     ff = active.shape[1]
@@ -1183,7 +1204,7 @@
         compiler_params=pltpu.CompilerParams(
             collective_id=1, has_side_effects=True, vmem_limit_bytes=60 * 2**20
         ),
-    )(vectors, weights, cot, active, slope, hidden)
+    )(gain, weights, cot, active, slope, hidden)
 
 
 def read_ordered(ref, at, blocks, part):
@@ -1202,7 +1223,7 @@
 def attend_back_kernel(
     dp_size,
     sol_size,
-    vectors_ref,
+    bias_ref,
     weights,
     normed_two_hbm,
     grad_up_hbm,
@@ -1466,6 +1487,7 @@
     )
     store(half_send_v, prefix_half_out)
 
+    bias = read_ordered(bias_ref, pl.ds(0, 1), blocks, shard)
     small = mlp_low_v.shape[0]
     pieces = rows // small
 
@@ -1496,7 +1518,7 @@
             hidden_v[...]
             + mlp_low_v[...].astype(WIDE)
             + mlp_recv_v[...].astype(WIDE)
-            + vectors_ref[4:5, :]
+            + bias
         )
         if t > 1:
             tile_store(t - 2).wait()
@@ -1518,7 +1540,7 @@
     dp_size,
     sol_size,
     shard,
-    vectors,
+    bias,
     weights,
     normed_two,
     grad_up,
@@ -1591,7 +1613,7 @@
             collective_id=2, has_side_effects=True, vmem_limit_bytes=60 * 2**20
         ),
     )(
-        vectors,
+        bias,
         weights,
         normed_two,
         grad_up,
@@ -1609,7 +1631,7 @@
     dp_size,
     sol_size,
     x_ref,
-    vectors_ref,
+    gain_ref,
     early_ref,
     normed_hbm,
     branch_hbm,
@@ -1759,7 +1781,7 @@
         for i in range(parts):
             if 1 <= step - i < sol_size:
                 chain(sol_size - 1 - (step - i), i)
-        ring.to(2 + step)
+        ring.to(1 + step)
         if step == 4:
             ring.prepare()
 
@@ -1771,7 +1793,7 @@
         for i in range(parts):
             half_cross(i).wait()
 
-    gain = vectors_ref[0:1, :]
+    gain = read_ordered(gain_ref, pl.ds(0, 1), blocks, shard)
 
     def tile_load(t):
         return pltpu.make_async_copy(
@@ -1823,6 +1845,7 @@
 
     for k in range(len(partners)):
         table_copy(k).start()
+        ring.to(9 + k)
         table_copy(k).wait_recv()
         if k + 1 < len(partners):
             table_v[k + 1] = table_v[k] + table_recv_v[k]
@@ -1844,7 +1867,7 @@
     sol_size,
     shard,
     x,
-    vectors,
+    gain,
     early,
     normed,
     branch,
@@ -1908,7 +1931,7 @@
         ),
     )(
         x,
-        vectors,
+        gain,
         early,
         normed,
         branch,
@@ -2359,15 +2382,10 @@
 ):
     width = inputs.shape[1]
     shard_rows = query_weight.shape[0]
-    ff_cols = up_weight.shape[1] // 2
     dp_size, sol_size = lax.axis_size("dp"), lax.axis_size("sol")
-    here = Place(dp_size, sol_size)
-    core = here.core
-    first_core = core == 0
-    order = jnp.stack(here.blocks()).astype(jnp.int32)
-    vectors = jnp.stack([attn_gain, attn_shift, mlp_gain, mlp_shift, down_bias])
-    vectors = jnp.take(vectors.reshape(5, here.count * 2, shard_rows), order, axis=1).reshape(5, width)
-    up_bias_c = jnp.where(first_core, up_bias[:ff_cols], up_bias[ff_cols:])[None]
+    attn_gain, attn_shift, mlp_gain, mlp_shift, up_bias, down_bias = [
+        v.reshape(1, -1) for v in (attn_gain, attn_shift, mlp_gain, mlp_shift, up_bias, down_bias)
+    ]
     (
         weights,
         normed_all,
@@ -2385,20 +2403,19 @@
         dp_size,
         sol_size,
         inputs,
-        vectors,
-        up_bias_c,
+        (attn_gain, attn_shift, mlp_gain, mlp_shift, up_bias),
         live_rows,
         cotangent,
         (query_weight, key_weight, value_weight, out_weight, up_weight, down_weight),
     )
     grad_up, grad_branch, grad_hidden, mlp_low, down_grad, early_sums = run_down(
-        dp_size, sol_size, shard_rows, vectors, weights, cot_pair, active, slope, hidden
+        dp_size, sol_size, shard_rows, mlp_gain, weights, cot_pair, active, slope, hidden
     )
     query_grad, kv_grad, own_low, prefix_half, up_grad, outputs, _ = run_attend_back(
         dp_size,
         sol_size,
         shard_rows,
-        vectors,
+        down_bias,
         weights,
         normed_two,
         grad_up,
@@ -2415,7 +2432,7 @@
         sol_size,
         shard_rows,
         inputs,
-        vectors,
+        attn_gain,
         early_sums,
         normed_all,
         grad_branch,

time: 602 us -> 580 us (0.963)
  Pallas kernels: 587 us -> 574 us
    pallas_call x1, Pallas kernels: 273 us -> 263 us  [run_forward(): pl.pallas_call(functools.partial(forward_kernel, dp_size, sol_size), out_...]
where the time goes in v5:
time: 580 us; the launch traced here: 576 us
  Pallas kernels  574 us (99%)
    pallas_call x1, Pallas kernels, run_forward(): pl.pallas_call(functools.partial(forward_kernel, dp_size, sol_size), out_...  263 us
    pallas_call x1, Pallas kernels, run_last(): pl.pallas_call(functools.partial(last_kernel, dp_size, sol_size), out_sha...  118 us
    pallas_call x1, Pallas kernels, run_down(): pl.pallas_call(functools.partial(down_kernel, dp_size, sol_size), out_sha...  92.6 us
    pallas_call x1, Pallas kernels, run_attend_back(): pl.pallas_call(functools.partial(attend_back_kernel, dp_size, sol_size),...  91.7 us

profile of v5, /device:TPU:0, one launch (start us, length us, event | category | flops | bytes accessed | tf_op | source)
XLA Modules:
  0.0 575.7 jit_solution(16840990259679840807)
XLA Ops:
  0.7 263.3 %shard_map.254 = (bf16[3,2048,2048]{2,1,0:T(8,128)(2,1)}, bf16[2048,2048]{1,0:T(8,128)(2,1)}, bf16[1024,2048]{1,0:T(8,128)(2,1)}, bf16[1024,512]{1,0:T(8,128)(2,...) custom-call(bf16[512,2048]{1,0:T(8,128)(2,1)} %x_ref.3, ...), custom_call_target="tpu_custom_call" | custom-call | tf_op jit(solution)/shard_map/pallas_call | solution.py:723
  264.0 92.6 %shard_map.255 = (bf16[1024,2048]{1,0:T(8,128)(2,1)}, bf16[1024,2048]{1,0:T(8,128)(2,1)}, f32[512,2048]{1,0:T(8,128)}, bf16[512,2048]{1,0:T(8,128)(2,1)}, f32[128,4096]{1,0:T(8,128)}, /*index=5*/f32[8,2048]{1,0:T(8,128)}) custom-call(f32[1,2048]{1,0:T(1,128)} %bitcast.15, bf16[3,2048,2048]{2,1,0:T(8,128)(2,1)} %get-tuple-element.52.weights, ...), custom_call_target="tpu_custom_call" | custom-call | tf_op jit(solution)/shard_map/pallas_call | solution.py:1183
  356.6 91.7 %shard_map.256 = (bf16[1024,512]{1,0:T(8,128)(2,1)}, bf16[2048,1024]{1,0:T(8,128)(2,1)}, bf16[512,2048]{1,0:T(8,128)(2,1)}, bf16[256,2048]{1,0:T(8,128)(2,1)}, f...) custom-call(f32[1,2048]{1,0:T(1,128)} %bitcast.27, ...), custom_call_target="tpu_custom_call" | custom-call | tf_op jit(solution)/shard_map/pallas_call | solution.py:1577
  448.3 118.1 %shard_map.257 = (f32[128,1024]{1,0:T(8,128)}, f32[128,1024]{1,0:T(8,128)}, f32[128,1024]{1,0:T(8,128)}, f32[128,1024]{1,0:T(8,128)}, bf16[512,2048]{1,0:T(8,128)(2,1)}, /*index=5*/f32[8,2048]{1,0:T(8,128)}) custom-call(bf16[512,2048]{1,0:T(8,128)(2,1)} %x_ref.3, f32[1,2048]{1,0:T(1,128)} %bitcast.17, f32[8,2048]{1,0:T(8,128)} %get-tuple-element.66.early_ref, ...), custom_call_target="tpu_custom_call" | custom-call | tf_op jit(solution)/shard_map/pallas_call | solution.py:1897
  566.4 0.0 copy-start
  566.4 7.8 %shard_map.258 = (bf16[512,2048]{1,0:T(8,128)(2,1)}, bf16[512,2048]{1,0:T(8,128)(2,1)}, f32[128,1024]{1,0:T(8,128)}, f32[128,1024]{1,0:T(8,128)}, f32[128,1024]{...) custom-call(bf16[512,2048]{1,0:T(8,128)(2,1)} %get-tuple-element.65.refs_0_, ...), custom_call_target="tpu_custom_call" | custom-call | tf_op jit(solution)/shard_map/pallas_call | solution.py:1970
  574.2 0.0 copy-done
  574.2 0.6 fusion
  574.9 0.6 copy.29
  (1 shorter events, 0.0 us)
Async XLA Ops:
  566.4 7.8 %copy-start = (f32[8,2048]{1,0:T(8,128)S(1)}, f32[8,2048]{1,0:T(8,128)}, u32[]{:S(2)}) copy-start(f32[8,2048]{1,0:T(8,128)} %get-tuple-element.83) | copy-start | bytes 196612

commit v6 on v5

--- a/solution.py
+++ b/solution.py
@@ -414,12 +414,12 @@
 
     cot_load = pltpu.make_async_copy(cot_hbm, active_v.at[pl.ds(0, rows)], cot_sem.at[1])
     start_swap(0)
+
+    start_ring(0, 0)
+    start_ring(0, 1)
     start_swap(1)
     start_swap(2)
     cot_load.start()
-
-    start_ring(0, 0)
-    start_ring(0, 1)
 
     def ordered(ref, at):
         return jnp.concatenate(
@@ -1944,18 +1944,20 @@
     )
 
 
+FINISH_PARTS = 4
+
+
 def finish_kernel(*refs):
     count = (len(refs) - 2) // 3
     ins, outs, rooms = refs[:count], refs[count : 2 * count], refs[2 * count : 3 * count]
     in_sem, out_sem = refs[3 * count :]
-    loads = [
-        pltpu.make_async_copy(src, room, in_sem.at[i])
-        for i, (src, room) in enumerate(zip(ins, rooms))
-    ]
-    stores = [
-        pltpu.make_async_copy(room, dst, out_sem.at[i])
-        for i, (room, dst) in enumerate(zip(rooms, outs))
-    ]
+    loads, stores = [], []
+    for i, (src, dst, room) in enumerate(zip(ins, outs, rooms)):
+        part = src.shape[0] // FINISH_PARTS
+        for k in range(FINISH_PARTS):
+            at = pl.ds(k * part, part)
+            loads.append(pltpu.make_async_copy(src.at[at], room.at[at], in_sem.at[i, k]))
+            stores.append(pltpu.make_async_copy(room.at[at], dst.at[at], out_sem.at[i, k]))
     for copy in loads:
         copy.start()
     for load, store in zip(loads, stores):
@@ -1973,7 +1975,7 @@
         in_specs=[any_spec()] * len(arrays),
         out_specs=[any_spec()] * len(arrays),
         scratch_shapes=[pltpu.VMEM(a.shape, a.dtype) for a in arrays]
-        + [dma((len(arrays),)), dma((len(arrays),))],
+        + [dma((len(arrays), FINISH_PARTS))] * 2,
         compiler_params=pltpu.CompilerParams(vmem_limit_bytes=60 * 2**20),
     )(*arrays)
 

time: 580 us -> 581 us (level)
  no operation moved by 1% of the time
where the time goes in v6:
time: 581 us; the launch traced here: 576 us
  Pallas kernels  574 us (99%)
    pallas_call x1, Pallas kernels, run_forward(): pl.pallas_call(functools.partial(forward_kernel, dp_size, sol_size), out_...  263 us
    pallas_call x1, Pallas kernels, run_last(): pl.pallas_call(functools.partial(last_kernel, dp_size, sol_size), out_sha...  118 us
    pallas_call x1, Pallas kernels, run_down(): pl.pallas_call(functools.partial(down_kernel, dp_size, sol_size), out_sha...  92.6 us
    pallas_call x1, Pallas kernels, run_attend_back(): pl.pallas_call(functools.partial(attend_back_kernel, dp_size, sol_size),...  91.7 us

profile of v6, /device:TPU:0, one launch (start us, length us, event | category | flops | bytes accessed | tf_op | source)
XLA Modules:
  0.0 576.3 jit_solution(2886583188527466123)
XLA Ops:
  0.7 263.3 %shard_map.254 = (bf16[3,2048,2048]{2,1,0:T(8,128)(2,1)}, bf16[2048,2048]{1,0:T(8,128)(2,1)}, bf16[1024,2048]{1,0:T(8,128)(2,1)}, bf16[1024,512]{1,0:T(8,128)(2,...) custom-call(bf16[512,2048]{1,0:T(8,128)(2,1)} %x_ref.3, ...), custom_call_target="tpu_custom_call" | custom-call | tf_op jit(solution)/shard_map/pallas_call | solution.py:723
  264.0 92.6 %shard_map.255 = (bf16[1024,2048]{1,0:T(8,128)(2,1)}, bf16[1024,2048]{1,0:T(8,128)(2,1)}, f32[512,2048]{1,0:T(8,128)}, bf16[512,2048]{1,0:T(8,128)(2,1)}, f32[128,4096]{1,0:T(8,128)}, /*index=5*/f32[8,2048]{1,0:T(8,128)}) custom-call(f32[1,2048]{1,0:T(1,128)} %bitcast.15, bf16[3,2048,2048]{2,1,0:T(8,128)(2,1)} %get-tuple-element.52.weights, ...), custom_call_target="tpu_custom_call" | custom-call | tf_op jit(solution)/shard_map/pallas_call | solution.py:1183
  356.6 91.7 %shard_map.256 = (bf16[1024,512]{1,0:T(8,128)(2,1)}, bf16[2048,1024]{1,0:T(8,128)(2,1)}, bf16[512,2048]{1,0:T(8,128)(2,1)}, bf16[256,2048]{1,0:T(8,128)(2,1)}, f...) custom-call(f32[1,2048]{1,0:T(1,128)} %bitcast.27, ...), custom_call_target="tpu_custom_call" | custom-call | tf_op jit(solution)/shard_map/pallas_call | solution.py:1577
  448.3 118.1 %shard_map.257 = (f32[128,1024]{1,0:T(8,128)}, f32[128,1024]{1,0:T(8,128)}, f32[128,1024]{1,0:T(8,128)}, f32[128,1024]{1,0:T(8,128)}, bf16[512,2048]{1,0:T(8,128)(2,1)}, /*index=5*/f32[8,2048]{1,0:T(8,128)}) custom-call(bf16[512,2048]{1,0:T(8,128)(2,1)} %x_ref.3, f32[1,2048]{1,0:T(1,128)} %bitcast.17, f32[8,2048]{1,0:T(8,128)} %get-tuple-element.66.early_ref, ...), custom_call_target="tpu_custom_call" | custom-call | tf_op jit(solution)/shard_map/pallas_call | solution.py:1897
  566.4 0.0 copy-start
  566.4 8.4 %shard_map.258 = (bf16[512,2048]{1,0:T(8,128)(2,1)}, bf16[512,2048]{1,0:T(8,128)(2,1)}, f32[128,1024]{1,0:T(8,128)}, f32[128,1024]{1,0:T(8,128)}, f32[128,1024]{...) custom-call(bf16[512,2048]{1,0:T(8,128)(2,1)} %get-tuple-element.65.refs_0_, ...), custom_call_target="tpu_custom_call" | custom-call | tf_op jit(solution)/shard_map/pallas_call | solution.py:1972
  574.9 0.0 copy-done
  574.9 0.6 fusion
  575.5 0.6 copy.29
  (1 shorter events, 0.0 us)
Async XLA Ops:
  566.4 8.5 %copy-start = (f32[8,2048]{1,0:T(8,128)S(1)}, f32[8,2048]{1,0:T(8,128)}, u32[]{:S(2)}) copy-start(f32[8,2048]{1,0:T(8,128)} %get-tuple-element.83) | copy-start | bytes 196612
